TPU v7x, 128 devices: a whole 4x4x4 slice. The times are simulated.
128 devices in a mesh: seq: 32 (over z_lo, x, y), batch: 4 (over z_hi, core).
Axes of the slice: x: 4, y: 4, z: 4 (z_hi: 2, z_lo: 2; z = z_hi * 2 + z_lo), core: 2. Of those that a mesh axis runs over, the one named last changes fastest.
Arguments:
- latent: bfloat16 [256, 256, 1152], P(('batch', 'seq')), parts along dimension 0, may hold values from -120 to 120, as said below
- modulation: float32 [24, 1152], P('batch'), parts along dimension 0, may hold values from -1.5 to 9
- w_spatial_qkv: bfloat16 [1152, 3456], replicated, may hold values from -0.1875 to 0.1875
- w_spatial_out: bfloat16 [1152, 1152], replicated, may hold values from -0.1875 to 0.1875
- w_temporal_qkv: bfloat16 [1152, 3456], replicated, may hold values from -0.1875 to 0.1875
- w_temporal_out: bfloat16 [1152, 1152], replicated, may hold values from -0.1875 to 0.1875
- cross_query: bfloat16 [1152, 1152], P('seq'), may hold values from -0.1875 to 0.1875
- cross_out: bfloat16 [1152, 1152], P('seq'), may hold values from -0.1875 to 0.1875
- text_keys: bfloat16 [480, 1152], P('batch'), parts along dimension 0, may hold values from -6 to 6
- text_values: bfloat16 [480, 1152], P('batch'), parts along dimension 0, may hold values from -6 to 6
- text_len: int32 [4], P('batch'), parts along dimension 0, may hold values from 30 to 120, as said below
Outputs:
- features_out: bfloat16 [256, 256, 1152], P(('batch', 'seq')), parts along dimension 0
There are 4 independent parts, one for each index of `batch`. A program takes and returns all parts, laid end to end along the dimension named above; an argument that names none is the same for every part. Nothing has to cross between parts.
Inputs may be any that keep to these rules, and one draw needn't show every extreme that they name: `latent`: token features of order one; some rows may be far larger. Slots 0 to text_len - 1 hold the caption.
All inputs are finite; a program needn't handle non-finite values.
Results may differ from a plain program's by a relative error of at most 0.028.
The roundings to bfloat16 on the way count: a program that leaves them out, or rounds other values in their place, can miss the bound.
Values may be sent and summed in bfloat16 or wider, within the bound.
No kernel may reach another device: no remote copies, remote signals or barrier semaphores. Data moves between devices by JAX's collectives and lax.ppermute only.
A program may use at most 128 MiB of HBM per device.

v0:
```python
import jax
import jax.numpy as jnp
from jax import lax
from jax.sharding import PartitionSpec as P

H = 16


def norm_mod(rows, shift, scale):
    values = rows.astype(jnp.float32)
    mean = jnp.mean(values, axis=-1, keepdims=True)
    centered = values - mean
    var = jnp.mean(centered * centered, axis=-1, keepdims=True)
    return (centered * lax.rsqrt(var + 1e-06) * (1.0 + scale) + shift).astype(jnp.bfloat16)


def softmax_weights(scores):
    top = jnp.max(scores, axis=-1, keepdims=True)
    expo = jnp.exp(scores - top)
    return (expo / jnp.sum(expo, axis=-1, keepdims=True)).astype(jnp.bfloat16)


def within_frames(qkv):
    frames, tokens, triple = qkv.shape
    width = triple // 3
    head_size = width // H
    split = qkv.reshape(frames, tokens, 3, H, head_size)
    scores = jnp.einsum(
        "fqhd,fkhd->fhqk", split[:, :, 0], split[:, :, 1], preferred_element_type=jnp.float32
    )
    weights = softmax_weights(scores / jnp.sqrt(jnp.float32(head_size)))
    mixed = jnp.einsum(
        "fhqk,fkhd->fqhd", weights, split[:, :, 2], preferred_element_type=jnp.float32
    )
    return mixed.reshape(frames, tokens, width).astype(jnp.bfloat16)


def across_frames(qkv):
    frames, places, triple = qkv.shape
    width = triple // 3
    head_size = width // H
    split = qkv.reshape(frames, places, 3, H, head_size)
    scores = jnp.einsum(
        "qphd,kphd->phqk", split[:, :, 0], split[:, :, 1], preferred_element_type=jnp.float32
    )
    weights = softmax_weights(scores / jnp.sqrt(jnp.float32(head_size)))
    mixed = jnp.einsum(
        "phqk,kphd->qphd", weights, split[:, :, 2], preferred_element_type=jnp.float32
    )
    return mixed.reshape(frames, places, width).astype(jnp.bfloat16)


def project(rows, weight):
    lead = rows.shape[:-1]
    flat = rows.reshape(-1, rows.shape[-1])
    return jnp.dot(flat, weight, preferred_element_type=jnp.float32).reshape(
        lead + (weight.shape[1],)
    )


def body(
    latent,
    modulation,
    w_spatial_qkv,
    w_spatial_out,
    w_temporal_qkv,
    w_temporal_out,
    cross_query,
    cross_out,
    text_keys,
    text_values,
    text_len,
):
    width = latent.shape[2]
    spatial_in = norm_mod(latent, modulation[0], modulation[1])
    spatial_qkv = project(spatial_in, w_spatial_qkv).astype(jnp.bfloat16)
    spatial_ctx = within_frames(spatial_qkv)
    after_spatial = (
        latent.astype(jnp.float32) + modulation[2] * project(spatial_ctx, w_spatial_out)
    ).astype(jnp.bfloat16)
    temporal_in = norm_mod(after_spatial, modulation[3], modulation[4])
    temporal_qkv = project(temporal_in, w_temporal_qkv).astype(jnp.bfloat16)
    placed_qkv = lax.all_to_all(temporal_qkv, "seq", split_axis=1, concat_axis=0, tiled=True)
    placed_ctx = across_frames(placed_qkv)
    temporal_ctx = lax.all_to_all(placed_ctx, "seq", split_axis=0, concat_axis=1, tiled=True)
    after_temporal = (
        after_spatial.astype(jnp.float32) + modulation[5] * project(temporal_ctx, w_temporal_out)
    ).astype(jnp.bfloat16)
    flat_rows = after_temporal.reshape(-1, width)
    columns = flat_rows
    cross_q = jnp.dot(
        columns,
        lax.all_gather(cross_query, "seq", axis=0, tiled=True),
        preferred_element_type=jnp.float32,
    ).astype(jnp.bfloat16)
    head_size = width // H
    slots = text_keys.shape[0]
    valid = jnp.arange(slots, dtype=jnp.int32) < text_len[0]
    q_heads = cross_q.reshape(-1, H, head_size)
    scores = jnp.einsum(
        "thd,lhd->htl",
        q_heads,
        text_keys.reshape(slots, H, head_size),
        preferred_element_type=jnp.float32,
    )
    scores = jnp.where(
        valid[None, None, :], scores / jnp.sqrt(jnp.float32(head_size)), jnp.float32(-1e30)
    )
    weights = softmax_weights(scores)
    cross_ctx = jnp.einsum(
        "htl,lhd->thd",
        weights,
        text_values.reshape(slots, H, head_size),
        preferred_element_type=jnp.float32,
    )
    cross_ctx = cross_ctx.reshape(-1, width).astype(jnp.bfloat16)
    columns = cross_ctx
    cross_proj = jnp.dot(
        columns,
        lax.all_gather(cross_out, "seq", axis=0, tiled=True),
        preferred_element_type=jnp.float32,
    )
    result = flat_rows.astype(jnp.float32) + cross_proj
    return result.reshape(after_temporal.shape).astype(jnp.bfloat16)


def solution(mesh):
    placed = (
        P(("batch", "seq"), None, None),
        P("batch", None),
        P(),
        P(),
        P(),
        P(),
        P("seq", None),
        P("seq", None),
        P("batch", None),
        P("batch", None),
        P("batch"),
    )
    return jax.shard_map(
        body, mesh=mesh, in_specs=placed, out_specs=P(("batch", "seq"), None, None), check_vma=False
    )
```

profile of v0, /device:TPU:0, one launch (start us, length us, event | category | flops | bytes accessed | tf_op | source)
XLA Modules:
  0.0 374.0 jit_solution(14728728869646354995)
XLA Ops:
  6.5 0.0 copy-start
  6.5 0.0 all-gather.5.cloned.1.call-start
  6.5 0.7 all-gather.5.cloned.1.call-update
  7.3 0.0 copy-start.2
  7.3 1.2 slice_reduce_fusion.1
  8.4 1.5 convert_reduce_fusion.1
  10.0 1.7 fusion.35
  11.7 10.0 %fusion.8 = bf16[2,256,3456]{2,1,0:T(8,128)(2,1)} fusion(bf16[1152,3456]{1,0:T(8,128)(2,1)} %param.13, bf16[2,256,1152]{2,1,0:T(8,128)(2,1)S(1)} %copy-done.2, f32[1152]{0:T(1024)S(1)} %get-tuple-element.6, f32[1152]{0:T(1024)S(1)} %get-tuple-element.7, f32[2,256]{1,0:T(2,128)S(1)} %add_rsqrt_fusion.1, f32[2,256]{1,0:T(2,128)S(1)} %broadcast_multiply_fusion.1), kind=kOutput, calls=%fused_computation.11 | convolution fusion | flops 4082171904 | bytes 12694528 | tf_op jit(solution)/shard_map/dot_general | solution.py:56
  21.7 5.8 %copy.37 = bf16[2,256,3456]{1,2,0:T(8,128)(2,1)} copy(bf16[2,256,3456]{2,1,0:T(8,128)(2,1)} %fusion.8) | data formatting | bytes 7077888 | tf_op jit(solution)/shard_map/convert_element_type | solution.py:76
  27.5 2.9 fusion.51
  30.4 6.3 %fusion.69 = (f32[2,16,256]{2,1,0:T(8,128)S(1)}, f32[2,16,256,256]{2,3,1,0:T(8,128)S(1)}) fusion(f32[2,16,256,256]{2,3,1,0:T(8,128)S(1)} %fusion.51), kind=kOutput, calls=%fused_computation.96 | output fusion | flops 8388863 | bytes 16809984 | tf_op jit(solution)/shard_map/sub | solution.py:19
  36.7 0.0 copy-start.3
  36.7 2.3 fusion.48
  39.1 2.1 convert_reduce_fusion
  41.2 0.0 copy-start.4
  41.2 0.4 fusion.31
  41.7 0.5 copy-done.4
  42.2 9.0 %fusion.11 = bf16[2,256,3456]{2,1,0:T(8,128)(2,1)S(1)} fusion(bf16[1152,3456]{1,0:T(8,128)(2,1)} %param.15, bf16[2,256,1152]{2,1,0:T(8,128)(2,1)S(1)} %get-tuple-element.17, f32[1152]{0:T(1024)S(1)} %get-tuple-element.9, f32[1152]{0:T(1024)S(1)} %get-tuple-element.10, f32[2,256]{1,0:T(2,128)S(1)} %add_rsqrt_fusion, f32[2,256]{1,0:T(2,128)S(1)} %broadcast_multiply_fusion), kind=kOutput, calls=%fused_computation.12 | convolution fusion | flops 4082171904 | bytes 12694528 | tf_op jit(solution)/shard_map/dot_general | solution.py:56
  51.2 5.4 %copy.43 = bf16[2,256,3456]{2,0,1:T(2,128)(2,1)} copy(bf16[2,256,3456]{2,1,0:T(8,128)(2,1)S(1)} %fusion.11) | data formatting | bytes 7077888 | tf_op jit(solution)/shard_map/convert_element_type | solution.py:82
  56.6 8.8 %all-to-all-start = ((bf16[2,256,3456]{2,0,1:T(2,128)(2,1)}), bf16[2,256,3456]{2,0,1:T(2,128)(2,1)}, u32[]{:S(2)}, u32[]{:S(2)}) async-start(bf16[2,256,3456]{2,0,1:T(2,128)(2,1)} %copy.43), calls=%async_computation | async-start | bytes 7077888 | tf_op jit(solution)/shard_map/all_to_all | solution.py:83
  65.5 0.0 all-gather.7.cloned.1.call-start
  65.5 0.7 all-gather.7.cloned.1.call-update
  66.2 51.4 %all-to-all-done = bf16[2,256,3456]{2,0,1:T(2,128)(2,1)} async-done(((bf16[2,256,3456]{2,0,1:T(2,128)(2,1)}), bf16[2,256,3456]{2,0,1:T(2,128)(2,1)}, u32[]{:S(2)}, u32[]{:S(2)}) %all-to-all-start) | async-done | bytes 3538976 | tf_op jit(solution)/shard_map/all_to_all | solution.py:83
  117.6 4.2 %copy.76 = bf16[2,32,8,3456]{3,2,0,1:T(8,128)(2,1)} copy(bf16[2,32,8,3456]{3,0,2,1:T(2,128)(2,1)} %bitcast.9) | data formatting | bytes 7077888 | tf_op jit(solution)/shard_map/all_to_all | solution.py:83
  121.8 13.7 %reshape.98 = bf16[64,8,3,16,72]{4,3,2,1,0:T(8,128)(2,1)} reshape(bf16[32,2,8,3456]{3,2,1,0:T(8,128)(2,1)} %bitcast.86) | data formatting | bytes 7077888 | tf_op jit(solution)/shard_map/reshape | solution.py:42
  135.5 5.6 %fusion.68 = (bf16[64,8,1,16,72]{4,3,2,1,0:T(8,128)(2,1)S(1)}, bf16[64,8,1,16,72]{4,3,2,1,0:T(8,128)(2,1)S(1)}, bf16[64,8,1,16,72]{4,3,2,1,0:T(8,128)(2,1)S(1)}) fusion(bf16[64,8,3,16,72]{4,3,2,1,0:T(8,128)(2,1)} %reshape.98), kind=kLoop, calls=%fused_computation.95 | loop fusion | bytes 7077888 | tf_op jit(solution)/shard_map/slice | solution.py:48
  141.1 2.5 fusion.40
  143.6 6.1 %fusion.70 = (f32[8,16,64]{2,1,0:T(8,128)S(1)}, f32[8,16,64,64]{2,3,1,0:T(8,128)S(1)}) fusion(f32[8,16,64,64]{2,3,1,0:T(8,128)S(1)} %fusion.40), kind=kOutput, calls=%fused_computation.97 | output fusion | flops 2097215 | bytes 4227072 | tf_op jit(solution)/shard_map/sub | solution.py:19
  149.7 2.5 convert_bitcast_fusion
  152.3 1.4 copy.49
  153.6 0.0 copy-start.6
  153.7 0.0 copy-start.7
  153.7 3.4 convert_element_type.90
  157.1 6.9 %all-to-all-start.1 = ((bf16[64,8,1152]{2,1,0:T(8,128)(2,1)}), bf16[64,8,1152]{2,1,0:T(8,128)(2,1)S(1)}, u32[]{:S(2)}, u32[]{:S(2)}) async-start(bf16[64,8,1152]{2,1,0:T(8,128)(2,1)} %convert_element_type.90), calls=%async_computation.1 | async-start | bytes 2359296 | tf_op jit(solution)/shard_map/all_to_all | solution.py:85
  164.0 0.2 copy.52
  164.9 0.2 copy.53
  165.1 17.9 %all-to-all-done.1 = bf16[64,8,1152]{2,1,0:T(8,128)(2,1)S(1)} async-done(((bf16[64,8,1152]{2,1,0:T(8,128)(2,1)}), bf16[64,8,1152]{2,1,0:T(8,128)(2,1)S(1)}, u32[]{:S(2)}, u32[]{:S(2)}) %all-to-all-start.1) | async-done | bytes 1179680 | tf_op jit(solution)/shard_map/all_to_all | solution.py:85
  183.0 0.0 copy-done.5
  183.0 4.6 %fusion.24 = bf16[2,256,1152]{2,1,0:T(8,128)(2,1)} fusion(bf16[2,256,1152]{2,1,0:T(8,128)(2,1)S(1)} %copy-done.5, bf16[1152,1152]{1,0:T(8,128)(2,1)} %param.16, bf16[2,32,8,1152]{3,2,0,1:T(8,128)(2,1)S(1)} %bitcast.89, f32[1152]{0:T(1024)S(1)} %get-tuple-element.5), kind=kOutput, calls=%fused_computation.36 | convolution fusion | flops 1361313792 | bytes 6197760 | tf_op jit(solution)/shard_map/dot_general | solution.py:56
  187.6 9.9 %all-gather.5.cloned.1.call-done = bf16[32,36,1152]{2,1,0:T(8,128)(2,1)} async-done(((bf16[1,36,1152]{2,1,0:T(8,128)(2,1)}), bf16[32,36,1152]{2,1,0:T(8,128)(2,1)}) %all-gather.5.cloned.1.call-update) | async-done | bytes 2654224 | tf_op jit(solution)/shard_map/all_gather | solution.py:93
  197.5 3.6 reshape.104
  201.1 4.1 %convolution_convert_fusion = bf16[512,1152]{1,0:T(8,128)(2,1)} fusion(bf16[512,1152]{1,0:T(8,128)(2,1)} %bitcast.91, bf16[1152,1152]{1,0:T(8,128)(2,1)S(1)} %reshape.104), kind=kOutput, calls=%fused_computation.34 | convolution fusion | flops 1359544320 | bytes 5013504 | tf_op jit(solution)/shard_map/dot_general | solution.py:91
  205.2 1.6 copy.51
  206.8 3.6 fusion.71
  210.4 3.6 fusion.47
  214.0 142.5 %all-gather.7.cloned.1.call-done = bf16[32,36,1152]{2,1,0:T(8,128)(2,1)} async-done(((bf16[1,36,1152]{2,1,0:T(8,128)(2,1)}), bf16[32,36,1152]{2,1,0:T(8,128)(2,1)}) %all-gather.7.cloned.1.call-update) | async-done | bytes 2654224 | tf_op jit(solution)/shard_map/all_gather | solution.py:120
  356.5 5.2 %reshape.106 = bf16[1152,1152]{1,0:T(8,128)(2,1)} reshape(bf16[32,36,1152]{2,1,0:T(8,128)(2,1)} %all-gather.7.cloned.1.call-done) | data formatting | bytes 5308416
  361.7 5.5 %fusion.22 = bf16[512,1152]{1,0:T(8,128)(2,1)} fusion(bf16[512,1152]{0,1:T(8,128)(2,1)} %bitcast.93, bf16[1152,1152]{1,0:T(8,128)(2,1)} %reshape.106, bf16[512,1152]{1,0:T(8,128)(2,1)} %bitcast.92), kind=kOutput, calls=%fused_computation.33 | convolution fusion | flops 1360723968 | bytes 6193152 | tf_op jit(solution)/shard_map/dot_general | solution.py:118
  (13 shorter events, 0.1 us)
Async XLA Ops:
  6.5 32.5 %copy-start = (bf16[1152,1152]{1,0:T(8,128)(2,1)S(1)}, bf16[1152,1152]{1,0:T(8,128)(2,1)}, u32[]{:S(2)}) copy-start(bf16[1152,1152]{1,0:T(8,128)(2,1)} %param.14) | copy-start | bytes 7962628
  6.5 191.0 %all-gather.5.cloned.1.call-start = ((), (), s32[]{:S(2)}) async-start(), calls=%async_computation.2 | async-start | bytes 3041280 | tf_op jit(solution)/shard_map/all_gather | solution.py:93
  7.3 4.4 %copy-start.2 = (bf16[2,256,1152]{2,1,0:T(8,128)(2,1)S(1)}, bf16[2,256,1152]{2,1,0:T(8,128)(2,1)}, u32[]{:S(2)}) copy-start(bf16[2,256,1152]{2,1,0:T(8,128)(2,1)} %param.11) | copy-start | bytes 3538948
  36.7 2.3 copy-start.3
  41.2 1.0 copy-start.4
  56.6 61.0 %all-to-all-start = ((bf16[2,256,3456]{2,0,1:T(2,128)(2,1)}), bf16[2,256,3456]{2,0,1:T(2,128)(2,1)}, u32[]{:S(2)}, u32[]{:S(2)}) async-start(bf16[2,256,3456]{2,0,1:T(2,128)(2,1)} %copy.43), calls=%async_computation | async-start | bytes 7077888 | tf_op jit(solution)/shard_map/all_to_all | solution.py:83
  65.5 291.0 %all-gather.7.cloned.1.call-start = ((), (), s32[]{:S(2)}) async-start(), calls=%async_computation.3 | async-start | bytes 3041280 | tf_op jit(solution)/shard_map/all_gather | solution.py:120
  153.6 10.3 %copy-start.6 = (bf16[120,1152]{1,0:T(8,128)(2,1)S(1)}, bf16[120,1152]{1,0:T(8,128)(2,1)}, u32[]{:S(2)}) copy-start(bf16[120,1152]{1,0:T(8,128)(2,1)} %param.19) | copy-start | bytes 829444
  153.7 11.2 %copy-start.7 = (bf16[120,1152]{1,0:T(8,128)(2,1)S(1)}, bf16[120,1152]{1,0:T(8,128)(2,1)}, u32[]{:S(2)}) copy-start(bf16[120,1152]{1,0:T(8,128)(2,1)} %param.20) | copy-start | bytes 829444
  157.1 25.9 %copy-start.5 = (bf16[2,256,1152]{2,1,0:T(8,128)(2,1)S(1)}, bf16[2,256,1152]{2,1,0:T(8,128)(2,1)}, u32[]{:S(2)}) copy-start(bf16[2,256,1152]{2,1,0:T(8,128)(2,1)} %copy-done.4) | copy-start | bytes 3538948
  157.1 25.9 %all-to-all-start.1 = ((bf16[64,8,1152]{2,1,0:T(8,128)(2,1)}), bf16[64,8,1152]{2,1,0:T(8,128)(2,1)S(1)}, u32[]{:S(2)}, u32[]{:S(2)}) async-start(bf16[64,8,1152]{2,1,0:T(8,128)(2,1)} %convert_element_type.90), calls=%async_computation.1 | async-start | bytes 2359296 | tf_op jit(solution)/shard_map/all_to_all | solution.py:85
  361.7 5.5 %copy-start.1 = (bf16[1152,1152]{1,0:T(8,128)(2,1)S(1)}, bf16[1152,1152]{1,0:T(8,128)(2,1)}, u32[]{:S(2)}) copy-start(bf16[1152,1152]{1,0:T(8,128)(2,1)} %param.14) | copy-start | bytes 7962628
Sparse Core Ops, SparseCore 0:
  9.0 188.4 all-gather.4
  199.2 157.3 all-gather.6
where the time goes:
time: 375 us; the launch traced here: 374 us
  waiting for transfers between devices  223 us (59%)
  matrix products  52.8 us (14%)
  local copies, waits for them, and re-layouts  50.8 us (14%)
  other arithmetic  17.3 us (5%)
  starting transfers between devices  15.8 us (4%)
  between operations  14.2 us (4%)
    all_gather x1, waiting for transfers between devices, body(): lax.all_gather(cross_out, 'seq', axis=0, tiled=True)  142 us
    all_to_all x1, waiting for transfers between devices, body(): lax.all_to_all(temporal_qkv, 'seq', split_axis=1, concat_axis=0, tiled=True)  51.4 us
    dot_general x4, matrix products, project(): jnp.dot(flat, weight, preferred_element_type=jnp.float32)  25.7 us
    all_to_all x1, waiting for transfers between devices, body(): lax.all_to_all(placed_ctx, 'seq', split_axis=0, concat_axis=1, tiled=True)  17.9 us
    reshape x1, local copies, waits for them, and re-layouts, across_frames(): split = qkv.reshape(frames, places, 3, H, head_size)  13.7 us
    sub x2, other arithmetic, softmax_weights(): expo = jnp.exp(scores - top)  12.4 us
    all_gather x1, waiting for transfers between devices, body(): lax.all_gather(cross_query, 'seq', axis=0, tiled=True)  9.91 us
    unnamed x20, local copies, waits for them, and re-layouts  9.78 us
  transfers between devices with their start and end apart: 4, of which 4 were waited for; matrix products, arithmetic and copies ran while one was open for 29% of the time, Pallas kernels for 0%

commit v1 on v0

--- a/solution.py
+++ b/solution.py
@@ -1,9 +1,11 @@
 import jax
 import jax.numpy as jnp
 from jax import lax
-from jax.sharding import PartitionSpec as P
+from jax.sharding import Mesh, PartitionSpec as P
 
 H = 16
+SEQ = ("z_lo", "x", "y")
+ALL = ("z_hi", "core", "z_lo", "x", "y")
 
 
 def norm_mod(rows, shift, scale):
@@ -58,6 +60,17 @@
     )
 
 
+def gather_cross(cross_query, cross_out):
+    core = lax.axis_index("core")
+    mine = jnp.where(core == 0, cross_query, cross_out)
+    copies = jnp.broadcast_to(mine[None], (32,) + mine.shape)
+    whole = lax.all_to_all(copies, SEQ, split_axis=0, concat_axis=0, tiled=False)
+    other = lax.ppermute(whole, "core", [(0, 1), (1, 0)])
+    query = jnp.where(core == 0, whole, other).reshape(-1, mine.shape[1])
+    out = jnp.where(core == 0, other, whole).reshape(-1, mine.shape[1])
+    return query, out
+
+
 def body(
     latent,
     modulation,
@@ -72,27 +85,22 @@
     text_len,
 ):
     width = latent.shape[2]
+    whole_query, whole_out = gather_cross(cross_query, cross_out)
     spatial_in = norm_mod(latent, modulation[0], modulation[1])
     spatial_qkv = project(spatial_in, w_spatial_qkv).astype(jnp.bfloat16)
     spatial_ctx = within_frames(spatial_qkv)
     after_spatial = (
         latent.astype(jnp.float32) + modulation[2] * project(spatial_ctx, w_spatial_out)
     ).astype(jnp.bfloat16)
+    after_spatial = lax.all_to_all(after_spatial, SEQ, split_axis=1, concat_axis=0, tiled=True)
     temporal_in = norm_mod(after_spatial, modulation[3], modulation[4])
     temporal_qkv = project(temporal_in, w_temporal_qkv).astype(jnp.bfloat16)
-    placed_qkv = lax.all_to_all(temporal_qkv, "seq", split_axis=1, concat_axis=0, tiled=True)
-    placed_ctx = across_frames(placed_qkv)
-    temporal_ctx = lax.all_to_all(placed_ctx, "seq", split_axis=0, concat_axis=1, tiled=True)
+    temporal_ctx = across_frames(temporal_qkv)
     after_temporal = (
         after_spatial.astype(jnp.float32) + modulation[5] * project(temporal_ctx, w_temporal_out)
     ).astype(jnp.bfloat16)
     flat_rows = after_temporal.reshape(-1, width)
-    columns = flat_rows
-    cross_q = jnp.dot(
-        columns,
-        lax.all_gather(cross_query, "seq", axis=0, tiled=True),
-        preferred_element_type=jnp.float32,
-    ).astype(jnp.bfloat16)
+    cross_q = project(flat_rows, whole_query).astype(jnp.bfloat16)
     head_size = width // H
     slots = text_keys.shape[0]
     valid = jnp.arange(slots, dtype=jnp.int32) < text_len[0]
@@ -114,30 +122,27 @@
         preferred_element_type=jnp.float32,
     )
     cross_ctx = cross_ctx.reshape(-1, width).astype(jnp.bfloat16)
-    columns = cross_ctx
-    cross_proj = jnp.dot(
-        columns,
-        lax.all_gather(cross_out, "seq", axis=0, tiled=True),
-        preferred_element_type=jnp.float32,
-    )
-    result = flat_rows.astype(jnp.float32) + cross_proj
-    return result.reshape(after_temporal.shape).astype(jnp.bfloat16)
+    result = flat_rows.astype(jnp.float32) + project(cross_ctx, whole_out)
+    result = result.reshape(after_temporal.shape).astype(jnp.bfloat16)
+    return lax.all_to_all(result, SEQ, split_axis=0, concat_axis=1, tiled=True)
 
 
 def solution(mesh):
+    fine = Mesh(mesh.devices.reshape(2, 4, 4, 2, 2), ("z_lo", "x", "y", "z_hi", "core"))
+    part = ("z_hi", "core")
     placed = (
-        P(("batch", "seq"), None, None),
-        P("batch", None),
+        P(ALL, None, None),
+        P(part, None),
         P(),
         P(),
         P(),
         P(),
-        P("seq", None),
-        P("seq", None),
-        P("batch", None),
-        P("batch", None),
-        P("batch"),
+        P(SEQ, None),
+        P(SEQ, None),
+        P(part, None),
+        P(part, None),
+        P(part),
     )
     return jax.shard_map(
-        body, mesh=mesh, in_specs=placed, out_specs=P(("batch", "seq"), None, None), check_vma=False
+        body, mesh=fine, in_specs=placed, out_specs=P(ALL, None, None), check_vma=False
     )

time: 375 us -> 221 us (0.59)
  the two profiles are of different devices: /device:TPU:0 before, /device:TPU:1 now
where the time goes in v1:
time: 221 us; the launch traced here: 220 us
  local copies, waits for them, and re-layouts  52.6 us (24%)
  matrix products  52.1 us (24%)
  waiting for transfers between devices  45 us (20%)
  other arithmetic  26.8 us (12%)
  blocking collectives  23.6 us (11%)
  starting transfers between devices  18.4 us (8%)
    dot_general x6, matrix products, project(): jnp.dot(flat, weight, preferred_element_type=jnp.float32)  34.2 us
    all_to_all x1, waiting for transfers between devices, gather_cross(): lax.all_to_all(copies, SEQ, split_axis=0, concat_axis=0, tiled=False)  28.6 us
    all_to_all x1, blocking collectives, body(): return lax.all_to_all(result, SEQ, split_axis=0, concat_axis=1, tiled=True)  23.6 us
    all_to_all x1, waiting for transfers between devices, body(): lax.all_to_all(after_spatial, SEQ, split_axis=1, concat_axis=0, tiled=True)  16.4 us
    reshape x1, local copies, waits for them, and re-layouts, across_frames(): split = qkv.reshape(frames, places, 3, H, head_size)  13.7 us
    sub x2, other arithmetic, softmax_weights(): expo = jnp.exp(scores - top)  12.4 us
    all_to_all x1, starting transfers between devices, body(): lax.all_to_all(after_spatial, SEQ, split_axis=1, concat_axis=0, tiled=True)  9.22 us
    convert_element_type x2, local copies, waits for them, and re-layouts, across_frames(): return mixed.reshape(frames, places, width).astype(jnp.bfloat16)  7.3 us
  transfers between devices with their start and end apart: 3, of which 2 were waited for; matrix products, arithmetic and copies ran while one was open for 27% of the time, Pallas kernels for 0%

profile of v1, /device:TPU:1, one launch (start us, length us, event | category | flops | bytes accessed | tf_op | source)
XLA Modules:
  0.0 219.5 jit_solution(15133735958186069926)
XLA Ops:
  0.0 1.8 slice_reduce_fusion.1
  1.8 1.5 convert_reduce_fusion
  3.3 1.7 fusion.32
  5.0 10.0 %fusion.8 = bf16[2,256,3456]{2,1,0:T(8,128)(2,1)} fusion(bf16[1152,3456]{1,0:T(8,128)(2,1)} %param.13, bf16[2,256,1152]{2,1,0:T(8,128)(2,1)S(1)} %copy-done.5, f32[1152]{0:T(1024)S(1)} %get-tuple-element.6, f32[1152]{0:T(1024)S(1)} %get-tuple-element.7, f32[2,256]{1,0:T(2,128)S(1)} %add_rsqrt_fusion.1, f32[2,256]{1,0:T(2,128)S(1)} %broadcast_multiply_fusion.1), kind=kOutput, calls=%fused_computation.11 | convolution fusion | flops 4082171904 | bytes 12694528 | tf_op jit(solution)/shard_map/dot_general | solution.py:58
  15.0 5.8 %copy.65 = bf16[2,256,3456]{1,2,0:T(8,128)(2,1)} copy(bf16[2,256,3456]{2,1,0:T(8,128)(2,1)} %fusion.8) | data formatting | bytes 7077888 | tf_op jit(solution)/shard_map/convert_element_type | solution.py:90
  20.7 2.9 %fusion.53 = f32[2,16,256,256]{2,3,1,0:T(8,128)S(1)} fusion(bf16[2,256,3,16,72]{1,4,3,2,0:T(8,128)(2,1)} %bitcast.104), kind=kOutput, calls=%fused_computation.70 | convolution fusion | flops 301989888 | bytes 10747904 | tf_op jit(solution)/shard_map/fqhd,fkhd->fhqk/dot_general | solution.py:30
  23.7 6.3 %fusion.65 = (f32[2,16,256]{2,1,0:T(8,128)S(1)}, f32[2,16,256,256]{2,3,1,0:T(8,128)S(1)}) fusion(f32[2,16,256,256]{2,3,1,0:T(8,128)S(1)} %fusion.53), kind=kOutput, calls=%fused_computation.96 | output fusion | flops 8388863 | bytes 16809984 | tf_op jit(solution)/shard_map/sub | solution.py:21
  30.0 0.0 copy-start.6
  30.0 2.3 %fusion.51 = bf16[2,16,72,256]{3,2,1,0:T(8,128)(2,1)S(1)} fusion(f32[2,16,256,256]{2,3,1,0:T(8,128)S(1)} %get-tuple-element.17, f32[2,16,256]{2,1,0:T(8,128)S(1)} %get-tuple-element.16, bf16[2,256,3,16,72]{1,4,3,2,0:T(8,128)(2,1)} %bitcast.105), kind=kOutput, calls=%fused_computation.68 | convolution fusion | flops 306774016 | bytes 10780672 | tf_op jit(solution)/shard_map/fhqk,fkhd->fqhd/dot_general | solution.py:34
  32.3 1.9 fusion.25
  34.3 2.2 %copy.71 = bf16[2,256,1152]{2,0,1:T(2,128)(2,1)} copy(bf16[2,256,1152]{2,1,0:T(8,128)(2,1)S(1)} %fusion.25) | data formatting | bytes 2359296 | tf_op jit(solution)/shard_map/convert_element_type | solution.py:94
  36.5 9.2 %all-to-all-start = ((bf16[2,256,1152]{2,0,1:T(2,128)(2,1)}), bf16[2,256,1152]{2,0,1:T(2,128)(2,1)S(1)}, u32[]{:S(2)}, u32[]{:S(2)}) async-start(bf16[2,256,1152]{2,0,1:T(2,128)(2,1)} %copy.71), calls=%async_computation | async-start | bytes 2359296 | tf_op jit(solution)/shard_map/all_to_all | solution.py:95
  45.8 16.4 %all-to-all-done = bf16[2,256,1152]{2,0,1:T(2,128)(2,1)S(1)} async-done(((bf16[2,256,1152]{2,0,1:T(2,128)(2,1)}), bf16[2,256,1152]{2,0,1:T(2,128)(2,1)S(1)}, u32[]{:S(2)}, u32[]{:S(2)}) %all-to-all-start) | async-done | bytes 1179680 | tf_op jit(solution)/shard_map/all_to_all | solution.py:95
  62.2 2.0 broadcast_in_dim.11
  64.1 0.0 copy-done.3
  64.2 5.0 %all-to-all-start.1 = ((bf16[32,36,1152]{2,1,0:T(8,128)(2,1)}), bf16[32,36,1152]{2,1,0:T(8,128)(2,1)S(1)}, u32[]{:S(2)}, u32[]{:S(2)}) async-start(bf16[32,36,1152]{2,1,0:T(8,128)(2,1)} %broadcast_in_dim.11), calls=%async_computation.1 | async-start | bytes 5898240 | tf_op jit(solution)/shard_map/all_to_all | solution.py:67
  69.2 0.2 copy.81
  70.1 1.2 copy.82
  71.3 0.6 iota_compare_fusion
  71.9 1.4 copy.72
  73.3 0.8 bitcast_convert_fusion
  74.1 0.2 bitcast_reduce_fusion
  74.4 0.4 fusion.41
  74.8 1.5 fusion.39
  76.3 28.6 %all-to-all-done.1 = bf16[32,36,1152]{2,1,0:T(8,128)(2,1)S(1)} async-done(((bf16[32,36,1152]{2,1,0:T(8,128)(2,1)}), bf16[32,36,1152]{2,1,0:T(8,128)(2,1)S(1)}, u32[]{:S(2)}, u32[]{:S(2)}) %all-to-all-start.1) | async-done | bytes 2654240 | tf_op jit(solution)/shard_map/all_to_all | solution.py:67
  104.9 1.9 copy.78
  106.8 4.1 %collective-permute-start = (bf16[32,36,1152]{2,0,1:T(8,128)(2,1)}, bf16[32,36,1152]{2,0,1:T(8,128)(2,1)}, u32[]{:S(2)}, u32[]{:S(2)}) collective-permute-start(bf16[32,36,1152]{2,0,1:T(8,128)(2,1)} %copy.78), channel_id=1, source_target_pairs={{0,1},{1,0},{2,3},{3,2},{4,5},{5,4},{6,7},{7,6},{8,9},{9,8},{10,11... | collective-permute-start | bytes 7962632 | tf_op jit(solution)/shard_map/ppermute | solution.py:68
  110.9 9.6 %fusion.11 = bf16[64,8,3456]{2,1,0:T(8,128)(2,1)} fusion(bf16[64,8,1152]{2,1,0:T(8,128)(2,1)S(1)} %copy-done.9, bf16[1152,3456]{1,0:T(8,128)(2,1)} %param.15), kind=kOutput, calls=%fused_computation.12 | convolution fusion | flops 4078632960 | bytes 12681216 | tf_op jit(solution)/shard_map/dot_general | solution.py:58
  120.5 13.7 %reshape.152 = bf16[64,8,3,16,72]{4,3,2,1,0:T(8,128)(2,1)} reshape(bf16[64,8,3456]{2,1,0:T(8,128)(2,1)} %fusion.11) | data formatting | bytes 7077888 | tf_op jit(solution)/shard_map/reshape | solution.py:44
  134.1 5.6 %fusion.64 = (bf16[64,8,1,16,72]{4,3,2,1,0:T(8,128)(2,1)S(1)}, bf16[64,8,1,16,72]{4,3,2,1,0:T(8,128)(2,1)S(1)}, bf16[64,8,1,16,72]{4,3,2,1,0:T(8,128)(2,1)S(1)}) fusion(bf16[64,8,3,16,72]{4,3,2,1,0:T(8,128)(2,1)} %reshape.152), kind=kLoop, calls=%fused_computation.95 | loop fusion | bytes 7077888 | tf_op jit(solution)/shard_map/slice | solution.py:50
  139.7 2.5 %fusion.43 = f32[8,16,64,64]{2,3,1,0:T(8,128)S(1)} fusion(bf16[64,8,1,16,72]{4,3,2,1,0:T(8,128)(2,1)S(1)} %get-tuple-element.13, bf16[64,8,1,16,72]{4,3,2,1,0:T(8,128)(2,1)S(1)} %get-tuple-element.12), kind=kOutput, calls=%fused_computation.57 | convolution fusion | flops 75497472 | bytes 4456448 | tf_op jit(solution)/shard_map/qphd,kphd->phqk/dot_general | solution.py:45
  142.2 6.1 %fusion.66 = (f32[8,16,64]{2,1,0:T(8,128)S(1)}, f32[8,16,64,64]{2,3,1,0:T(8,128)S(1)}) fusion(f32[8,16,64,64]{2,3,1,0:T(8,128)S(1)} %fusion.43), kind=kOutput, calls=%fused_computation.97 | output fusion | flops 2097215 | bytes 4227072 | tf_op jit(solution)/shard_map/sub | solution.py:21
  148.4 2.5 %convert_bitcast_fusion = bf16[64,8,16,72]{3,0,2,1:T(8,128)(2,1)S(1)} fusion(f32[8,16,64,64]{2,3,1,0:T(8,128)S(1)} %get-tuple-element.19, f32[8,16,64]{2,1,0:T(8,128)S(1)} %get-tuple-element.18, bf16[64,8,1,16,72]{4,3,2,1,0:T(8,128)(2,1)S(1)} %get-tuple-element.11), kind=kOutput, calls=%fused_computation.60 | convolution fusion | flops 77135872 | bytes 4489216 | tf_op jit(solution)/shard_map/phqk,kphd->qphd/dot_general | solution.py:49
  150.9 2.7 %copy.77 = bf16[64,8,16,72]{3,2,1,0:T(8,128)(2,1)} copy(bf16[64,8,16,72]{3,0,2,1:T(8,128)(2,1)S(1)} %convert_bitcast_fusion) | data formatting | bytes 2359296 | tf_op jit(solution)/shard_map/convert_element_type | solution.py:52
  153.6 4.6 %convert_element_type.115 = bf16[64,8,1152]{2,1,0:T(8,128)(2,1)} reshape(bf16[64,8,16,72]{3,2,1,0:T(8,128)(2,1)} %copy.77) | data formatting | bytes 2359296 | tf_op jit(solution)/shard_map/convert_element_type | solution.py:52
  158.2 5.8 %fusion.28 = bf16[512,1152]{1,0:T(8,128)(2,1)} fusion(f32[64,8,1152]{2,1,0:T(8,128)} %bitcast.106, bf16[64,8,1152]{2,1,0:T(8,128)(2,1)} %convert_element_type.115, bf16[1152,1152]{1,0:T(8,128)(2,1)} %param.16, f32[1152]{0:T(1024)S(1)} %copy-done.14), kind=kOutput, calls=%fused_computation.38 | convolution fusion | flops 1360723968 | bytes 7377408 | tf_op jit(solution)/shard_map/dot_general | solution.py:58
  164.0 5.9 %broadcast_select_fusion = (bf16[32,36,1152]{2,1,0:T(8,128)(2,1)}, bf16[32,36,1152]{2,1,0:T(8,128)(2,1)}) fusion(bf16[32,36,1152]{2,1,0:T(8,128)(2,1)S(1)} %all-to-all-done.1, pred[]{:T(512)S(6)} %eq.2, bf16[32,36,1152]{2,0,1:T(8,128)(2,1)} %collective-permute-done), kind=kLoop, calls=%fused_computation.34 | loop fusion | flops 2654208 | bytes 10616833 | tf_op jit(solution)/shard_map/jit(_where)/select_n | solution.py:70
  169.9 5.2 %reshape.154 = bf16[1152,1152]{1,0:T(8,128)(2,1)} reshape(bf16[32,36,1152]{2,1,0:T(8,128)(2,1)} %get-tuple-element.15) | data formatting | bytes 5308416 | tf_op jit(solution)/shard_map/reshape | solution.py:69
  175.1 5.1 %convolution_convert_fusion = bf16[512,1152]{1,0:T(8,128)(2,1)} fusion(bf16[512,1152]{1,0:T(8,128)(2,1)} %fusion.28, bf16[1152,1152]{1,0:T(8,128)(2,1)} %reshape.154), kind=kOutput, calls=%fused_computation.32 | convolution fusion | flops 1359544320 | bytes 5013504 | tf_op jit(solution)/shard_map/dot_general | solution.py:58
  180.2 2.4 %copy.80 = bf16[512,1152]{0,1:T(8,128)(2,1)} copy(bf16[512,1152]{1,0:T(8,128)(2,1)} %convolution_convert_fusion) | data formatting | bytes 2359296 | tf_op jit(solution)/shard_map/convert_element_type | solution.py:103
  182.6 2.2 %reshape.158 = bf16[1152,1152]{1,0:T(8,128)(2,1)} reshape(bf16[32,36,1152]{2,1,0:T(8,128)(2,1)S(1)} %copy-done.2) | data formatting | bytes 5308416 | tf_op jit(solution)/shard_map/reshape | solution.py:70
  184.8 4.9 %fusion.67 = (f32[16,512]{1,0:T(8,128)S(1)}, f32[16,512,120]{1,2,0:T(8,128)}) fusion(pred[120]{0:T(512)(128)(4,1)S(1)} %copy-done.15, bf16[512,16,72]{0,2,1:T(8,128)(2,1)} %bitcast.108, bf16[120,16,72]{0,2,1:T(8,128)(2,1)S(1)} %bitcast.113), kind=kOutput, calls=%fused_computation.98 | convolution fusion | flops 145490032 | bytes 5421176 | tf_op jit(solution)/shard_map/sub | solution.py:21
  189.7 2.7 %fusion.50 = bf16[16,512,72]{1,2,0:T(8,128)(2,1)S(1)} fusion(bf16[120,16,72]{0,2,1:T(8,128)(2,1)S(1)} %bitcast.112, f32[16,512,120]{1,2,0:T(8,128)} %get-tuple-element.21, f32[16,512]{1,0:T(8,128)S(1)} %get-tuple-element.20), kind=kOutput, calls=%fused_computation.67 | convolution fusion | flops 144113664 | bytes 5421056 | tf_op jit(solution)/shard_map/htl,lhd->thd/dot_general | solution.py:118
  192.4 0.2 copy-done.7
  192.6 0.3 copy-done.10
  192.9 1.9 fusion.29
  194.8 23.6 %all_to_all.32 = bf16[64,8,1152]{2,1,0:T(8,128)(2,1)S(1)} all-to-all(bf16[64,8,1152]{2,1,0:T(8,128)(2,1)S(1)} %fusion.29), channel_id=1, replica_groups=mesh['z_lo'=2,'x'=4,'y'=4,'z_hi'=2,'core'=2] {'z_lo','x','y'}, dimensions={0} | all-to-all | bytes 2359296 | tf_op jit(solution)/shard_map/all_to_all | solution.py:127
  218.4 1.1 copy.107
  (34 shorter events, 0.1 us)
Async XLA Ops:
  0.0 32.3 %copy-start = (bf16[1152,1152]{1,0:T(8,128)(2,1)S(1)}, bf16[1152,1152]{1,0:T(8,128)(2,1)}, u32[]{:S(2)}) copy-start(bf16[1152,1152]{1,0:T(8,128)(2,1)} %param.14) | copy-start | bytes 7962628
  0.0 5.0 %copy-start.5 = (bf16[2,256,1152]{2,1,0:T(8,128)(2,1)S(1)}, bf16[2,256,1152]{2,1,0:T(8,128)(2,1)}, u32[]{:S(2)}) copy-start(bf16[2,256,1152]{2,1,0:T(8,128)(2,1)} %param.11) | copy-start | bytes 3538948
  30.0 2.3 %copy-start.6 = (bf16[2,256,1152]{2,1,0:T(8,128)(2,1)S(1)}, bf16[2,256,1152]{2,1,0:T(8,128)(2,1)}, u32[]{:S(2)}) copy-start(bf16[2,256,1152]{2,1,0:T(8,128)(2,1)} %param.11) | copy-start | bytes 3538948
  34.3 11.5 %copy-start.12 = (bf16[36,1152]{1,0:T(8,128)(2,1)S(1)}, bf16[36,1152]{1,0:T(8,128)(2,1)}, u32[]{:S(2)}) copy-start(bf16[36,1152]{1,0:T(8,128)(2,1)} %param.17) | copy-start | bytes 248836
  34.3 11.5 %copy-start.13 = (bf16[36,1152]{1,0:T(8,128)(2,1)S(1)}, bf16[36,1152]{1,0:T(8,128)(2,1)}, u32[]{:S(2)}) copy-start(bf16[36,1152]{1,0:T(8,128)(2,1)} %param.18) | copy-start | bytes 248836
  36.5 25.6 %all-to-all-start = ((bf16[2,256,1152]{2,0,1:T(2,128)(2,1)}), bf16[2,256,1152]{2,0,1:T(2,128)(2,1)S(1)}, u32[]{:S(2)}, u32[]{:S(2)}) async-start(bf16[2,256,1152]{2,0,1:T(2,128)(2,1)} %copy.71), calls=%async_computation | async-start | bytes 2359296 | tf_op jit(solution)/shard_map/all_to_all | solution.py:95
  62.2 2.0 copy-start.3
  64.1 5.1 %copy-start.11 = (bf16[120,1152]{1,0:T(8,128)(2,1)S(1)}, bf16[120,1152]{1,0:T(8,128)(2,1)}, u32[]{:S(2)}) copy-start(bf16[120,1152]{1,0:T(8,128)(2,1)} %param.19) | copy-start | bytes 829444
  64.2 40.8 %all-to-all-start.1 = ((bf16[32,36,1152]{2,1,0:T(8,128)(2,1)}), bf16[32,36,1152]{2,1,0:T(8,128)(2,1)S(1)}, u32[]{:S(2)}, u32[]{:S(2)}) async-start(bf16[32,36,1152]{2,1,0:T(8,128)(2,1)} %broadcast_in_dim.11), calls=%async_computation.1 | async-start | bytes 5898240 | tf_op jit(solution)/shard_map/all_to_all | solution.py:67
  71.3 2.0 copy-start.4
  73.3 1.5 copy-start.8
  104.9 6.0 %copy-start.9 = (bf16[64,8,1152]{2,1,0:T(8,128)(2,1)S(1)}, bf16[64,8,1152]{2,1,0:T(8,128)(2,1)}, u32[]{:S(2)}) copy-start(bf16[64,8,1152]{2,1,0:T(8,128)(2,1)} %fusion.39) | copy-start | bytes 3538948
  106.8 57.2 %collective-permute-start = (bf16[32,36,1152]{2,0,1:T(8,128)(2,1)}, bf16[32,36,1152]{2,0,1:T(8,128)(2,1)}, u32[]{:S(2)}, u32[]{:S(2)}) collective-permute-start(bf16[32,36,1152]{2,0,1:T(8,128)(2,1)} %copy.78), channel_id=1, source_target_pairs={{0,1},{1,0},{2,3},{3,2},{4,5},{5,4},{6,7},{7,6},{8,9},{9,8},{10,11... | collective-permute-start | bytes 7962632 | tf_op jit(solution)/shard_map/ppermute | solution.py:68
  153.6 4.6 %copy-start.14 = (f32[1152]{0:T(1024)S(1)}, f32[1152]{0:T(1024)}, u32[]{:S(2)}) copy-start(f32[1152]{0:T(1024)} %get-tuple-element.5) | copy-start | bytes 13828
  175.1 7.5 %copy-start.2 = (bf16[32,36,1152]{2,1,0:T(8,128)(2,1)S(1)}, bf16[32,36,1152]{2,1,0:T(8,128)(2,1)}, u32[]{:S(2)}) copy-start(bf16[32,36,1152]{2,1,0:T(8,128)(2,1)} %get-tuple-element.14) | copy-start | bytes 7962628
  182.6 2.2 %copy-start.15 = (pred[120]{0:T(512)(128)(4,1)S(1)}, pred[120]{0:T(512)(128)(4,1)}, u32[]{:S(2)}) copy-start(pred[120]{0:T(512)(128)(4,1)} %iota_compare_fusion) | copy-start | bytes 364
  189.7 2.9 %copy-start.7 = (bf16[1152,1152]{1,0:T(8,128)(2,1)S(1)}, bf16[1152,1152]{1,0:T(8,128)(2,1)}, u32[]{:S(2)}) copy-start(bf16[1152,1152]{1,0:T(8,128)(2,1)} %reshape.158) | copy-start | bytes 7962628
  189.7 3.2 %copy-start.10 = (bf16[512,1152]{1,0:T(8,128)(2,1)S(1)}, bf16[512,1152]{1,0:T(8,128)(2,1)}, u32[]{:S(2)}) copy-start(bf16[512,1152]{1,0:T(8,128)(2,1)} %fusion.28) | copy-start | bytes 3538948
  192.9 26.6 %copy-start.1 = (bf16[1152,1152]{1,0:T(8,128)(2,1)S(1)}, bf16[1152,1152]{1,0:T(8,128)(2,1)}, u32[]{:S(2)}) copy-start(bf16[1152,1152]{1,0:T(8,128)(2,1)} %param.14) | copy-start | bytes 7962628

commit v2 on v1

v2 whole, which is shorter than its diff:
```python
import functools
import jax
import jax.numpy as jnp
import numpy as np
from jax import lax
from jax.experimental import pallas as pl
from jax.experimental.pallas import tpu as pltpu
from jax.sharding import Mesh, PartitionSpec as P

H = 16
HEAD = 72
LANES = 9
D = 1152
S = 256
T = 512
WIN = 256
SLOTS = 128
BLOCK = 144
SEQ = ("z_lo", "x", "y")
ALL = ("z_hi", "core", "z_lo", "x", "y")
EXP_SCALE = float(np.log2(np.e) / np.sqrt(72.0))
CHUNK = 768
F32 = jnp.float32
BF16 = jnp.bfloat16
NT = (((1,), (1,)), ((), ()))


def mm(a, b):
    return jnp.dot(a, b, preferred_element_type=F32)


def mm_nt(a, b):
    return lax.dot_general(a, b, NT, preferred_element_type=F32)


def window(head):
    return min(HEAD * head // 128 * 128, D - WIN)


def head_mask(head):
    lane = lax.broadcasted_iota(jnp.int32, (1, WIN), 1) + window(head)
    inside = (lane >= HEAD * head) & (lane < HEAD * head + HEAD)
    return jnp.where(inside, 1.0, 0.0).astype(BF16)


def identity(n):
    rows = lax.broadcasted_iota(jnp.int32, (n, n), 0)
    cols = lax.broadcasted_iota(jnp.int32, (n, n), 1)
    return jnp.where(rows == cols, 1.0, 0.0).astype(BF16)


def norm_mod(values, shift, scale):
    mean = jnp.mean(values, axis=-1, keepdims=True)
    centered = values - mean
    var = jnp.mean(centered * centered, axis=-1, keepdims=True)
    return (centered * lax.rsqrt(var + 1e-06) * (1.0 + scale) + shift).astype(BF16)


def column_chunks(width, chunk):
    return [(at, min(chunk, width - at)) for at in range(0, width, chunk)]


def fetch(src, dst, sems, chunk):
    copies = []
    for n, (at, size) in enumerate(column_chunks(src.shape[1], chunk)):
        cols = pl.ds(at, size)
        copies.append(pltpu.make_async_copy(src.at[:, cols], dst.at[:, cols], sems.at[n]))
    for copy in copies:
        copy.start()
    return copies


def transpose_into(dst, eye, src, at):
    for lo, size in column_chunks(D, WIN):
        dst[lo : lo + size, :] = mm_nt(eye[:size, :size], src(lo, size)).astype(dst.dtype)


def project_qkv(xn, w_vm, copies, qkv):
    for copy, (at, size) in zip(copies, column_chunks(3 * D, CHUNK)):
        copy.wait()
        for lo in range(0, xn.shape[0], S):
            rows = slice(lo, lo + S)
            qkv[rows, at : at + size] = mm(xn[rows, :], w_vm[:, at : at + size]).astype(BF16)


def softmax_cols(scores):
    top = jnp.max(scores, axis=0, keepdims=True)
    expo = jnp.exp2(scores * EXP_SCALE - top * EXP_SCALE)
    return expo, jnp.sum(expo, axis=0, keepdims=True)


def attend_full(scores):
    expo, total = softmax_cols(scores)
    return expo.astype(BF16), total


def attend_blocks(scores):
    lane = lax.broadcasted_iota(jnp.int32, (64, 128), 1)
    low = lane < 64
    left = jnp.where(low, scores[0:64, :128], scores[64:128, :128])
    right = jnp.where(low, scores[128:192, 128:], scores[192:256, 128:])
    le, lt = softmax_cols(left)
    re, rt = softmax_cols(right)
    zero = jnp.zeros((64, 128), F32)
    wide = jnp.concatenate(
        [
            jnp.concatenate([jnp.where(low, le, zero), zero], 1),
            jnp.concatenate([jnp.where(low, zero, le), zero], 1),
            jnp.concatenate([zero, jnp.where(low, re, zero)], 1),
            jnp.concatenate([zero, jnp.where(low, zero, re)], 1),
        ],
        0,
    )
    return wide.astype(BF16), jnp.concatenate([lt, rt], 1)


def self_attention(qkv, v_t, ctx_t, ctx, weigh):
    eye = identity(WIN)

    def group(g, carry):
        rows = pl.ds(g * S, S) if isinstance(g, int) else pl.ds(pl.multiple_of(g * S, S), S)
        transpose_into(v_t, eye, lambda lo, size: qkv[rows, 2 * D + lo : 2 * D + lo + size], 0)
        for head in range(H):
            at = window(head)
            query = qkv[rows, at : at + WIN] * head_mask(head)
            keys = qkv[rows, D + at : D + at + WIN]
            weights, total = weigh(mm_nt(keys, query))
            lo = head * HEAD
            mixed = mm(v_t[lo : lo + HEAD, :].astype(BF16), weights)
            ctx_t[lo : lo + HEAD, :] = mixed * (1.0 / total)
        ctx[rows, :] = mm_nt(eye, ctx_t[...].astype(BF16)).astype(BF16)
        return carry

    if qkv.shape[0] == S:
        group(0, 0)
    else:
        lax.fori_loop(0, qkv.shape[0] // S, group, 0)


def spatial_kernel(frame, *refs):
    if frame == 0:
        first, (lat, mod, w_hbm, wo_hbm, out, *scratch) = None, refs
    else:
        first, lat, mod, w_hbm, wo_hbm, out, *scratch = refs
    xn, w_vm, wo_vm, qkv, v_t, ctx_t, ctx, proj, sems, osem = scratch
    copies = fetch(w_hbm, w_vm, sems, CHUNK)
    out_copy = pltpu.make_async_copy(wo_hbm, wo_vm, osem)
    out_copy.start()
    shift, scale, gate = mod[0:1, :], mod[1:2, :], mod[2:3, :]

    def norm_rows(i, carry):
        rows = pl.ds(pl.multiple_of(i * 32, 32), 32)
        xn[rows, :] = norm_mod(lat[frame, rows, :].astype(F32), shift, scale)
        return carry

    lax.fori_loop(0, S // 32, norm_rows, 0)
    project_qkv(xn, w_vm, copies, qkv)
    self_attention(qkv, v_t, ctx_t, ctx, attend_full)
    out_copy.wait()
    proj[...] = mm(ctx[...], wo_vm[...])

    def finish(i, carry):
        rows = pl.ds(pl.multiple_of(i * 32, 32), 32)
        value = lat[frame, rows, :].astype(F32) + gate * proj[rows, :]
        if frame == 0:
            out[rows, :] = value.astype(BF16)
        else:
            parts = [first[rows, :].astype(F32).reshape(4, 8, D), value.reshape(4, 8, D)]
            out[pl.ds(pl.multiple_of(i * 4, 4), 4)] = jnp.concatenate(parts, axis=1).astype(BF16)
        return carry

    lax.fori_loop(0, S // 32, finish, 0)


def vmem():
    return pl.BlockSpec(memory_space=pltpu.VMEM)


def hbm():
    return pl.BlockSpec(memory_space=pl.ANY)


def block_scratch(rows):
    n = len(column_chunks(3 * D, CHUNK))
    return [
        pltpu.VMEM((rows, D), BF16),
        pltpu.VMEM((D, 3 * D), BF16),
        pltpu.VMEM((D, D), BF16),
        pltpu.VMEM((rows, 3 * D), BF16),
        pltpu.VMEM((D, S), F32),
        pltpu.VMEM((D, S), F32),
        pltpu.VMEM((rows, D), BF16),
        pltpu.VMEM((rows, D), F32),
        pltpu.SemaphoreType.DMA((n,)),
        pltpu.SemaphoreType.DMA,
    ]


PARAMS = pltpu.CompilerParams(vmem_limit_bytes=48 * 1024 * 1024)


def spatial(frame, first, lat, mod, w, wo):
    shape = (S, D) if frame == 0 else (32, 16, D)
    lead = [] if frame == 0 else [first]
    return pl.pallas_call(
        functools.partial(spatial_kernel, frame),
        out_shape=jax.ShapeDtypeStruct(shape, BF16),
        in_specs=[vmem()] * len(lead) + [vmem(), vmem(), hbm(), hbm()],
        out_specs=vmem(),
        scratch_shapes=block_scratch(S),
        compiler_params=PARAMS,
        cost_estimate=pl.CostEstimate(flops=4_000_000_000, bytes_accessed=13_000_000, transcendentals=1_000_000),
        name=f"spatial_{frame}",
    )(*lead, lat, mod, w, wo)


def temporal_kernel(x, mod, w_hbm, wo_hbm, out, xn, w_vm, wo_vm, qkv, v_t, ctx_t, ctx, proj, sems, osem, wide):
    copies = fetch(w_hbm, w_vm, sems, CHUNK)
    out_copy = pltpu.make_async_copy(wo_hbm, wo_vm, osem)
    out_copy.start()
    shift, scale, gate = mod[3:4, :], mod[4:5, :], mod[5:6, :]

    def widen(i, carry):
        value = x[i].astype(F32)
        for j in range(LANES):
            wide[j, pl.ds(pl.multiple_of(i * 16, 16), 16), :] = value[:, j * 128 : j * 128 + 128]
        return carry

    lax.fori_loop(0, 32, widen, 0, unroll=4)

    def norm_rows(i, carry):
        p, q = i // 2, i % 2
        picked = pl.ds(q * 256 + p, 32, stride=8)
        values = jnp.concatenate([wide[j, picked, :] for j in range(LANES)], axis=1)
        rows = pl.ds(pl.multiple_of(i * 32, 32), 32)
        out[rows, :] = values.astype(BF16)
        xn[rows, :] = norm_mod(values, shift, scale)
        return carry

    lax.fori_loop(0, 16, norm_rows, 0)
    project_qkv(xn, w_vm, copies, qkv)
    self_attention(qkv, v_t, ctx_t, ctx, attend_blocks)
    out_copy.wait()
    for f in range(2):
        rows = slice(f * S, f * S + S)
        proj[rows, :] = mm(ctx[rows, :], wo_vm[...])

    def finish(i, carry):
        rows = pl.ds(pl.multiple_of(i * 32, 32), 32)
        out[rows, :] = (out[rows, :].astype(F32) + gate * proj[rows, :]).astype(BF16)
        return carry

    lax.fori_loop(0, 16, finish, 0)


def temporal(x, mod, w, wo):
    return pl.pallas_call(
        temporal_kernel,
        out_shape=jax.ShapeDtypeStruct((T, D), BF16),
        in_specs=[vmem(), vmem(), hbm(), hbm()],
        out_specs=vmem(),
        scratch_shapes=block_scratch(T) + [pltpu.VMEM((LANES, T, 128), F32)],
        compiler_params=PARAMS,
        cost_estimate=pl.CostEstimate(flops=8_000_000_000, bytes_accessed=13_000_000, transcendentals=600_000),
        name="temporal",
    )(x, mod, w, wo)


def cross_kernel(place, x, keys, values, *refs):
    pieces, (out, w_vm, query, v_t, ctx_t, ctx, wide, sems) = refs[:10], refs[10:]
    length, core, z_lo, x_at = place[0], place[1], place[2], place[3]

    def put(which, src, z, x_from):
        rows = pl.ds(pl.multiple_of(z * (D // 2) + x_from * BLOCK, 16), BLOCK)
        pltpu.make_async_copy(src, w_vm.at[which, rows, :], sems.at[which]).start()

    left, right, far = (x_at + 3) % 4, (x_at + 1) % 4, (x_at + 2) % 4
    for own in range(2):
        which = core if own == 0 else 1 - core
        here, from_left, from_right, far_same, far_other = pieces[5 * own : 5 * own + 5]
        for n, z in enumerate((z_lo, 1 - z_lo)):
            put(which, here.at[n], z, x_at)
            put(which, from_left.at[n], z, left)
            put(which, from_right.at[n], z, right)
        put(which, far_same, z_lo, far)
        put(which, far_other, 1 - z_lo, far)

    def whole(which):
        pltpu.make_async_copy(w_vm.at[which], w_vm.at[which], sems.at[which]).wait()

    eye = identity(WIN)
    for lo, size in column_chunks(D, WIN):
        v_t[lo : lo + size, :] = mm_nt(eye[:size, :size], values[:, lo : lo + size])
    whole(0)
    for f in range(2):
        rows = slice(f * S, f * S + S)
        query[rows, :] = mm(x[rows, :], w_vm[0]).astype(BF16)
    valid = lax.broadcasted_iota(jnp.int32, (SLOTS, S), 0) < length

    def group(g, carry):
        rows = pl.ds(pl.multiple_of(g * S, S), S)
        for head in range(H):
            at = window(head)
            masked = keys[:, at : at + WIN] * head_mask(head)
            scores = mm_nt(masked, query[rows, at : at + WIN])
            expo, total = softmax_cols(jnp.where(valid, scores, -1e30))
            lo = head * HEAD
            mixed = mm(v_t[lo : lo + HEAD, :].astype(BF16), expo.astype(BF16))
            ctx_t[lo : lo + HEAD, :] = mixed * (1.0 / total)
        ctx[rows, :] = mm_nt(eye, ctx_t[...].astype(BF16)).astype(BF16)
        return carry

    lax.fori_loop(0, 2, group, 0)
    whole(1)
    for f in range(2):
        rows = slice(f * S, f * S + S)
        ctx_rows = mm(ctx[rows, :], w_vm[1])
        value = x[rows, :].astype(F32) + ctx_rows
        for p in range(4):
            for j in range(LANES):
                wide[j, pl.ds(f * 4 + p, 64, stride=8), :] = value[p * 64 : p * 64 + 64, j * 128 : j * 128 + 128]

    def narrow(i, carry):
        rows = pl.ds(pl.multiple_of(i * 16, 16), 16)
        out[i] = jnp.concatenate([wide[j, rows, :] for j in range(LANES)], axis=1).astype(BF16)
        return carry

    lax.fori_loop(0, 32, narrow, 0, unroll=4)


def cross(place, x, keys, values, pieces):
    return pl.pallas_call(
        cross_kernel,
        out_shape=jax.ShapeDtypeStruct((32, 16, D), BF16),
        in_specs=[pl.BlockSpec(memory_space=pltpu.SMEM), vmem(), vmem(), vmem()] + [hbm()] * len(pieces),
        out_specs=vmem(),
        scratch_shapes=[
            pltpu.VMEM((2, D, D), BF16),
            pltpu.VMEM((T, D), BF16),
            pltpu.VMEM((D, SLOTS), F32),
            pltpu.VMEM((D, S), F32),
            pltpu.VMEM((T, D), BF16),
            pltpu.VMEM((LANES, T, 128), F32),
            pltpu.SemaphoreType.DMA((2,)),
        ],
        compiler_params=PARAMS,
        cost_estimate=pl.CostEstimate(flops=4_000_000_000, bytes_accessed=8_000_000, transcendentals=1_000_000),
        name="cross",
    )(place, x, keys, values, *pieces)


def shift(array, axis, by, size):
    return lax.ppermute(array, axis, [(i, (i + by) % size) for i in range(size)])


def gather_first(cross_query, cross_out):
    mine = jnp.where(lax.axis_index("core") == 0, cross_query, cross_out)

    def over_yz(by_z, by):
        pairs = [
            (z * 4 + y, (z + by_z) % 2 * 4 + (y + by) % 4) for z in range(2) for y in range(4)
        ]
        return lax.ppermute(mine, ("z_lo", "y"), pairs)

    found = []
    for by_z in range(2):
        rows = [mine if (by_z, by) == (0, 0) else over_yz(by_z, by) for by in (3, 2, 1, 0)]
        found.append(jnp.stack(rows + rows[:3]))
    found = jnp.stack(found)
    start = 3 - lax.axis_index("y")
    ordered = lax.dynamic_slice_in_dim(found, start, 4, axis=1)
    return ordered.reshape(2, BLOCK, D)


def gather_second(here):
    left = shift(here, "x", 1, 4)
    right = shift(here, "x", -1, 4)
    far_same = shift(left[0], "x", 1, 4)
    far_other = shift(right[1], "x", -1, 4)
    pieces = [here, left, right, far_same, far_other]
    return pieces + [shift(piece, "core", 1, 2) for piece in pieces]


def body(
    latent,
    modulation,
    w_spatial_qkv,
    w_spatial_out,
    w_temporal_qkv,
    w_temporal_out,
    cross_query,
    cross_out,
    text_keys,
    text_values,
    text_len,
):
    near = gather_first(cross_query, cross_out)
    first = spatial(0, None, latent, modulation, w_spatial_qkv, w_spatial_out)
    near, first = lax.optimization_barrier((near, first))
    pieces = gather_second(near)
    after_spatial = spatial(1, first, latent, modulation, w_spatial_qkv, w_spatial_out)
    placed = lax.all_to_all(after_spatial, SEQ, split_axis=0, concat_axis=0, tiled=True)
    after_temporal = temporal(placed, modulation, w_temporal_qkv, w_temporal_out)
    place = jnp.stack(
        [text_len[0], lax.axis_index("core"), lax.axis_index("z_lo"), lax.axis_index("x")]
    ).astype(jnp.int32)
    fill = ((0, SLOTS - text_keys.shape[0]), (0, 0))
    keys, values = jnp.pad(text_keys, fill), jnp.pad(text_values, fill)
    result = cross(place, after_temporal, keys, values, pieces)
    returned = lax.all_to_all(result, SEQ, split_axis=0, concat_axis=0, tiled=True)
    return returned.reshape(32, 2, 8, D).transpose(1, 0, 2, 3).reshape(2, S, D)


def solution(mesh):
    fine = Mesh(mesh.devices.reshape(2, 4, 4, 2, 2), ("z_lo", "x", "y", "z_hi", "core"))
    part = ("z_hi", "core")
    placed = (
        P(ALL, None, None),
        P(part, None),
        P(),
        P(),
        P(),
        P(),
        P(SEQ, None),
        P(SEQ, None),
        P(part, None),
        P(part, None),
        P(part),
    )
    return jax.shard_map(
        body, mesh=fine, in_specs=placed, out_specs=P(ALL, None, None), check_vma=False
    )
```

time: 221 us -> 145 us (0.66)
  Pallas kernels: 0 us -> 58.5 us
  matrix products: 52.1 us -> 0 us
  local copies, waits for them, and re-layouts: 52.6 us -> 11.9 us
  waiting for transfers between devices: 45 us -> 10.1 us
  other arithmetic: 26.8 us -> 1.09 us
  starting transfers between devices: 18.4 us -> 36.3 us
    pallas_call x0 -> x4, Pallas kernels: none -> 58.5 us  [the longest x2 22.6 us: spatial(): pl.pallas_call(functools.partial(spatial_kernel, frame), out_shape=jax.Sh...]
    dot_general x11 -> x0, matrix products: 47.2 us -> none  [the longest x6 34.2 us: project(): jnp.dot(flat, weight, preferred_element_type=jnp.float32)]
    all_to_all x2 -> x1, waiting for transfers between devices: 45 us -> 0.01 us  [body(): lax.all_to_all(after_spatial, SEQ, split_axis=0, concat_axis=0, tiled=True)]
    ppermute x1 -> x16, starting transfers between devices: 4.14 us -> 30.3 us  [the longest x9 18.5 us: shift(): lax.ppermute(array, axis, [(i, (i + by) % size) for i in range(size)])]
    reshape x3 -> x1, local copies, waits for them, and re-layouts: 21 us -> 1.1 us  [body(): return returned.reshape(32, 2, 8, D).transpose(1, 0, 2, 3).reshape(2, S, D)]
    convert_element_type x6 -> x0, local copies, waits for them, and re-layouts: 19.1 us -> none  [the longest x2 7.3 us: across_frames(): return mixed.reshape(frames, places, width).astype(jnp.bfloat16)]
    sub x2 -> x0, other arithmetic: 12.4 us -> none  [softmax_weights(): expo = jnp.exp(scores - top)]
    ppermute x1 -> x16, waiting for transfers between devices: 0.01 us -> 10.1 us  [the longest x7 6.27 us: over_yz(): return lax.ppermute(mine, ('z_lo', 'y'), pairs)]
  transfers between devices with their start and end apart: 3 -> 17, of which waited for: 2 -> 3; matrix products, arithmetic and copies ran while one was open for 27% -> 3% of each run, Pallas kernels for 0% -> 29%
where the time goes in v2:
time: 145 us; the launch traced here: 144 us
  Pallas kernels  58.5 us (40%)
  starting transfers between devices  36.3 us (25%)
  blocking collectives  25.3 us (17%)
  local copies, waits for them, and re-layouts  11.9 us (8%)
  waiting for transfers between devices  10.1 us (7%)
    all_to_all x1, blocking collectives, body(): lax.all_to_all(result, SEQ, split_axis=0, concat_axis=0, tiled=True)  25.3 us
    pallas_call x2, Pallas kernels, spatial(): pl.pallas_call(functools.partial(spatial_kernel, frame), out_shape=jax.Sh...  22.6 us
    pallas_call x1, Pallas kernels, temporal(): pl.pallas_call(temporal_kernel, out_shape=jax.ShapeDtypeStruct((T, D), BF...  18.7 us
    ppermute x9, starting transfers between devices, shift(): lax.ppermute(array, axis, [(i, (i + by) % size) for i in range(size)])  18.5 us
    pallas_call x1, Pallas kernels, cross(): pl.pallas_call(cross_kernel, out_shape=jax.ShapeDtypeStruct((32, 16, D),...  17.3 us
    ppermute x7, starting transfers between devices, over_yz(): return lax.ppermute(mine, ('z_lo', 'y'), pairs)  11.8 us
    unnamed x30, local copies, waits for them, and re-layouts  6.74 us
    ppermute x7, waiting for transfers between devices, over_yz(): return lax.ppermute(mine, ('z_lo', 'y'), pairs)  6.27 us
  transfers between devices with their start and end apart: 17, of which 3 were waited for; matrix products, arithmetic and copies ran while one was open for 3% of the time, Pallas kernels for 29%

profile of v2, /device:TPU:1, one launch (start us, length us, event | category | flops | bytes accessed | tf_op | source)
XLA Modules:
  0.0 144.1 jit_solution(15443576910495205356)
XLA Ops:
  0.0 0.9 broadcast_select_fusion
  0.9 2.5 %collective-permute-start.6 = (bf16[36,1152]{1,0:T(8,128)(2,1)S(1)}, bf16[36,1152]{1,0:T(8,128)(2,1)S(1)}, u32[]{:S(2)}, u32[]{:S(2)}) collective-permute-start(bf16[36,1152]{1,0:T(8,128)(2,1)S(1)} %broadcast_select_fusion), channel_id=1, source_target_pairs={{0,64},{4,68},{8,72},{12,76},{64,0},{68,4},{72,8},{76,12},{1,65},{... | collective-permute-start | bytes 248840 | tf_op jit(solution)/shard_map/ppermute | solution.py:363
  3.5 1.1 collective-permute-start.5
  4.5 3.7 %collective-permute-start.4 = (bf16[36,1152]{1,0:T(8,128)(2,1)S(1)}, bf16[36,1152]{1,0:T(8,128)(2,1)S(1)}, u32[]{:S(2)}, u32[]{:S(2)}) collective-permute-start(bf16[36,1152]{1,0:T(8,128)(2,1)S(1)} %broadcast_select_fusion), channel_id=1, source_target_pairs={{0,72},{4,76},{8,64},{12,68},{64,8},{68,12},{72,0},{76,4},{1,73},{... | collective-permute-start | bytes 248840 | tf_op jit(solution)/shard_map/ppermute | solution.py:363
  8.3 0.9 collective-permute-start.3
  9.1 0.2 collective-permute-start
  9.3 1.7 %copy-done = bf16[1152,1152]{1,0:T(8,128)(2,1)S(1)} copy-done((bf16[1152,1152]{1,0:T(8,128)(2,1)S(1)}, bf16[1152,1152]{1,0:T(8,128)(2,1)}, u32[]{:S(2)}) %copy-start) | copy-done | bytes 2654232
  11.1 1.3 copy-done.3
  12.4 0.8 copy-done.5
  13.1 10.8 %spatial_0.1.refs_0_ = bf16[256,1152]{1,0:T(8,128)(2,1)S(1)} custom-call(bf16[2,256,1152]{2,1,0:T(8,128)(2,1)S(1)} %copy-done.3, f32[6,1152]{1,0:T(8,128)S(1)} %copy-done.5, bf16[1152,3456]{1,0:T(8,128)(2,1)} %refs_3_.3, bf16[1152,1152]{1,0:T(8,128)(2,1)S(1)} %copy-done), custom_call_target="tpu_custom_call" | custom-call | flops 4000000000 | bytes 13000000 | tf_op jit(solution)/shard_map/spatial_0/pallas_call | solution.py:205
  23.9 0.0 collective-permute-done
  23.9 2.1 %collective-permute-start.1 = (bf16[36,1152]{1,0:T(8,128)(2,1)S(1)}, bf16[36,1152]{1,0:T(8,128)(2,1)S(1)}, u32[]{:S(2)}, u32[]{:S(2)}) collective-permute-start(bf16[36,1152]{1,0:T(8,128)(2,1)S(1)} %broadcast_select_fusion), channel_id=1, source_target_pairs={{0,8},{4,12},{8,0},{12,4},{64,72},{68,76},{72,64},{76,68},{1,9},{5... | collective-permute-start | bytes 248840 | tf_op jit(solution)/shard_map/ppermute | solution.py:363
  26.0 2.9 %collective-permute-done.1 = bf16[36,1152]{1,0:T(8,128)(2,1)S(1)} collective-permute-done((bf16[36,1152]{1,0:T(8,128)(2,1)S(1)}, bf16[36,1152]{1,0:T(8,128)(2,1)S(1)}, u32[]{:S(2)}, u32[]{:S(2)}) %collective-permute-start.1) | collective-permute-done | bytes 82976 | tf_op jit(solution)/shard_map/ppermute | solution.py:363
  28.9 1.3 collective-permute-start.2
  30.2 3.3 %collective-permute-done.2 = bf16[36,1152]{1,0:T(8,128)(2,1)S(1)} collective-permute-done((bf16[36,1152]{1,0:T(8,128)(2,1)S(1)}, bf16[36,1152]{1,0:T(8,128)(2,1)S(1)}, u32[]{:S(2)}, u32[]{:S(2)}) %collective-permute-start.2) | collective-permute-done | bytes 82976 | tf_op jit(solution)/shard_map/ppermute | solution.py:363
  33.6 0.0 collective-permute-done.3
  33.8 0.0 copy-start.4
  33.8 0.1 fusion
  33.9 0.0 copy-start.1
  33.9 0.0 copy-start.6
  33.9 0.5 copy.13
  34.4 0.1 copy.17.refs_0_
  34.5 2.5 %collective-permute-start.8 = (bf16[2,144,1152]{2,1,0:T(8,128)(2,1)S(1)}, bf16[2,144,1152]{2,1,0:T(8,128)(2,1)S(1)}, u32[]{:S(2)}, u32[]{:S(2)}) collective-permute-start(bf16[2,144,1152]{2,1,0:T(8,128)(2,1)S(1)} %copy.17.refs_0_), channel_id=1, source_target_pairs={{0,48},{16,0},{32,16},{48,32},{1,49},{17,1},{33,17},{49,33},{2,50}... | collective-permute-start | bytes 1990664 | tf_op jit(solution)/shard_map/ppermute | solution.py:353
  37.1 0.0 collective-permute-start.7
  37.1 11.8 %spatial_1.1 = bf16[32,16,1152]{2,1,0:T(8,128)(2,1)} custom-call(bf16[256,1152]{1,0:T(8,128)(2,1)S(1)} %spatial_0.1.refs_0_, bf16[2,256,1152]{2,1,0:T(8,128)(2,1)S(1)} %copy-done.4, f32[6,1152]{1,0:T(8,128)S(1)} %copy-done.6, bf16[1152,3456]{1,0:T(8,128)(2,1)} %refs_3_.3, bf16[1152,1152]{1,0:T(8,128)(2,1)S(1)} %copy-done.1), custom_call_target="tpu_custom_call" | custom-call | flops 4000000000 | bytes 13000000 | tf_op jit(solution)/shard_map/spatial_1/pallas_call | solution.py:205
  48.9 6.0 %all-to-all-start = ((bf16[32,16,1152]{2,1,0:T(8,128)(2,1)}), bf16[32,16,1152]{2,1,0:T(8,128)(2,1)S(1)}, u32[]{:S(2)}, u32[]{:S(2)}) async-start(bf16[32,16,1152]{2,1,0:T(8,128)(2,1)} %spatial_1.1), calls=%async_computation | async-start | bytes 2359296 | tf_op jit(solution)/shard_map/all_to_all | solution.py:402
  55.0 0.0 copy-start.8
  55.0 0.0 collective-permute-done.8.refs_2_
  55.0 0.7 slice_bitcast_fusion
  55.7 2.4 %collective-permute-start.10 = (bf16[144,1152]{1,0:T(8,128)(2,1)}, bf16[144,1152]{1,0:T(8,128)(2,1)S(1)}, u32[]{:S(2)}, u32[]{:S(2)}) collective-permute-start(bf16[144,1152]{1,0:T(8,128)(2,1)} %slice_bitcast_fusion), channel_id=1, source_target_pairs={{0,48},{16,0},{32,16},{48,32},{1,49},{17,1},{33,17},{49,33},{2,50}... | collective-permute-start | bytes 995336 | tf_op jit(solution)/shard_map/ppermute | solution.py:353
  58.2 0.0 collective-permute-done.7.refs_1_
  58.2 1.7 %slice_bitcast_fusion.1 = bf16[144,1152]{1,0:T(8,128)(2,1)} fusion(bf16[2,144,1152]{2,1,0:T(8,128)(2,1)} %collective-permute-done.7.refs_1_), kind=kLoop, calls=%fused_computation.5 | loop fusion | bytes 663552 | tf_op jit(solution)/shard_map/squeeze | solution.py:378
  59.9 0.0 collective-permute-start.9
  60.6 1.0 pad.8.values
  61.6 0.1 pad_add_fusion.place
  61.7 5.7 %collective-permute-start.11 = (bf16[2,144,1152]{2,1,0:T(8,128)(2,1)S(1)}, bf16[2,144,1152]{2,1,0:T(8,128)(2,1)}, u32[]{:S(2)}, u32[]{:S(2)}) collective-permute-start(bf16[2,144,1152]{2,1,0:T(8,128)(2,1)S(1)} %copy.17.refs_0_), channel_id=1, source_target_pairs={{0,1},{1,0},{2,3},{3,2},{4,5},{5,4},{6,7},{7,6},{8,9},{9,8},{10,11... | collective-permute-start | bytes 1990664 | tf_op jit(solution)/shard_map/ppermute | solution.py:353
  67.3 0.1 collective-permute-start.13
  67.4 0.4 collective-permute-start.12
  67.9 3.8 %collective-permute-done.10.refs_4_ = bf16[144,1152]{1,0:T(8,128)(2,1)S(1)} collective-permute-done((bf16[144,1152]{1,0:T(8,128)(2,1)}, bf16[144,1152]{1,0:T(8,128)(2,1)S(1)}, u32[]{:S(2)}, u32[]{:S(2)}) %collective-permute-start.10) | collective-permute-done | bytes 331808 | tf_op jit(solution)/shard_map/ppermute | solution.py:353
  71.6 6.0 %collective-permute-start.15 = (bf16[144,1152]{1,0:T(8,128)(2,1)S(1)}, bf16[144,1152]{1,0:T(8,128)(2,1)}, u32[]{:S(2)}, u32[]{:S(2)}) collective-permute-start(bf16[144,1152]{1,0:T(8,128)(2,1)S(1)} %collective-permute-done.10.refs_4_), channel_id=1, source_target_pairs={{0,1},{1,0},{2,3},{3,2},{4,5},{5,4},{6,7},{7,6},{8,9},{9,8},{10,11... | collective-permute-start | bytes 995336 | tf_op jit(solution)/shard_map/ppermute | solution.py:353
  77.7 1.3 collective-permute-start.14
  79.0 1.7 %copy-done.2 = bf16[1152,1152]{1,0:T(8,128)(2,1)S(1)} copy-done((bf16[1152,1152]{1,0:T(8,128)(2,1)S(1)}, bf16[1152,1152]{1,0:T(8,128)(2,1)}, u32[]{:S(2)}) %copy-start.2) | copy-done | bytes 2654232
  80.7 18.7 %temporal.1.x = bf16[512,1152]{1,0:T(8,128)(2,1)S(1)} custom-call(bf16[32,16,1152]{2,1,0:T(8,128)(2,1)S(1)} %all-to-all-done.x, f32[6,1152]{1,0:T(8,128)S(1)} %copy-done.6, bf16[1152,3456]{1,0:T(8,128)(2,1)} %w_hbm.1, bf16[1152,1152]{1,0:T(8,128)(2,1)S(1)} %copy-done.2), custom_call_target="tpu_custom_call" | custom-call | flops 8000000000 | bytes 13000000 | tf_op jit(solution)/shard_map/temporal/pallas_call | solution.py:257
  99.4 0.0 copy-start.7
  99.4 1.0 copy-done.7
  100.5 17.3 %cross.1 = bf16[32,16,1152]{2,1,0:T(8,128)(2,1)} custom-call(s32[4]{0:T(128)S(1)} %pad_add_fusion.place, bf16[512,1152]{1,0:T(8,128)(2,1)} %copy-done.7, bf16[128,1152]{1,0:T(8,128)(2,1)S(1)} %pad.7.keys, bf16[128,1152]{1,0:T(8,128)(2,1)S(1)} %pad.8.values, bf16[2,144,1152]{2,1,0:T(8,128)(2,1)S(1)} %copy.17.refs_0_, ...), custom_call_target="tpu_custom_call" | custom-call | flops 4000000000 | bytes 8000000 | tf_op jit(solution)/shard_map/cross/pallas_call | solution.py:332
  117.7 25.3 %all_to_all.10 = bf16[32,16,1152]{2,1,0:T(8,128)(2,1)S(1)} all-to-all(bf16[32,16,1152]{2,1,0:T(8,128)(2,1)} %cross.1), channel_id=1, replica_groups=mesh['z_lo'=2,'x'=4,'y'=4,'z_hi'=2,'core'=2] {'z_lo','x','y'}, dimensions={0} | all-to-all | bytes 2359296 | tf_op jit(solution)/shard_map/all_to_all | solution.py:410
  143.0 1.1 copy_bitcast_fusion
  (33 shorter events, 0.3 us)
Async XLA Ops:
  0.9 32.8 %collective-permute-start.6 = (bf16[36,1152]{1,0:T(8,128)(2,1)S(1)}, bf16[36,1152]{1,0:T(8,128)(2,1)S(1)}, u32[]{:S(2)}, u32[]{:S(2)}) collective-permute-start(bf16[36,1152]{1,0:T(8,128)(2,1)S(1)} %broadcast_select_fusion), channel_id=1, source_target_pairs={{0,64},{4,68},{8,72},{12,76},{64,0},{68,4},{72,8},{76,12},{1,65},{... | collective-permute-start | bytes 248840 | tf_op jit(solution)/shard_map/ppermute | solution.py:363
  3.5 30.2 %collective-permute-start.5 = (bf16[36,1152]{1,0:T(8,128)(2,1)S(1)}, bf16[36,1152]{1,0:T(8,128)(2,1)S(1)}, u32[]{:S(2)}, u32[]{:S(2)}) collective-permute-start(bf16[36,1152]{1,0:T(8,128)(2,1)S(1)} %broadcast_select_fusion), channel_id=1, source_target_pairs={{0,68},{4,72},{8,76},{12,64},{64,4},{68,8},{72,12},{76,0},{1,69},{... | collective-permute-start | bytes 248840 | tf_op jit(solution)/shard_map/ppermute | solution.py:363
  4.5 29.1 %collective-permute-start.4 = (bf16[36,1152]{1,0:T(8,128)(2,1)S(1)}, bf16[36,1152]{1,0:T(8,128)(2,1)S(1)}, u32[]{:S(2)}, u32[]{:S(2)}) collective-permute-start(bf16[36,1152]{1,0:T(8,128)(2,1)S(1)} %broadcast_select_fusion), channel_id=1, source_target_pairs={{0,72},{4,76},{8,64},{12,68},{64,8},{68,12},{72,0},{76,4},{1,73},{... | collective-permute-start | bytes 248840 | tf_op jit(solution)/shard_map/ppermute | solution.py:363
  8.3 25.3 %collective-permute-start.3 = (bf16[36,1152]{1,0:T(8,128)(2,1)S(1)}, bf16[36,1152]{1,0:T(8,128)(2,1)S(1)}, u32[]{:S(2)}, u32[]{:S(2)}) collective-permute-start(bf16[36,1152]{1,0:T(8,128)(2,1)S(1)} %broadcast_select_fusion), channel_id=1, source_target_pairs={{0,76},{4,64},{8,68},{12,72},{64,12},{68,0},{72,4},{76,8},{1,77},{... | collective-permute-start | bytes 248840 | tf_op jit(solution)/shard_map/ppermute | solution.py:363
  9.1 14.8 %collective-permute-start = (bf16[36,1152]{1,0:T(8,128)(2,1)S(1)}, bf16[36,1152]{1,0:T(8,128)(2,1)S(1)}, u32[]{:S(2)}, u32[]{:S(2)}) collective-permute-start(bf16[36,1152]{1,0:T(8,128)(2,1)S(1)} %broadcast_select_fusion), channel_id=1, source_target_pairs={{0,12},{4,0},{8,4},{12,8},{64,76},{68,64},{72,68},{76,72},{1,13},{... | collective-permute-start | bytes 248840 | tf_op jit(solution)/shard_map/ppermute | solution.py:363
  9.3 1.7 %copy-start = (bf16[1152,1152]{1,0:T(8,128)(2,1)S(1)}, bf16[1152,1152]{1,0:T(8,128)(2,1)}, u32[]{:S(2)}) copy-start(bf16[1152,1152]{1,0:T(8,128)(2,1)} %refs_4_.1) | copy-start | bytes 7962628
  11.1 1.3 copy-start.3
  12.4 0.8 copy-start.5
  23.9 5.0 %collective-permute-start.1 = (bf16[36,1152]{1,0:T(8,128)(2,1)S(1)}, bf16[36,1152]{1,0:T(8,128)(2,1)S(1)}, u32[]{:S(2)}, u32[]{:S(2)}) collective-permute-start(bf16[36,1152]{1,0:T(8,128)(2,1)S(1)} %broadcast_select_fusion), channel_id=1, source_target_pairs={{0,8},{4,12},{8,0},{12,4},{64,72},{68,76},{72,64},{76,68},{1,9},{5... | collective-permute-start | bytes 248840 | tf_op jit(solution)/shard_map/ppermute | solution.py:363
  28.9 4.6 %collective-permute-start.2 = (bf16[36,1152]{1,0:T(8,128)(2,1)S(1)}, bf16[36,1152]{1,0:T(8,128)(2,1)S(1)}, u32[]{:S(2)}, u32[]{:S(2)}) collective-permute-start(bf16[36,1152]{1,0:T(8,128)(2,1)S(1)} %broadcast_select_fusion), channel_id=1, source_target_pairs={{0,4},{4,8},{8,12},{12,0},{64,68},{68,72},{72,76},{76,64},{1,5},{5... | collective-permute-start | bytes 248840 | tf_op jit(solution)/shard_map/ppermute | solution.py:363
  33.8 3.3 %copy-start.4 = (bf16[2,256,1152]{2,1,0:T(8,128)(2,1)S(1)}, bf16[2,256,1152]{2,1,0:T(8,128)(2,1)}, u32[]{:S(2)}) copy-start(bf16[2,256,1152]{2,1,0:T(8,128)(2,1)} %refs_1_.3) | copy-start | bytes 3538948
  33.9 3.2 %copy-start.1 = (bf16[1152,1152]{1,0:T(8,128)(2,1)S(1)}, bf16[1152,1152]{1,0:T(8,128)(2,1)}, u32[]{:S(2)}) copy-start(bf16[1152,1152]{1,0:T(8,128)(2,1)} %refs_4_.1) | copy-start | bytes 7962628
  33.9 3.2 %copy-start.6 = (f32[6,1152]{1,0:T(8,128)S(1)}, f32[6,1152]{1,0:T(8,128)}, u32[]{:S(2)}) copy-start(f32[6,1152]{1,0:T(8,128)} %mod.1) | copy-start | bytes 82948
  34.5 20.4 %collective-permute-start.8 = (bf16[2,144,1152]{2,1,0:T(8,128)(2,1)S(1)}, bf16[2,144,1152]{2,1,0:T(8,128)(2,1)S(1)}, u32[]{:S(2)}, u32[]{:S(2)}) collective-permute-start(bf16[2,144,1152]{2,1,0:T(8,128)(2,1)S(1)} %copy.17.refs_0_), channel_id=1, source_target_pairs={{0,48},{16,0},{32,16},{48,32},{1,49},{17,1},{33,17},{49,33},{2,50}... | collective-permute-start | bytes 1990664 | tf_op jit(solution)/shard_map/ppermute | solution.py:353
  37.1 21.1 %collective-permute-start.7 = (bf16[2,144,1152]{2,1,0:T(8,128)(2,1)S(1)}, bf16[2,144,1152]{2,1,0:T(8,128)(2,1)}, u32[]{:S(2)}, u32[]{:S(2)}) collective-permute-start(bf16[2,144,1152]{2,1,0:T(8,128)(2,1)S(1)} %copy.17.refs_0_), channel_id=1, source_target_pairs={{0,16},{16,32},{32,48},{48,0},{1,17},{17,33},{33,49},{49,1},{2,18}... | collective-permute-start | bytes 1990664 | tf_op jit(solution)/shard_map/ppermute | solution.py:353
  48.9 30.1 %all-to-all-start = ((bf16[32,16,1152]{2,1,0:T(8,128)(2,1)}), bf16[32,16,1152]{2,1,0:T(8,128)(2,1)S(1)}, u32[]{:S(2)}, u32[]{:S(2)}) async-start(bf16[32,16,1152]{2,1,0:T(8,128)(2,1)} %spatial_1.1), calls=%async_computation | async-start | bytes 2359296 | tf_op jit(solution)/shard_map/all_to_all | solution.py:402
  55.0 5.6 %copy-start.8 = (bf16[120,1152]{1,0:T(8,128)(2,1)S(1)}, bf16[120,1152]{1,0:T(8,128)(2,1)}, u32[]{:S(2)}) copy-start(bf16[120,1152]{1,0:T(8,128)(2,1)} %param.19) | copy-start | bytes 829444
  55.7 15.9 %collective-permute-start.10 = (bf16[144,1152]{1,0:T(8,128)(2,1)}, bf16[144,1152]{1,0:T(8,128)(2,1)S(1)}, u32[]{:S(2)}, u32[]{:S(2)}) collective-permute-start(bf16[144,1152]{1,0:T(8,128)(2,1)} %slice_bitcast_fusion), channel_id=1, source_target_pairs={{0,48},{16,0},{32,16},{48,32},{1,49},{17,1},{33,17},{49,33},{2,50}... | collective-permute-start | bytes 995336 | tf_op jit(solution)/shard_map/ppermute | solution.py:353
  59.9 17.8 %collective-permute-start.9 = (bf16[144,1152]{1,0:T(8,128)(2,1)}, bf16[144,1152]{1,0:T(8,128)(2,1)}, u32[]{:S(2)}, u32[]{:S(2)}) collective-permute-start(bf16[144,1152]{1,0:T(8,128)(2,1)} %slice_bitcast_fusion.1), channel_id=1, source_target_pairs={{0,16},{16,32},{32,48},{48,0},{1,17},{17,33},{33,49},{49,1},{2,18}... | collective-permute-start | bytes 995336 | tf_op jit(solution)/shard_map/ppermute | solution.py:353
  61.7 38.8 %collective-permute-start.11 = (bf16[2,144,1152]{2,1,0:T(8,128)(2,1)S(1)}, bf16[2,144,1152]{2,1,0:T(8,128)(2,1)}, u32[]{:S(2)}, u32[]{:S(2)}) collective-permute-start(bf16[2,144,1152]{2,1,0:T(8,128)(2,1)S(1)} %copy.17.refs_0_), channel_id=1, source_target_pairs={{0,1},{1,0},{2,3},{3,2},{4,5},{5,4},{6,7},{7,6},{8,9},{9,8},{10,11... | collective-permute-start | bytes 1990664 | tf_op jit(solution)/shard_map/ppermute | solution.py:353
  67.3 33.1 %collective-permute-start.13 = (bf16[2,144,1152]{2,1,0:T(8,128)(2,1)S(1)}, bf16[2,144,1152]{2,1,0:T(8,128)(2,1)}, u32[]{:S(2)}, u32[]{:S(2)}) collective-permute-start(bf16[2,144,1152]{2,1,0:T(8,128)(2,1)S(1)} %collective-permute-done.8.refs_2_), channel_id=1, source_target_pairs={{0,1},{1,0},{2,3},{3,2},{4,5},{5,4},{6,7},{7,6},{8,9},{9,8},{10,11... | collective-permute-start | bytes 1990664 | tf_op jit(solution)/shard_map/ppermute | solution.py:353
  67.4 33.0 %collective-permute-start.12 = (bf16[2,144,1152]{2,1,0:T(8,128)(2,1)}, bf16[2,144,1152]{2,1,0:T(8,128)(2,1)}, u32[]{:S(2)}, u32[]{:S(2)}) collective-permute-start(bf16[2,144,1152]{2,1,0:T(8,128)(2,1)} %collective-permute-done.7.refs_1_), channel_id=1, source_target_pairs={{0,1},{1,0},{2,3},{3,2},{4,5},{5,4},{6,7},{7,6},{8,9},{9,8},{10,11... | collective-permute-start | bytes 1990664 | tf_op jit(solution)/shard_map/ppermute | solution.py:353
  71.6 28.8 %collective-permute-start.15 = (bf16[144,1152]{1,0:T(8,128)(2,1)S(1)}, bf16[144,1152]{1,0:T(8,128)(2,1)}, u32[]{:S(2)}, u32[]{:S(2)}) collective-permute-start(bf16[144,1152]{1,0:T(8,128)(2,1)S(1)} %collective-permute-done.10.refs_4_), channel_id=1, source_target_pairs={{0,1},{1,0},{2,3},{3,2},{4,5},{5,4},{6,7},{7,6},{8,9},{9,8},{10,11... | collective-permute-start | bytes 995336 | tf_op jit(solution)/shard_map/ppermute | solution.py:353
  77.7 22.8 %collective-permute-start.14 = (bf16[144,1152]{1,0:T(8,128)(2,1)}, bf16[144,1152]{1,0:T(8,128)(2,1)}, u32[]{:S(2)}, u32[]{:S(2)}) collective-permute-start(bf16[144,1152]{1,0:T(8,128)(2,1)} %collective-permute-done.9.refs_3_), channel_id=1, source_target_pairs={{0,1},{1,0},{2,3},{3,2},{4,5},{5,4},{6,7},{7,6},{8,9},{9,8},{10,11... | collective-permute-start | bytes 995336 | tf_op jit(solution)/shard_map/ppermute | solution.py:353
  79.0 1.8 %copy-start.2 = (bf16[1152,1152]{1,0:T(8,128)(2,1)S(1)}, bf16[1152,1152]{1,0:T(8,128)(2,1)}, u32[]{:S(2)}) copy-start(bf16[1152,1152]{1,0:T(8,128)(2,1)} %wo_hbm.1) | copy-start | bytes 7962628
  99.4 1.0 copy-start.7

commit v3 on v1

v3 whole, which is shorter than its diff:
```python
import jax
import jax.numpy as jnp
import numpy as np
from jax import lax
from jax.experimental import pallas as pl
from jax.experimental.pallas import tpu as pltpu
from jax.sharding import Mesh, PartitionSpec as P

H = 16
HEAD = 72
LANES = 9
D = 1152
S = 256
T = 512
WIN = 256
SLOTS = 128
BLOCK = 144
CUT = 80
CHUNK = 512
EXP_SCALE = float(np.log2(np.e) / np.sqrt(72.0))
F32 = jnp.float32
BF16 = jnp.bfloat16
NT = (((1,), (1,)), ((), ()))
SEQ = ("z_lo", "x", "y")
ALL = ("z_hi", "core", "z_lo", "x", "y")


def mm(a, b):
    return jnp.dot(a, b, preferred_element_type=F32)


def mm_nt(a, b):
    return lax.dot_general(a, b, NT, preferred_element_type=F32)


def window(head):
    return min(HEAD * head // 128 * 128, D - WIN)


def lane_mask(head, at, size):
    lane = lax.broadcasted_iota(jnp.int32, (1, size), 1) + at
    inside = (lane >= HEAD * head) & (lane < HEAD * head + HEAD)
    return jnp.where(inside, 1.0, 0.0).astype(BF16)


def heads_of(at, size):
    return [h for h in range(H) if h * HEAD < at + size and h * HEAD + HEAD > at]


def identity(n):
    rows = lax.broadcasted_iota(jnp.int32, (n, n), 0)
    cols = lax.broadcasted_iota(jnp.int32, (n, n), 1)
    return jnp.where(rows == cols, 1.0, 0.0).astype(BF16)


def norm_mod(values, shift, scale):
    mean = jnp.mean(values, axis=-1, keepdims=True)
    centered = values - mean
    var = jnp.mean(centered * centered, axis=-1, keepdims=True)
    return (centered * lax.rsqrt(var + 1e-06) * (1.0 + scale) + shift).astype(BF16)


def column_chunks(width, chunk):
    return [(at, min(chunk, width - at)) for at in range(0, width, chunk)]


def halves(body):
    def step(g, carry):
        body(g, pl.ds(pl.multiple_of(g * S, S), S))
        return carry

    lax.fori_loop(0, 2, step, 0)


def project_qkv(xn, w, qkv):
    for at, size in column_chunks(3 * D, CHUNK):
        for rows in (slice(0, S), slice(S, T)):
            qkv[rows, at : at + size] = mm(xn[rows, :], w[:, at : at + size]).astype(BF16)


def softmax_rows(scores):
    top = jnp.max(scores, axis=1, keepdims=True)
    expo = jnp.exp2(scores * EXP_SCALE - top * EXP_SCALE)
    return (expo * (1.0 / jnp.sum(expo, axis=1, keepdims=True))).astype(BF16)


def softmax_cols(scores):
    top = jnp.max(scores, axis=0, keepdims=True)
    expo = jnp.exp2(scores * EXP_SCALE - top * EXP_SCALE)
    return expo, 1.0 / jnp.sum(expo, axis=0, keepdims=True)


def softmax_blocks(scores):
    low = lax.broadcasted_iota(jnp.int32, (64, 128), 1) < 64
    left, over_left = softmax_cols(jnp.where(low, scores[0:64, :128], scores[64:128, :128]))
    right, over_right = softmax_cols(jnp.where(low, scores[128:192, 128:], scores[192:256, 128:]))
    zero = jnp.zeros((64, 128), F32)
    wide = jnp.concatenate(
        [
            jnp.concatenate([jnp.where(low, left, zero), zero], 1),
            jnp.concatenate([jnp.where(low, zero, left), zero], 1),
            jnp.concatenate([zero, jnp.where(low, right, zero)], 1),
            jnp.concatenate([zero, jnp.where(low, zero, right)], 1),
        ],
        0,
    )
    return wide.astype(BF16), jnp.concatenate([over_left, over_right], 1)


def spatial_kernel(lat, mod, w, wo, out, xn, qkv, weights, ctx):
    shift, scale, gate = mod[0:1, :], mod[1:2, :], mod[2:3, :]

    def norm_rows(i, carry):
        rows = pl.ds(pl.multiple_of(i * 64, 64), 64)
        xn[rows, :] = norm_mod(lat[rows, :].astype(F32), shift, scale)
        return carry

    lax.fori_loop(0, T // 64, norm_rows, 0, unroll=2)
    project_qkv(xn, w, qkv)

    def attend(g, rows):
        for head in range(H):
            at = window(head)
            query = qkv[rows, at : at + WIN] * lane_mask(head, at, WIN)
            weights[head] = softmax_rows(mm_nt(query, qkv[rows, D + at : D + at + WIN]))
        for at, size in column_chunks(D, WIN):
            values = qkv[rows, 2 * D + at : 2 * D + at + size]
            mixed = 0
            for head in heads_of(at, size):
                mixed = mixed + mm(weights[head], values * lane_mask(head, at, size))
            ctx[rows, at : at + size] = mixed.astype(BF16)

    halves(attend)
    for at, size in column_chunks(D, WIN):
        cols = slice(at, at + size)
        parts = []
        for rows in (slice(0, S), slice(S, T)):
            value = lat[rows, cols].astype(F32) + gate[:, cols] * mm(ctx[rows, :], wo[:, cols])
            parts.append(value.reshape(32, 8, size))
        out[:, :, cols] = jnp.concatenate(parts, axis=1).astype(BF16)


def temporal_kernel(x, mod, w, wo, out, xn, qkv, weights, ctx, rest, over, v_t, ctx_t, wide):
    shift, scale, gate = mod[3:4, :], mod[4:5, :], mod[5:6, :]

    def widen(i, carry):
        value = x[i].astype(F32)
        for j in range(LANES):
            wide[j, pl.ds(pl.multiple_of(i * 16, 16), 16), :] = value[:, j * 128 : j * 128 + 128]
        return carry

    lax.fori_loop(0, 32, widen, 0, unroll=4)

    def norm_rows(p, carry):
        picked = pl.ds(p, 64, stride=8)
        values = jnp.concatenate([wide[j, picked, :] for j in range(LANES)], axis=1)
        rows = pl.ds(pl.multiple_of(p * 64, 64), 64)
        rest[rows, :] = values.astype(BF16)
        xn[rows, :] = norm_mod(values, shift, scale)
        return carry

    lax.fori_loop(0, 8, norm_rows, 0, unroll=2)
    project_qkv(xn, w, qkv)
    eye = identity(WIN)

    def attend(g, rows):
        for at, size in column_chunks(D, WIN):
            v_t[at : at + size, :] = mm_nt(eye[:size, :size], qkv[rows, 2 * D + at : 2 * D + at + size])
        for head in range(H):
            at = window(head)
            query = qkv[rows, at : at + WIN] * lane_mask(head, at, WIN)
            weights[head], over[head] = softmax_blocks(mm_nt(qkv[rows, D + at : D + at + WIN], query))
        for head in range(H):
            mine = slice(head * HEAD, head * HEAD + HEAD)
            ctx_t[mine, :] = mm(v_t[mine, :].astype(BF16), weights[head]) * over[head]
        ctx[rows, :] = mm_nt(eye, ctx_t[...].astype(BF16)).astype(BF16)

    halves(attend)
    for at, size in column_chunks(D, WIN):
        cols = slice(at, at + size)
        for g in range(2):
            rows = slice(g * S, g * S + S)
            value = rest[rows, cols].astype(F32) + gate[:, cols] * mm(ctx[rows, :], wo[:, cols])
            for p in range(4):
                for j in range(size // 128):
                    piece = value[p * 64 : p * 64 + 64, j * 128 : j * 128 + 128]
                    wide[at // 128 + j, pl.ds(g * 4 + p, 64, stride=8), :] = piece

    def narrow(i, carry):
        rows = pl.ds(pl.multiple_of(i * 16, 16), 16)
        out[i] = jnp.concatenate([wide[j, rows, :] for j in range(LANES)], axis=1).astype(BF16)
        return carry

    lax.fori_loop(0, 32, narrow, 0, unroll=4)


def cross_kernel(place, x, keys, values, *refs):
    pieces, (out, w, query, weights, over, v_t, ctx_t, ctx, sems) = refs[:10], refs[10:]
    length, core, z_lo, x_at = place[0], place[1], place[2], place[3]

    def put(which, src, z, x_from, skip, size):
        row = pl.multiple_of(z * (D // 2) + x_from * BLOCK + skip, 16)
        pltpu.make_async_copy(src, w.at[which, pl.ds(row, size), :], sems.at[which]).start()

    left, right, far = (x_at + 3) % 4, (x_at + 1) % 4, (x_at + 2) % 4
    for own in range(2):
        which = core if own == 0 else 1 - core
        here, from_left, from_right, far_first, far_last = pieces[5 * own : 5 * own + 5]
        for n, z in enumerate((z_lo, 1 - z_lo)):
            put(which, here.at[n], z, x_at, 0, BLOCK)
            put(which, from_left.at[n], z, left, 0, BLOCK)
            put(which, from_right.at[n], z, right, 0, BLOCK)
            put(which, far_first.at[n], z, far, 0, CUT)
            put(which, far_last.at[n], z, far, CUT, BLOCK - CUT)

    def whole(which):
        pltpu.make_async_copy(w.at[which], w.at[which], sems.at[which]).wait()

    eye = identity(WIN)
    for at, size in column_chunks(D, WIN):
        v_t[at : at + size, :] = mm_nt(eye[:size, :size], values[:, at : at + size])
    whole(0)
    for at, size in column_chunks(D, CHUNK):
        for g in range(2):
            rows = x[g * 16 : g * 16 + 16].reshape(S, D)
            query[g * S : g * S + S, at : at + size] = mm(rows, w[0, :, at : at + size]).astype(BF16)
    valid = lax.broadcasted_iota(jnp.int32, (SLOTS, T), 0) < length
    for head in range(H):
        at = window(head)
        masked = keys[:, at : at + WIN] * lane_mask(head, at, WIN)
        scores = mm_nt(masked, query[:, at : at + WIN])
        expo, over[head] = softmax_cols(jnp.where(valid, scores, -1e30))
        weights[head] = expo.astype(BF16)
    for head in range(H):
        mine = slice(head * HEAD, head * HEAD + HEAD)
        ctx_t[mine, :] = mm(v_t[mine, :].astype(BF16), weights[head]) * over[head]
    for g in range(2):
        rows = slice(g * S, g * S + S)
        ctx[rows, :] = mm_nt(eye, ctx_t[:, rows].astype(BF16)).astype(BF16)
    whole(1)
    for at, size in column_chunks(D, WIN):
        cols = slice(at, at + size)
        for g in range(2):
            value = x[g * 16 : g * 16 + 16, :, cols].astype(F32).reshape(S, size)
            value = value + mm(ctx[g * S : g * S + S, :], w[1, :, cols])
            value = value.reshape(16, 2, 8, size)
            for f in range(2):
                out[f, g * 128 : g * 128 + 128, cols] = value[:, f].reshape(128, size).astype(BF16)


def vmem(*shape):
    return pltpu.VMEM(shape, BF16)


def call(kernel, name, shape, scratch, flops, transcendentals, *args, smem=0, anywhere=0):
    spaces = [pltpu.SMEM] * smem + [pltpu.VMEM] * (len(args) - smem - anywhere) + [pl.ANY] * anywhere
    return pl.pallas_call(
        kernel,
        out_shape=jax.ShapeDtypeStruct(shape, BF16),
        in_specs=[pl.BlockSpec(memory_space=space) for space in spaces],
        out_specs=pl.BlockSpec(memory_space=pltpu.VMEM),
        scratch_shapes=scratch,
        compiler_params=pltpu.CompilerParams(vmem_limit_bytes=22 * 1024 * 1024),
        cost_estimate=pl.CostEstimate(
            flops=flops, bytes_accessed=13_000_000, transcendentals=transcendentals
        ),
        name=name,
    )(*args)


def spatial(*args):
    scratch = [vmem(T, D), vmem(T, 3 * D), vmem(H, S, S), vmem(T, D)]
    return call(spatial_kernel, "spatial", (32, 16, D), scratch, 8_000_000_000, 2_100_000, *args)


def temporal(*args):
    scratch = [
        vmem(T, D),
        vmem(T, 3 * D),
        vmem(H, S, S),
        vmem(T, D),
        vmem(T, D),
        pltpu.VMEM((H, 1, S), F32),
        pltpu.VMEM((D, S), F32),
        pltpu.VMEM((D, S), F32),
        pltpu.VMEM((LANES, T, 128), F32),
    ]
    return call(temporal_kernel, "temporal", (32, 16, D), scratch, 8_000_000_000, 600_000, *args)


def cross(place, x, keys, values, pieces):
    scratch = [
        vmem(2, D, D),
        vmem(T, D),
        vmem(H, SLOTS, T),
        pltpu.VMEM((H, 1, T), F32),
        pltpu.VMEM((D, SLOTS), F32),
        pltpu.VMEM((D, T), F32),
        vmem(T, D),
        pltpu.SemaphoreType.DMA((2,)),
    ]
    args = (place, x, keys, values, *pieces)
    return call(
        cross_kernel, "cross", (2, S, D), scratch, 4_000_000_000, 1_000_000, *args, smem=1, anywhere=10
    )


def shift(array, axis, by, size):
    return lax.ppermute(array, axis, [(i, (i + by) % size) for i in range(size)])


def gather_y(cross_query, cross_out):
    mine = jnp.where(lax.axis_index("core") == 0, cross_query, cross_out)
    return [shift(mine, "y", by, 4) for by in (3, 2, 1)] + [mine]


def in_order(rows):
    found = jnp.stack(rows + rows[:3])
    ordered = lax.dynamic_slice_in_dim(found, 3 - lax.axis_index("y"), 4, axis=0)
    return ordered.reshape(BLOCK, D)


def over_core(piece):
    return shift(piece, "core", 1, 2)


def body(
    latent,
    modulation,
    w_spatial_qkv,
    w_spatial_out,
    w_temporal_qkv,
    w_temporal_out,
    cross_query,
    cross_out,
    text_keys,
    text_values,
    text_len,
):
    rows = gather_y(cross_query, cross_out)
    after_spatial = spatial(latent.reshape(T, D), modulation, w_spatial_qkv, w_spatial_out)
    rows, after_spatial = lax.optimization_barrier((rows, after_spatial))
    placed = lax.all_to_all(after_spatial, SEQ, split_axis=0, concat_axis=0, tiled=True)
    block = in_order(rows)
    here = jnp.stack([block, shift(block, "z_lo", 1, 2)])
    left = shift(here, "x", 1, 4)
    right = shift(here, "x", -1, 4)
    after_temporal = temporal(placed, modulation, w_temporal_qkv, w_temporal_out)
    returned = lax.all_to_all(after_temporal, SEQ, split_axis=0, concat_axis=0, tiled=True)
    far_first = shift(left[:, :CUT], "x", 1, 4)
    far_last = shift(right[:, CUT:], "x", -1, 4)
    pieces = [here, left, right, far_first, far_last]
    pieces = pieces + [over_core(piece) for piece in pieces]
    place = jnp.stack(
        [text_len[0], lax.axis_index("core"), lax.axis_index("z_lo"), lax.axis_index("x")]
    ).astype(jnp.int32)
    fill = ((0, SLOTS - text_keys.shape[0]), (0, 0))
    keys, values = jnp.pad(text_keys, fill), jnp.pad(text_values, fill)
    return cross(place, returned, keys, values, pieces)


def solution(mesh):
    fine = Mesh(mesh.devices.reshape(2, 4, 4, 2, 2), ("z_lo", "x", "y", "z_hi", "core"))
    part = ("z_hi", "core")
    placed = (
        P(ALL, None, None),
        P(part, None),
        P(),
        P(),
        P(),
        P(),
        P(SEQ, None),
        P(SEQ, None),
        P(part, None),
        P(part, None),
        P(part),
    )
    return jax.shard_map(
        body, mesh=fine, in_specs=placed, out_specs=P(ALL, None, None), check_vma=False
    )
```

time: 221 us -> 119 us (0.54)
  matrix products: 52.1 us -> 0 us
  local copies, waits for them, and re-layouts: 52.6 us -> 14.4 us
  Pallas kernels: 0 us -> 35.1 us
  other arithmetic: 26.8 us -> 1.05 us
  blocking collectives: 23.6 us -> 0 us
  starting transfers between devices: 18.4 us -> 30.1 us
  waiting for transfers between devices: 45 us -> 36.5 us
    dot_general x11 -> x0, matrix products: 47.2 us -> none  [the longest x6 34.2 us: project(): jnp.dot(flat, weight, preferred_element_type=jnp.float32)]
    all_to_all x2, waiting for transfers between devices: 45 us -> 0.01 us  [the longest x1 0.01 us: body(): lax.all_to_all(after_spatial, SEQ, split_axis=0, concat_axis=0, tiled=True)]
    ppermute x1 -> x13, waiting for transfers between devices: 0.01 us -> 36.5 us  [shift(): lax.ppermute(array, axis, [(i, (i + by) % size) for i in range(size)])]
    pallas_call x0 -> x3, Pallas kernels: none -> 35.1 us  [call(): pl.pallas_call(kernel, out_shape=jax.ShapeDtypeStruct(shape, BF16), in_sp...]
    all_to_all x1 -> x0, blocking collectives: 23.6 us -> none  [body(): return lax.all_to_all(result, SEQ, split_axis=0, concat_axis=1, tiled=True)]
    reshape x3 -> x1, local copies, waits for them, and re-layouts: 21 us -> 0.07 us  [in_order(): return ordered.reshape(BLOCK, D)]
    convert_element_type x6 -> x0, local copies, waits for them, and re-layouts: 19.1 us -> none  [the longest x2 7.3 us: across_frames(): return mixed.reshape(frames, places, width).astype(jnp.bfloat16)]
    sub x2 -> x0, other arithmetic: 12.4 us -> none  [softmax_weights(): expo = jnp.exp(scores - top)]
  transfers between devices with their start and end apart: 3 -> 15, of which waited for: 2 -> 3; matrix products, arithmetic and copies ran while one was open for 27% -> 2% of each run, Pallas kernels for 0% -> 21%
where the time goes in v3:
time: 119 us; the launch traced here: 118 us
  waiting for transfers between devices  36.5 us (31%)
  Pallas kernels  35.1 us (29%)
  starting transfers between devices  30.1 us (25%)
  local copies, waits for them, and re-layouts  14.4 us (12%)
    ppermute x13, waiting for transfers between devices, shift(): lax.ppermute(array, axis, [(i, (i + by) % size) for i in range(size)])  36.5 us
    pallas_call x3, Pallas kernels, call(): pl.pallas_call(kernel, out_shape=jax.ShapeDtypeStruct(shape, BF16), in_sp...  35.1 us
    ppermute x13, starting transfers between devices, shift(): lax.ppermute(array, axis, [(i, (i + by) % size) for i in range(size)])  16.1 us
    unnamed x22, local copies, waits for them, and re-layouts  12.1 us
    all_to_all x1, starting transfers between devices, body(): lax.all_to_all(after_temporal, SEQ, split_axis=0, concat_axis=0, tiled=True)  8.17 us
    all_to_all x1, starting transfers between devices, body(): lax.all_to_all(after_spatial, SEQ, split_axis=0, concat_axis=0, tiled=True)  5.89 us
  transfers between devices with their start and end apart: 15, of which 3 were waited for; matrix products, arithmetic and copies ran while one was open for 2% of the time, Pallas kernels for 21%

profile of v3, /device:TPU:1, one launch (start us, length us, event | category | flops | bytes accessed | tf_op | source)
XLA Modules:
  0.0 118.2 jit_solution(1874664004625235454)
XLA Ops:
  0.0 0.9 broadcast_select_fusion
  0.9 2.2 %collective-permute-start.2 = (bf16[36,1152]{1,0:T(8,128)(2,1)S(1)}, bf16[36,1152]{1,0:T(8,128)(2,1)S(1)}, u32[]{:S(2)}, u32[]{:S(2)}) collective-permute-start(bf16[36,1152]{1,0:T(8,128)(2,1)S(1)} %broadcast_select_fusion), channel_id=1, source_target_pairs={{0,4},{4,8},{8,12},{12,0},{1,5},{5,9},{9,13},{13,1},{2,6},{6,10},{... | collective-permute-start | bytes 248840 | tf_op jit(solution)/shard_map/ppermute | solution.py:309
  3.1 2.6 %collective-permute-start.1 = (bf16[36,1152]{1,0:T(8,128)(2,1)S(1)}, bf16[36,1152]{1,0:T(8,128)(2,1)S(1)}, u32[]{:S(2)}, u32[]{:S(2)}) collective-permute-start(bf16[36,1152]{1,0:T(8,128)(2,1)S(1)} %broadcast_select_fusion), channel_id=1, source_target_pairs={{0,8},{4,12},{8,0},{12,4},{1,9},{5,13},{9,1},{13,5},{2,10},{6,14},... | collective-permute-start | bytes 248840 | tf_op jit(solution)/shard_map/ppermute | solution.py:309
  5.7 1.1 collective-permute-start
  6.8 3.3 %copy-done = bf16[1152,3456]{1,0:T(8,128)(2,1)S(1)} copy-done((bf16[1152,3456]{1,0:T(8,128)(2,1)S(1)}, bf16[1152,3456]{1,0:T(8,128)(2,1)}, u32[]{:S(2)}) %copy-start) | copy-done | bytes 7962648
  10.1 1.7 %copy-done.2 = bf16[1152,1152]{1,0:T(8,128)(2,1)S(1)} copy-done((bf16[1152,1152]{1,0:T(8,128)(2,1)S(1)}, bf16[1152,1152]{1,0:T(8,128)(2,1)}, u32[]{:S(2)}) %copy-start.2) | copy-done | bytes 2654232
  11.8 1.3 %copy-done.4 = bf16[2,256,1152]{2,1,0:T(8,128)(2,1)S(1)} copy-done((bf16[2,256,1152]{2,1,0:T(8,128)(2,1)S(1)}, bf16[2,256,1152]{2,1,0:T(8,128)(2,1)}, u32[]{:S(2)}) %copy-start.4) | copy-done | bytes 1179672
  13.1 0.8 copy-done.5
  13.8 12.7 %spatial.1 = bf16[32,16,1152]{2,1,0:T(8,128)(2,1)} custom-call(bf16[512,1152]{1,0:T(8,128)(2,1)S(1)} %bitcast.16, f32[6,1152]{1,0:T(8,128)S(1)} %copy-done.5, bf16[1152,3456]{1,0:T(8,128)(2,1)S(1)} %copy-done, bf16[1152,1152]{1,0:T(8,128)(2,1)S(1)} %copy-done.2), custom_call_target="tpu_custom_call" | custom-call | flops 8000000000 | bytes 13000000 | tf_op jit(solution)/shard_map/spatial/pallas_call | solution.py:257
  26.5 0.0 collective-permute-done.2
  26.5 0.0 collective-permute-done.1
  26.5 0.0 collective-permute-done
  26.5 5.9 %all-to-all-start = ((bf16[32,16,1152]{2,1,0:T(8,128)(2,1)}), bf16[32,16,1152]{2,1,0:T(8,128)(2,1)S(1)}, u32[]{:S(2)}, u32[]{:S(2)}) async-start(bf16[32,16,1152]{2,1,0:T(8,128)(2,1)} %spatial.1), calls=%async_computation | async-start | bytes 2359296 | tf_op jit(solution)/shard_map/all_to_all | solution.py:343
  32.6 0.1 reshape.7
  32.7 0.0 copy-start.6
  32.7 1.3 %collective-permute-start.3 = (bf16[144,1152]{1,0:T(8,128)(2,1)S(1)}, bf16[144,1152]{1,0:T(8,128)(2,1)S(1)}, u32[]{:S(2)}, u32[]{:S(2)}) collective-permute-start(bf16[144,1152]{1,0:T(8,128)(2,1)S(1)} %reshape.7), channel_id=1, source_target_pairs={{0,64},{64,0},{1,65},{65,1},{2,66},{66,2},{3,67},{67,3},{4,68},{68... | collective-permute-start | bytes 995336 | tf_op jit(solution)/shard_map/ppermute | solution.py:309
  34.0 0.1 stack_reshape.3
  34.1 18.9 %collective-permute-done.3 = bf16[144,1152]{1,0:T(8,128)(2,1)S(1)} collective-permute-done((bf16[144,1152]{1,0:T(8,128)(2,1)S(1)}, bf16[144,1152]{1,0:T(8,128)(2,1)S(1)}, u32[]{:S(2)}, u32[]{:S(2)}) %collective-permute-start.3) | collective-permute-done | bytes 331808 | tf_op jit(solution)/shard_map/ppermute | solution.py:309
  53.0 0.1 pad_maximum_fusion.refs_0_
  53.1 2.5 %collective-permute-start.5 = (bf16[2,144,1152]{2,1,0:T(8,128)(2,1)S(1)}, bf16[2,144,1152]{2,1,0:T(8,128)(2,1)}, u32[]{:S(2)}, u32[]{:S(2)}) collective-permute-start(bf16[2,144,1152]{2,1,0:T(8,128)(2,1)S(1)} %pad_maximum_fusion.refs_0_), channel_id=1, source_target_pairs={{0,48},{16,0},{32,16},{48,32},{1,49},{17,1},{33,17},{49,33},{2,50}... | collective-permute-start | bytes 1990664 | tf_op jit(solution)/shard_map/ppermute | solution.py:309
  55.6 0.0 collective-permute-start.4
  55.6 0.0 all-to-all-done.x
  55.6 0.0 copy-start.1
  55.6 3.3 %copy-done.1 = bf16[1152,3456]{1,0:T(8,128)(2,1)S(1)} copy-done((bf16[1152,3456]{1,0:T(8,128)(2,1)S(1)}, bf16[1152,3456]{1,0:T(8,128)(2,1)}, u32[]{:S(2)}) %copy-start.1) | copy-done | bytes 7962648
  58.8 1.7 %copy-done.3 = bf16[1152,1152]{1,0:T(8,128)(2,1)S(1)} copy-done((bf16[1152,1152]{1,0:T(8,128)(2,1)S(1)}, bf16[1152,1152]{1,0:T(8,128)(2,1)}, u32[]{:S(2)}) %copy-start.3) | copy-done | bytes 2654232
  60.6 12.5 %temporal.1 = bf16[32,16,1152]{2,1,0:T(8,128)(2,1)} custom-call(bf16[32,16,1152]{2,1,0:T(8,128)(2,1)S(1)} %all-to-all-done.x, f32[6,1152]{1,0:T(8,128)S(1)} %copy-done.6, bf16[1152,3456]{1,0:T(8,128)(2,1)S(1)} %copy-done.1, bf16[1152,1152]{1,0:T(8,128)(2,1)S(1)} %copy-done.3), custom_call_target="tpu_custom_call" | custom-call | flops 8000000000 | bytes 13000000 | tf_op jit(solution)/shard_map/temporal/pallas_call | solution.py:257
  73.1 8.2 %all-to-all-start.1 = ((bf16[32,16,1152]{2,1,0:T(8,128)(2,1)}), bf16[32,16,1152]{2,1,0:T(8,128)(2,1)S(1)}, u32[]{:S(2)}, u32[]{:S(2)}) async-start(bf16[32,16,1152]{2,1,0:T(8,128)(2,1)} %temporal.1), calls=%async_computation.1 | async-start | bytes 2359296 | tf_op jit(solution)/shard_map/all_to_all | solution.py:349
  81.2 0.0 copy-start.7
  81.3 0.0 collective-permute-done.4.refs_1_
  81.3 1.3 %collective-permute-start.6 = (bf16[2,80,1152]{2,1,0:T(8,128)(2,1)S(1)}, bf16[2,80,1152]{2,1,0:T(8,128)(2,1)S(1)}, u32[]{:S(2)}, u32[]{:S(2)}) collective-permute-start(bf16[2,80,1152]{2,1,0:T(8,128)(2,1)S(1)} %slice.8), channel_id=1, source_target_pairs={{0,16},{16,32},{32,48},{48,0},{1,17},{17,33},{33,49},{49,1},{2,18}... | collective-permute-start | bytes 1105928 | tf_op jit(solution)/shard_map/ppermute | solution.py:309
  82.6 2.2 %collective-permute-start.8 = (bf16[2,144,1152]{2,1,0:T(8,128)(2,1)S(1)}, bf16[2,144,1152]{2,1,0:T(8,128)(2,1)}, u32[]{:S(2)}, u32[]{:S(2)}) collective-permute-start(bf16[2,144,1152]{2,1,0:T(8,128)(2,1)S(1)} %pad_maximum_fusion.refs_0_), channel_id=1, source_target_pairs={{0,1},{1,0},{2,3},{3,2},{4,5},{5,4},{6,7},{7,6},{8,9},{9,8},{10,11... | collective-permute-start | bytes 1990664 | tf_op jit(solution)/shard_map/ppermute | solution.py:309
  84.8 0.0 collective-permute-done.5.refs_2_
  84.8 0.0 collective-permute-start.10
  84.8 0.5 collective-permute-start.9
  85.3 1.0 slice.9
  86.3 1.2 %collective-permute-start.7 = (bf16[2,64,1152]{2,1,0:T(8,128)(2,1)S(1)}, bf16[2,64,1152]{2,1,0:T(8,128)(2,1)}, u32[]{:S(2)}, u32[]{:S(2)}) collective-permute-start(bf16[2,64,1152]{2,1,0:T(8,128)(2,1)S(1)} %slice.9), channel_id=1, source_target_pairs={{0,48},{16,0},{32,16},{48,32},{1,49},{17,1},{33,17},{49,33},{2,50}... | collective-permute-start | bytes 884744 | tf_op jit(solution)/shard_map/ppermute | solution.py:309
  87.5 17.3 %collective-permute-done.6.refs_3_ = bf16[2,80,1152]{2,1,0:T(8,128)(2,1)S(1)} collective-permute-done((bf16[2,80,1152]{2,1,0:T(8,128)(2,1)S(1)}, bf16[2,80,1152]{2,1,0:T(8,128)(2,1)S(1)}, u32[]{:S(2)}, u32[]{:S(2)}) %collective-permute-start.6) | collective-permute-done | bytes 368672 | tf_op jit(solution)/shard_map/ppermute | solution.py:309
  104.8 1.1 collective-permute-start.11
  106.0 0.0 collective-permute-done.7.refs_4_
  106.0 0.0 collective-permute-start.12
  106.7 1.0 pad.8.values
  107.7 0.1 pad_add_fusion.place
  107.7 0.0 collective-permute-done.8.refs_5_
  107.7 0.3 collective-permute-done.12.refs_9_
  108.0 0.0 collective-permute-done.10.refs_7_
  108.0 0.0 collective-permute-done.9.refs_6_
  108.0 0.0 all-to-all-done.1.x
  108.0 10.0 %cross.1 = bf16[2,256,1152]{2,1,0:T(8,128)(2,1)} custom-call(s32[4]{0:T(128)S(1)} %pad_add_fusion.place, bf16[32,16,1152]{2,1,0:T(8,128)(2,1)S(1)} %all-to-all-done.1.x, bf16[128,1152]{1,0:T(8,128)(2,1)S(1)} %pad.7.keys, bf16[128,1152]{1,0:T(8,128)(2,1)S(1)} %pad.8.values, bf16[2,144,1152]{2,1,0:T(8,128)(2,1)S(1)} %pad_maximum_fusion.refs_0_, ...), custom_call_target="tpu_custom_call" | custom-call | flops 4000000000 | bytes 13000000 | tf_op jit(solution)/shard_map/cross/pallas_call | solution.py:257
  (18 shorter events, 0.2 us)
Async XLA Ops:
  0.9 25.6 %collective-permute-start.2 = (bf16[36,1152]{1,0:T(8,128)(2,1)S(1)}, bf16[36,1152]{1,0:T(8,128)(2,1)S(1)}, u32[]{:S(2)}, u32[]{:S(2)}) collective-permute-start(bf16[36,1152]{1,0:T(8,128)(2,1)S(1)} %broadcast_select_fusion), channel_id=1, source_target_pairs={{0,4},{4,8},{8,12},{12,0},{1,5},{5,9},{9,13},{13,1},{2,6},{6,10},{... | collective-permute-start | bytes 248840 | tf_op jit(solution)/shard_map/ppermute | solution.py:309
  3.1 23.4 %collective-permute-start.1 = (bf16[36,1152]{1,0:T(8,128)(2,1)S(1)}, bf16[36,1152]{1,0:T(8,128)(2,1)S(1)}, u32[]{:S(2)}, u32[]{:S(2)}) collective-permute-start(bf16[36,1152]{1,0:T(8,128)(2,1)S(1)} %broadcast_select_fusion), channel_id=1, source_target_pairs={{0,8},{4,12},{8,0},{12,4},{1,9},{5,13},{9,1},{13,5},{2,10},{6,14},... | collective-permute-start | bytes 248840 | tf_op jit(solution)/shard_map/ppermute | solution.py:309
  5.7 20.8 %collective-permute-start = (bf16[36,1152]{1,0:T(8,128)(2,1)S(1)}, bf16[36,1152]{1,0:T(8,128)(2,1)S(1)}, u32[]{:S(2)}, u32[]{:S(2)}) collective-permute-start(bf16[36,1152]{1,0:T(8,128)(2,1)S(1)} %broadcast_select_fusion), channel_id=1, source_target_pairs={{0,12},{4,0},{8,4},{12,8},{1,13},{5,1},{9,5},{13,9},{2,14},{6,2},{... | collective-permute-start | bytes 248840 | tf_op jit(solution)/shard_map/ppermute | solution.py:309
  6.8 3.3 %copy-start = (bf16[1152,3456]{1,0:T(8,128)(2,1)S(1)}, bf16[1152,3456]{1,0:T(8,128)(2,1)}, u32[]{:S(2)}) copy-start(bf16[1152,3456]{1,0:T(8,128)(2,1)} %w.2) | copy-start | bytes 23887876
  10.1 1.7 %copy-start.2 = (bf16[1152,1152]{1,0:T(8,128)(2,1)S(1)}, bf16[1152,1152]{1,0:T(8,128)(2,1)}, u32[]{:S(2)}) copy-start(bf16[1152,1152]{1,0:T(8,128)(2,1)} %wo.2) | copy-start | bytes 7962628
  11.8 1.3 %copy-start.4 = (bf16[2,256,1152]{2,1,0:T(8,128)(2,1)S(1)}, bf16[2,256,1152]{2,1,0:T(8,128)(2,1)}, u32[]{:S(2)}) copy-start(bf16[2,256,1152]{2,1,0:T(8,128)(2,1)} %param.11) | copy-start | bytes 3538948
  13.1 0.8 copy-start.5
  26.5 29.0 %all-to-all-start = ((bf16[32,16,1152]{2,1,0:T(8,128)(2,1)}), bf16[32,16,1152]{2,1,0:T(8,128)(2,1)S(1)}, u32[]{:S(2)}, u32[]{:S(2)}) async-start(bf16[32,16,1152]{2,1,0:T(8,128)(2,1)} %spatial.1), calls=%async_computation | async-start | bytes 2359296 | tf_op jit(solution)/shard_map/all_to_all | solution.py:343
  32.7 22.9 %copy-start.6 = (f32[6,1152]{1,0:T(8,128)S(1)}, f32[6,1152]{1,0:T(8,128)}, u32[]{:S(2)}) copy-start(f32[6,1152]{1,0:T(8,128)} %mod.3) | copy-start | bytes 82948
  32.7 20.3 %collective-permute-start.3 = (bf16[144,1152]{1,0:T(8,128)(2,1)S(1)}, bf16[144,1152]{1,0:T(8,128)(2,1)S(1)}, u32[]{:S(2)}, u32[]{:S(2)}) collective-permute-start(bf16[144,1152]{1,0:T(8,128)(2,1)S(1)} %reshape.7), channel_id=1, source_target_pairs={{0,64},{64,0},{1,65},{65,1},{2,66},{66,2},{3,67},{67,3},{4,68},{68... | collective-permute-start | bytes 995336 | tf_op jit(solution)/shard_map/ppermute | solution.py:309
  53.1 31.7 %collective-permute-start.5 = (bf16[2,144,1152]{2,1,0:T(8,128)(2,1)S(1)}, bf16[2,144,1152]{2,1,0:T(8,128)(2,1)}, u32[]{:S(2)}, u32[]{:S(2)}) collective-permute-start(bf16[2,144,1152]{2,1,0:T(8,128)(2,1)S(1)} %pad_maximum_fusion.refs_0_), channel_id=1, source_target_pairs={{0,48},{16,0},{32,16},{48,32},{1,49},{17,1},{33,17},{49,33},{2,50}... | collective-permute-start | bytes 1990664 | tf_op jit(solution)/shard_map/ppermute | solution.py:309
  55.6 25.7 %collective-permute-start.4 = (bf16[2,144,1152]{2,1,0:T(8,128)(2,1)S(1)}, bf16[2,144,1152]{2,1,0:T(8,128)(2,1)S(1)}, u32[]{:S(2)}, u32[]{:S(2)}) collective-permute-start(bf16[2,144,1152]{2,1,0:T(8,128)(2,1)S(1)} %pad_maximum_fusion.refs_0_), channel_id=1, source_target_pairs={{0,16},{16,32},{32,48},{48,0},{1,17},{17,33},{33,49},{49,1},{2,18}... | collective-permute-start | bytes 1990664 | tf_op jit(solution)/shard_map/ppermute | solution.py:309
  55.6 3.3 %copy-start.1 = (bf16[1152,3456]{1,0:T(8,128)(2,1)S(1)}, bf16[1152,3456]{1,0:T(8,128)(2,1)}, u32[]{:S(2)}) copy-start(bf16[1152,3456]{1,0:T(8,128)(2,1)} %w.3) | copy-start | bytes 23887876
  58.8 1.7 %copy-start.3 = (bf16[1152,1152]{1,0:T(8,128)(2,1)S(1)}, bf16[1152,1152]{1,0:T(8,128)(2,1)}, u32[]{:S(2)}) copy-start(bf16[1152,1152]{1,0:T(8,128)(2,1)} %wo.3) | copy-start | bytes 7962628
  73.1 35.0 %all-to-all-start.1 = ((bf16[32,16,1152]{2,1,0:T(8,128)(2,1)}), bf16[32,16,1152]{2,1,0:T(8,128)(2,1)S(1)}, u32[]{:S(2)}, u32[]{:S(2)}) async-start(bf16[32,16,1152]{2,1,0:T(8,128)(2,1)} %temporal.1), calls=%async_computation.1 | async-start | bytes 2359296 | tf_op jit(solution)/shard_map/all_to_all | solution.py:349
  81.2 25.4 %copy-start.7 = (bf16[120,1152]{1,0:T(8,128)(2,1)S(1)}, bf16[120,1152]{1,0:T(8,128)(2,1)}, u32[]{:S(2)}) copy-start(bf16[120,1152]{1,0:T(8,128)(2,1)} %param.19) | copy-start | bytes 829444
  81.3 23.5 %collective-permute-start.6 = (bf16[2,80,1152]{2,1,0:T(8,128)(2,1)S(1)}, bf16[2,80,1152]{2,1,0:T(8,128)(2,1)S(1)}, u32[]{:S(2)}, u32[]{:S(2)}) collective-permute-start(bf16[2,80,1152]{2,1,0:T(8,128)(2,1)S(1)} %slice.8), channel_id=1, source_target_pairs={{0,16},{16,32},{32,48},{48,0},{1,17},{17,33},{33,49},{49,1},{2,18}... | collective-permute-start | bytes 1105928 | tf_op jit(solution)/shard_map/ppermute | solution.py:309
  82.6 25.1 %collective-permute-start.8 = (bf16[2,144,1152]{2,1,0:T(8,128)(2,1)S(1)}, bf16[2,144,1152]{2,1,0:T(8,128)(2,1)}, u32[]{:S(2)}, u32[]{:S(2)}) collective-permute-start(bf16[2,144,1152]{2,1,0:T(8,128)(2,1)S(1)} %pad_maximum_fusion.refs_0_), channel_id=1, source_target_pairs={{0,1},{1,0},{2,3},{3,2},{4,5},{5,4},{6,7},{7,6},{8,9},{9,8},{10,11... | collective-permute-start | bytes 1990664 | tf_op jit(solution)/shard_map/ppermute | solution.py:309
  84.8 23.2 %collective-permute-start.10 = (bf16[2,144,1152]{2,1,0:T(8,128)(2,1)}, bf16[2,144,1152]{2,1,0:T(8,128)(2,1)}, u32[]{:S(2)}, u32[]{:S(2)}) collective-permute-start(bf16[2,144,1152]{2,1,0:T(8,128)(2,1)} %collective-permute-done.5.refs_2_), channel_id=1, source_target_pairs={{0,1},{1,0},{2,3},{3,2},{4,5},{5,4},{6,7},{7,6},{8,9},{9,8},{10,11... | collective-permute-start | bytes 1990664 | tf_op jit(solution)/shard_map/ppermute | solution.py:309
  84.8 23.2 %collective-permute-start.9 = (bf16[2,144,1152]{2,1,0:T(8,128)(2,1)S(1)}, bf16[2,144,1152]{2,1,0:T(8,128)(2,1)}, u32[]{:S(2)}, u32[]{:S(2)}) collective-permute-start(bf16[2,144,1152]{2,1,0:T(8,128)(2,1)S(1)} %collective-permute-done.4.refs_1_), channel_id=1, source_target_pairs={{0,1},{1,0},{2,3},{3,2},{4,5},{5,4},{6,7},{7,6},{8,9},{9,8},{10,11... | collective-permute-start | bytes 1990664 | tf_op jit(solution)/shard_map/ppermute | solution.py:309
  86.3 19.7 %collective-permute-start.7 = (bf16[2,64,1152]{2,1,0:T(8,128)(2,1)S(1)}, bf16[2,64,1152]{2,1,0:T(8,128)(2,1)}, u32[]{:S(2)}, u32[]{:S(2)}) collective-permute-start(bf16[2,64,1152]{2,1,0:T(8,128)(2,1)S(1)} %slice.9), channel_id=1, source_target_pairs={{0,48},{16,0},{32,16},{48,32},{1,49},{17,1},{33,17},{49,33},{2,50}... | collective-permute-start | bytes 884744 | tf_op jit(solution)/shard_map/ppermute | solution.py:309
  104.8 3.2 %collective-permute-start.11 = (bf16[2,80,1152]{2,1,0:T(8,128)(2,1)S(1)}, bf16[2,80,1152]{2,1,0:T(8,128)(2,1)}, u32[]{:S(2)}, u32[]{:S(2)}) collective-permute-start(bf16[2,80,1152]{2,1,0:T(8,128)(2,1)S(1)} %collective-permute-done.6.refs_3_), channel_id=1, source_target_pairs={{0,1},{1,0},{2,3},{3,2},{4,5},{5,4},{6,7},{7,6},{8,9},{9,8},{10,11... | collective-permute-start | bytes 1105928 | tf_op jit(solution)/shard_map/ppermute | solution.py:309
  106.0 2.1 %collective-permute-start.12 = (bf16[2,64,1152]{2,1,0:T(8,128)(2,1)}, bf16[2,64,1152]{2,1,0:T(8,128)(2,1)}, u32[]{:S(2)}, u32[]{:S(2)}) collective-permute-start(bf16[2,64,1152]{2,1,0:T(8,128)(2,1)} %collective-permute-done.7.refs_4_), channel_id=1, source_target_pairs={{0,1},{1,0},{2,3},{3,2},{4,5},{5,4},{6,7},{7,6},{8,9},{9,8},{10,11... | collective-permute-start | bytes 884744 | tf_op jit(solution)/shard_map/ppermute | solution.py:309

commit v4 on v3

--- a/solution.py
+++ b/solution.py
@@ -15,7 +15,6 @@
 WIN = 256
 SLOTS = 128
 BLOCK = 144
-CUT = 80
 CHUNK = 512
 EXP_SCALE = float(np.log2(np.e) / np.sqrt(72.0))
 F32 = jnp.float32
@@ -72,8 +71,18 @@
     lax.fori_loop(0, 2, step, 0)
 
 
-def project_qkv(xn, w, qkv):
-    for at, size in column_chunks(3 * D, CHUNK):
+def fetch(src, dst, sems):
+    copies = []
+    for n, (at, size) in enumerate(column_chunks(src.shape[1], CHUNK)):
+        cols = pl.ds(at, size)
+        copies.append(pltpu.make_async_copy(src.at[:, cols], dst.at[:, cols], sems.at[n]))
+        copies[-1].start()
+    return copies
+
+
+def project_qkv(xn, w, copies, qkv):
+    for copy, (at, size) in zip(copies, column_chunks(3 * D, CHUNK)):
+        copy.wait()
         for rows in (slice(0, S), slice(S, T)):
             qkv[rows, at : at + size] = mm(xn[rows, :], w[:, at : at + size]).astype(BF16)
 
@@ -107,7 +116,10 @@
     return wide.astype(BF16), jnp.concatenate([over_left, over_right], 1)
 
 
-def spatial_kernel(lat, mod, w, wo, out, xn, qkv, weights, ctx):
+def spatial_kernel(lat, mod, w_hbm, wo_hbm, out, xn, qkv, weights, ctx, w, wo, sem, wsems):
+    copies = fetch(w_hbm, w, wsems)
+    last = pltpu.make_async_copy(wo_hbm, wo, sem)
+    last.start()
     shift, scale, gate = mod[0:1, :], mod[1:2, :], mod[2:3, :]
 
     def norm_rows(i, carry):
@@ -116,7 +128,7 @@
         return carry
 
     lax.fori_loop(0, T // 64, norm_rows, 0, unroll=2)
-    project_qkv(xn, w, qkv)
+    project_qkv(xn, w, copies, qkv)
 
     def attend(g, rows):
         for head in range(H):
@@ -131,6 +143,7 @@
             ctx[rows, at : at + size] = mixed.astype(BF16)
 
     halves(attend)
+    last.wait()
     for at, size in column_chunks(D, WIN):
         cols = slice(at, at + size)
         parts = []
@@ -140,7 +153,12 @@
         out[:, :, cols] = jnp.concatenate(parts, axis=1).astype(BF16)
 
 
-def temporal_kernel(x, mod, w, wo, out, xn, qkv, weights, ctx, rest, over, v_t, ctx_t, wide):
+def temporal_kernel(
+    x, mod, w_hbm, wo_hbm, out, xn, qkv, weights, ctx, rest, over, v_t, ctx_t, wide, w, wo, sem, wsems
+):
+    copies = fetch(w_hbm, w, wsems)
+    last = pltpu.make_async_copy(wo_hbm, wo, sem)
+    last.start()
     shift, scale, gate = mod[3:4, :], mod[4:5, :], mod[5:6, :]
 
     def widen(i, carry):
@@ -160,7 +178,7 @@
         return carry
 
     lax.fori_loop(0, 8, norm_rows, 0, unroll=2)
-    project_qkv(xn, w, qkv)
+    project_qkv(xn, w, copies, qkv)
     eye = identity(WIN)
 
     def attend(g, rows):
@@ -176,6 +194,7 @@
         ctx[rows, :] = mm_nt(eye, ctx_t[...].astype(BF16)).astype(BF16)
 
     halves(attend)
+    last.wait()
     for at, size in column_chunks(D, WIN):
         cols = slice(at, at + size)
         for g in range(2):
@@ -198,20 +217,20 @@
     pieces, (out, w, query, weights, over, v_t, ctx_t, ctx, sems) = refs[:10], refs[10:]
     length, core, z_lo, x_at = place[0], place[1], place[2], place[3]
 
-    def put(which, src, z, x_from, skip, size):
-        row = pl.multiple_of(z * (D // 2) + x_from * BLOCK + skip, 16)
-        pltpu.make_async_copy(src, w.at[which, pl.ds(row, size), :], sems.at[which]).start()
+    def put(which, src, z, x_from):
+        row = pl.multiple_of(z * (D // 2) + x_from * BLOCK, 16)
+        pltpu.make_async_copy(src, w.at[which, pl.ds(row, BLOCK), :], sems.at[which]).start()
 
     left, right, far = (x_at + 3) % 4, (x_at + 1) % 4, (x_at + 2) % 4
     for own in range(2):
         which = core if own == 0 else 1 - core
-        here, from_left, from_right, far_first, far_last = pieces[5 * own : 5 * own + 5]
+        here, from_left, from_right, far_same, far_other = pieces[5 * own : 5 * own + 5]
         for n, z in enumerate((z_lo, 1 - z_lo)):
-            put(which, here.at[n], z, x_at, 0, BLOCK)
-            put(which, from_left.at[n], z, left, 0, BLOCK)
-            put(which, from_right.at[n], z, right, 0, BLOCK)
-            put(which, far_first.at[n], z, far, 0, CUT)
-            put(which, far_last.at[n], z, far, CUT, BLOCK - CUT)
+            put(which, here.at[n], z, x_at)
+            put(which, from_left.at[n], z, left)
+            put(which, from_right.at[n], z, right)
+        put(which, far_same, z_lo, far)
+        put(which, far_other, 1 - z_lo, far)
 
     def whole(which):
         pltpu.make_async_copy(w.at[which], w.at[which], sems.at[which]).wait()
@@ -252,15 +271,28 @@
     return pltpu.VMEM(shape, BF16)
 
 
-def call(kernel, name, shape, scratch, flops, transcendentals, *args, smem=0, anywhere=0):
-    spaces = [pltpu.SMEM] * smem + [pltpu.VMEM] * (len(args) - smem - anywhere) + [pl.ANY] * anywhere
+def weight_scratch():
+    n = len(column_chunks(3 * D, CHUNK))
+    return [
+        vmem(D, 3 * D),
+        vmem(D, D),
+        pltpu.SemaphoreType.DMA,
+        pltpu.SemaphoreType.DMA((n,)),
+    ]
+
+
+def call(kernel, name, shape, scratch, flops, transcendentals, spaces, *args):
+    args = [
+        pltpu.with_memory_space_constraint(arg, space) if space == pltpu.HBM else arg
+        for arg, space in zip(args, spaces)
+    ]
     return pl.pallas_call(
         kernel,
         out_shape=jax.ShapeDtypeStruct(shape, BF16),
-        in_specs=[pl.BlockSpec(memory_space=space) for space in spaces],
+        in_specs=[pl.BlockSpec(memory_space=pl.ANY if space == pltpu.HBM else space) for space in spaces],
         out_specs=pl.BlockSpec(memory_space=pltpu.VMEM),
         scratch_shapes=scratch,
-        compiler_params=pltpu.CompilerParams(vmem_limit_bytes=22 * 1024 * 1024),
+        compiler_params=pltpu.CompilerParams(vmem_limit_bytes=34 * 1024 * 1024),
         cost_estimate=pl.CostEstimate(
             flops=flops, bytes_accessed=13_000_000, transcendentals=transcendentals
         ),
@@ -270,7 +302,9 @@
 
 def spatial(*args):
     scratch = [vmem(T, D), vmem(T, 3 * D), vmem(H, S, S), vmem(T, D)]
-    return call(spatial_kernel, "spatial", (32, 16, D), scratch, 8_000_000_000, 2_100_000, *args)
+    scratch = scratch + weight_scratch()
+    spaces = [pltpu.VMEM, pltpu.VMEM, pltpu.HBM, pltpu.HBM]
+    return call(spatial_kernel, "spatial", (32, 16, D), scratch, 8_000_000_000, 2_100_000, spaces, *args)
 
 
 def temporal(*args):
@@ -285,7 +319,9 @@
         pltpu.VMEM((D, S), F32),
         pltpu.VMEM((LANES, T, 128), F32),
     ]
-    return call(temporal_kernel, "temporal", (32, 16, D), scratch, 8_000_000_000, 600_000, *args)
+    scratch = scratch + weight_scratch()
+    spaces = [pltpu.VMEM, pltpu.VMEM, pltpu.HBM, pltpu.HBM]
+    return call(temporal_kernel, "temporal", (32, 16, D), scratch, 8_000_000_000, 600_000, spaces, *args)
 
 
 def cross(place, x, keys, values, pieces):
@@ -300,18 +336,16 @@
         pltpu.SemaphoreType.DMA((2,)),
     ]
     args = (place, x, keys, values, *pieces)
-    return call(
-        cross_kernel, "cross", (2, S, D), scratch, 4_000_000_000, 1_000_000, *args, smem=1, anywhere=10
-    )
+    spaces = [pltpu.SMEM] + [pltpu.VMEM] * 3 + [pl.ANY] * len(pieces)
+    return call(cross_kernel, "cross", (2, S, D), scratch, 4_000_000_000, 1_000_000, spaces, *args)
 
 
 def shift(array, axis, by, size):
     return lax.ppermute(array, axis, [(i, (i + by) % size) for i in range(size)])
 
 
-def gather_y(cross_query, cross_out):
-    mine = jnp.where(lax.axis_index("core") == 0, cross_query, cross_out)
-    return [shift(mine, "y", by, 4) for by in (3, 2, 1)] + [mine]
+def over_y(rows):
+    return [shift(rows, "y", by, 4) for by in (3, 2, 1)] + [rows]
 
 
 def in_order(rows):
@@ -337,19 +371,24 @@
     text_values,
     text_len,
 ):
-    rows = gather_y(cross_query, cross_out)
+    mine = jnp.where(lax.axis_index("core") == 0, cross_query, cross_out)
+    rows = over_y(mine)
+    far_mine = shift(mine, "x", 2, 4)
     after_spatial = spatial(latent.reshape(T, D), modulation, w_spatial_qkv, w_spatial_out)
-    rows, after_spatial = lax.optimization_barrier((rows, after_spatial))
+    rows, far_mine, after_spatial = lax.optimization_barrier((rows, far_mine, after_spatial))
     placed = lax.all_to_all(after_spatial, SEQ, split_axis=0, concat_axis=0, tiled=True)
     block = in_order(rows)
+    far_rows = over_y(far_mine)
     here = jnp.stack([block, shift(block, "z_lo", 1, 2)])
+    far_same = in_order(far_rows)
+    here, far_same, placed = lax.optimization_barrier((here, far_same, placed))
     left = shift(here, "x", 1, 4)
     right = shift(here, "x", -1, 4)
+    far_other = shift(far_same, "z_lo", 1, 2)
     after_temporal = temporal(placed, modulation, w_temporal_qkv, w_temporal_out)
+    pieces = [here, left, right, far_same, far_other]
+    pieces, after_temporal = lax.optimization_barrier((pieces, after_temporal))
     returned = lax.all_to_all(after_temporal, SEQ, split_axis=0, concat_axis=0, tiled=True)
-    far_first = shift(left[:, :CUT], "x", 1, 4)
-    far_last = shift(right[:, CUT:], "x", -1, 4)
-    pieces = [here, left, right, far_first, far_last]
     pieces = pieces + [over_core(piece) for piece in pieces]
     place = jnp.stack(
         [text_len[0], lax.axis_index("core"), lax.axis_index("z_lo"), lax.axis_index("x")]

time: 119 us -> 108 us (0.908); the launches traced: 118 us -> 106 us
  local copies, waits for them, and re-layouts: 14.4 us -> 3.54 us
  waiting for transfers between devices: 36.5 us -> 29.5 us
  starting transfers between devices: 30.1 us -> 33.6 us
  Pallas kernels: 35.1 us -> 37.2 us
    ppermute x13 -> x16, waiting for transfers between devices: 36.5 us -> 21.1 us  [shift(): lax.ppermute(array, axis, [(i, (i + by) % size) for i in range(size)])]
    unnamed x22 -> x20, local copies, waits for them, and re-layouts: 12.1 us -> 2.22 us
    all_to_all x1, waiting for transfers between devices: 0.01 us -> 8.37 us  [body(): lax.all_to_all(after_temporal, SEQ, split_axis=0, concat_axis=0, tiled=True)]
    ppermute x13 -> x16, starting transfers between devices: 16.1 us -> 20.2 us  [shift(): lax.ppermute(array, axis, [(i, (i + by) % size) for i in range(size)])]
    pallas_call x3, Pallas kernels: 35.1 us -> 37.2 us  [call(): pl.pallas_call(kernel, out_shape=jax.ShapeDtypeStruct(shape, BF16), in_sp...]
  transfers between devices with their start and end apart: 15 -> 18, of which waited for: 3 -> 4; matrix products, arithmetic and copies ran while one was open for 2% -> 2% of each run, Pallas kernels for 21% -> 26%
where the time goes in v4:
time: 108 us; the launch traced here: 106 us
  Pallas kernels  37.2 us (34%)
  starting transfers between devices  33.6 us (31%)
  waiting for transfers between devices  29.5 us (27%)
  local copies, waits for them, and re-layouts  3.54 us (3%)
  between operations  1.1 us (1%)
    pallas_call x3, Pallas kernels, call(): pl.pallas_call(kernel, out_shape=jax.ShapeDtypeStruct(shape, BF16), in_sp...  37.2 us
    ppermute x16, waiting for transfers between devices, shift(): lax.ppermute(array, axis, [(i, (i + by) % size) for i in range(size)])  21.1 us
    ppermute x16, starting transfers between devices, shift(): lax.ppermute(array, axis, [(i, (i + by) % size) for i in range(size)])  20.2 us
    all_to_all x1, waiting for transfers between devices, body(): lax.all_to_all(after_temporal, SEQ, split_axis=0, concat_axis=0, tiled=True)  8.37 us
    all_to_all x1, starting transfers between devices, body(): lax.all_to_all(after_temporal, SEQ, split_axis=0, concat_axis=0, tiled=True)  7.64 us
    all_to_all x1, starting transfers between devices, body(): lax.all_to_all(after_spatial, SEQ, split_axis=0, concat_axis=0, tiled=True)  5.76 us
    unnamed x20, local copies, waits for them, and re-layouts  2.22 us
  transfers between devices with their start and end apart: 18, of which 4 were waited for; matrix products, arithmetic and copies ran while one was open for 2% of the time, Pallas kernels for 26%

profile of v4, /device:TPU:1, one launch (start us, length us, event | category | flops | bytes accessed | tf_op | source)
XLA Modules:
  0.0 106.0 jit_solution(10691436444568910205)
XLA Ops:
  0.0 0.9 broadcast_select_fusion
  0.9 3.7 %collective-permute-start.3 = (bf16[36,1152]{1,0:T(8,128)(2,1)S(1)}, bf16[36,1152]{1,0:T(8,128)(2,1)S(1)}, u32[]{:S(2)}, u32[]{:S(2)}) collective-permute-start(bf16[36,1152]{1,0:T(8,128)(2,1)S(1)} %broadcast_select_fusion), channel_id=1, source_target_pairs={{0,32},{16,48},{32,0},{48,16},{1,33},{17,49},{33,1},{49,17},{2,34}... | collective-permute-start | bytes 248840 | tf_op jit(solution)/shard_map/ppermute | solution.py:344
  4.6 1.3 %collective-permute-start.2 = (bf16[36,1152]{1,0:T(8,128)(2,1)S(1)}, bf16[36,1152]{1,0:T(8,128)(2,1)S(1)}, u32[]{:S(2)}, u32[]{:S(2)}) collective-permute-start(bf16[36,1152]{1,0:T(8,128)(2,1)S(1)} %broadcast_select_fusion), channel_id=1, source_target_pairs={{0,4},{4,8},{8,12},{12,0},{1,5},{5,9},{9,13},{13,1},{2,6},{6,10},{... | collective-permute-start | bytes 248840 | tf_op jit(solution)/shard_map/ppermute | solution.py:344
  5.9 2.6 %collective-permute-start.1 = (bf16[36,1152]{1,0:T(8,128)(2,1)S(1)}, bf16[36,1152]{1,0:T(8,128)(2,1)S(1)}, u32[]{:S(2)}, u32[]{:S(2)}) collective-permute-start(bf16[36,1152]{1,0:T(8,128)(2,1)S(1)} %broadcast_select_fusion), channel_id=1, source_target_pairs={{0,8},{4,12},{8,0},{12,4},{1,9},{5,13},{9,1},{13,5},{2,10},{6,14},... | collective-permute-start | bytes 248840 | tf_op jit(solution)/shard_map/ppermute | solution.py:344
  8.5 1.1 %collective-permute-start = (bf16[36,1152]{1,0:T(8,128)(2,1)S(1)}, bf16[36,1152]{1,0:T(8,128)(2,1)S(1)}, u32[]{:S(2)}, u32[]{:S(2)}) collective-permute-start(bf16[36,1152]{1,0:T(8,128)(2,1)S(1)} %broadcast_select_fusion), channel_id=1, source_target_pairs={{0,12},{4,0},{8,4},{12,8},{1,13},{5,1},{9,5},{13,9},{2,14},{6,2},{... | collective-permute-start | bytes 248840 | tf_op jit(solution)/shard_map/ppermute | solution.py:344
  9.6 1.3 %copy-done = bf16[2,256,1152]{2,1,0:T(8,128)(2,1)S(1)} copy-done((bf16[2,256,1152]{2,1,0:T(8,128)(2,1)S(1)}, bf16[2,256,1152]{2,1,0:T(8,128)(2,1)}, u32[]{:S(2)}) %copy-start) | copy-done | bytes 1179672
  10.8 0.8 copy-done.1
  11.6 13.9 %spatial.1 = bf16[32,16,1152]{2,1,0:T(8,128)(2,1)} custom-call(bf16[512,1152]{1,0:T(8,128)(2,1)S(1)} %bitcast.27, f32[6,1152]{1,0:T(8,128)S(1)} %copy-done.1, bf16[1152,3456]{1,0:T(8,128)(2,1)} %w_hbm.2, bf16[1152,1152]{1,0:T(8,128)(2,1)} %wo_hbm.2), custom_call_target="tpu_custom_call" | custom-call | flops 8000000000 | bytes 13000000 | tf_op jit(solution)/shard_map/spatial/pallas_call | solution.py:289
  25.5 0.0 collective-permute-done.3
  25.5 0.0 collective-permute-done.2
  25.5 0.0 collective-permute-done.1
  25.6 0.0 collective-permute-done
  25.6 0.5 collective-permute-start.7
  26.0 0.8 collective-permute-start.6
  26.8 1.7 %collective-permute-start.5 = (bf16[36,1152]{1,0:T(8,128)(2,1)S(1)}, bf16[36,1152]{1,0:T(8,128)(2,1)S(1)}, u32[]{:S(2)}, u32[]{:S(2)}) collective-permute-start(bf16[36,1152]{1,0:T(8,128)(2,1)S(1)} %collective-permute-done.3), channel_id=1, source_target_pairs={{0,12},{4,0},{8,4},{12,8},{1,13},{5,1},{9,5},{13,9},{2,14},{6,2},{... | collective-permute-start | bytes 248840 | tf_op jit(solution)/shard_map/ppermute | solution.py:344
  28.7 0.1 reshape.10
  28.8 0.1 stack_reshape.3
  28.8 5.8 %all-to-all-start = ((bf16[32,16,1152]{2,1,0:T(8,128)(2,1)}), bf16[32,16,1152]{2,1,0:T(8,128)(2,1)S(1)}, u32[]{:S(2)}, u32[]{:S(2)}) async-start(bf16[32,16,1152]{2,1,0:T(8,128)(2,1)} %spatial.1), calls=%async_computation | async-start | bytes 2359296 | tf_op jit(solution)/shard_map/all_to_all | solution.py:379
  34.6 1.3 %collective-permute-start.4 = (bf16[144,1152]{1,0:T(8,128)(2,1)S(1)}, bf16[144,1152]{1,0:T(8,128)(2,1)S(1)}, u32[]{:S(2)}, u32[]{:S(2)}) collective-permute-start(bf16[144,1152]{1,0:T(8,128)(2,1)S(1)} %reshape.10), channel_id=1, source_target_pairs={{0,64},{64,0},{1,65},{65,1},{2,66},{66,2},{3,67},{67,3},{4,68},{68... | collective-permute-start | bytes 995336 | tf_op jit(solution)/shard_map/ppermute | solution.py:344
  35.9 0.0 collective-permute-done.5
  35.9 0.0 collective-permute-done.6
  36.1 0.0 copy-start.2
  36.1 0.1 reshape.11.refs_3_
  36.2 18.9 %collective-permute-done.4 = bf16[144,1152]{1,0:T(8,128)(2,1)S(1)} collective-permute-done((bf16[144,1152]{1,0:T(8,128)(2,1)S(1)}, bf16[144,1152]{1,0:T(8,128)(2,1)S(1)}, u32[]{:S(2)}, u32[]{:S(2)}) %collective-permute-start.4) | collective-permute-done | bytes 331808 | tf_op jit(solution)/shard_map/ppermute | solution.py:344
  55.1 0.1 pad_maximum_fusion.refs_0_
  55.2 0.0 all-to-all-done.x
  55.2 2.4 %collective-permute-start.9 = (bf16[2,144,1152]{2,1,0:T(8,128)(2,1)S(1)}, bf16[2,144,1152]{2,1,0:T(8,128)(2,1)S(1)}, u32[]{:S(2)}, u32[]{:S(2)}) collective-permute-start(bf16[2,144,1152]{2,1,0:T(8,128)(2,1)S(1)} %pad_maximum_fusion.refs_0_), channel_id=1, source_target_pairs={{0,48},{16,0},{32,16},{48,32},{1,49},{17,1},{33,17},{49,33},{2,50}... | collective-permute-start | bytes 1990664 | tf_op jit(solution)/shard_map/ppermute | solution.py:344
  57.6 0.0 collective-permute-start.8
  57.6 1.7 %collective-permute-start.10 = (bf16[144,1152]{1,0:T(8,128)(2,1)S(1)}, bf16[144,1152]{1,0:T(8,128)(2,1)}, u32[]{:S(2)}, u32[]{:S(2)}) collective-permute-start(bf16[144,1152]{1,0:T(8,128)(2,1)S(1)} %reshape.11.refs_3_), channel_id=1, source_target_pairs={{0,64},{64,0},{1,65},{65,1},{2,66},{66,2},{3,67},{67,3},{4,68},{68... | collective-permute-start | bytes 995336 | tf_op jit(solution)/shard_map/ppermute | solution.py:344
  59.4 13.6 %temporal.1 = bf16[32,16,1152]{2,1,0:T(8,128)(2,1)} custom-call(bf16[32,16,1152]{2,1,0:T(8,128)(2,1)S(1)} %all-to-all-done.x, f32[6,1152]{1,0:T(8,128)S(1)} %copy-done.2, bf16[1152,3456]{1,0:T(8,128)(2,1)} %w_hbm.3, bf16[1152,1152]{1,0:T(8,128)(2,1)} %wo_hbm.3), custom_call_target="tpu_custom_call" | custom-call | flops 8000000000 | bytes 13000000 | tf_op jit(solution)/shard_map/temporal/pallas_call | solution.py:289
  73.0 0.0 copy-start.3
  73.0 0.0 collective-permute-done.9.refs_2_
  73.0 0.0 collective-permute-done.8.refs_1_
  73.0 7.6 %all-to-all-start.1 = ((bf16[32,16,1152]{2,1,0:T(8,128)(2,1)}), bf16[32,16,1152]{2,1,0:T(8,128)(2,1)S(1)}, u32[]{:S(2)}, u32[]{:S(2)}) async-start(bf16[32,16,1152]{2,1,0:T(8,128)(2,1)} %temporal.1), calls=%async_computation.1 | async-start | bytes 2359296 | tf_op jit(solution)/shard_map/all_to_all | solution.py:391
  80.7 2.1 %collective-permute-start.11 = (bf16[2,144,1152]{2,1,0:T(8,128)(2,1)S(1)}, bf16[2,144,1152]{2,1,0:T(8,128)(2,1)}, u32[]{:S(2)}, u32[]{:S(2)}) collective-permute-start(bf16[2,144,1152]{2,1,0:T(8,128)(2,1)S(1)} %pad_maximum_fusion.refs_0_), channel_id=1, source_target_pairs={{0,1},{1,0},{2,3},{3,2},{4,5},{5,4},{6,7},{7,6},{8,9},{9,8},{10,11... | collective-permute-start | bytes 1990664 | tf_op jit(solution)/shard_map/ppermute | solution.py:344
  82.8 0.1 collective-permute-start.12
  82.9 0.4 collective-permute-start.13
  83.3 0.1 collective-permute-start.14
  83.4 0.4 collective-permute-start.15
  84.5 1.0 pad.8.values
  85.5 0.1 pad_add_fusion.place
  85.6 1.9 %collective-permute-done.14.refs_8_ = bf16[144,1152]{1,0:T(8,128)(2,1)} collective-permute-done((bf16[144,1152]{1,0:T(8,128)(2,1)S(1)}, bf16[144,1152]{1,0:T(8,128)(2,1)}, u32[]{:S(2)}, u32[]{:S(2)}) %collective-permute-start.14) | collective-permute-done | bytes 331808 | tf_op jit(solution)/shard_map/ppermute | solution.py:344
  87.5 0.2 collective-permute-done.15.refs_9_
  87.7 0.0 collective-permute-done.11.refs_5_
  87.7 0.0 collective-permute-done.12.refs_6_
  87.8 0.0 collective-permute-done.13.refs_7_
  87.8 8.4 %all-to-all-done.1.x = bf16[32,16,1152]{2,1,0:T(8,128)(2,1)S(1)} async-done(((bf16[32,16,1152]{2,1,0:T(8,128)(2,1)}), bf16[32,16,1152]{2,1,0:T(8,128)(2,1)S(1)}, u32[]{:S(2)}, u32[]{:S(2)}) %all-to-all-start.1) | async-done | bytes 1179680 | tf_op jit(solution)/shard_map/all_to_all | solution.py:391
  96.1 9.7 %cross.1 = bf16[2,256,1152]{2,1,0:T(8,128)(2,1)} custom-call(s32[4]{0:T(128)S(1)} %pad_add_fusion.place, bf16[32,16,1152]{2,1,0:T(8,128)(2,1)S(1)} %all-to-all-done.1.x, bf16[128,1152]{1,0:T(8,128)(2,1)S(1)} %pad.7.keys, bf16[128,1152]{1,0:T(8,128)(2,1)S(1)} %pad.8.values, bf16[2,144,1152]{2,1,0:T(8,128)(2,1)S(1)} %pad_maximum_fusion.refs_0_, ...), custom_call_target="tpu_custom_call" | custom-call | flops 4000000000 | bytes 13000000 | tf_op jit(solution)/shard_map/cross/pallas_call | solution.py:289
  (23 shorter events, 0.3 us)
Async XLA Ops:
  0.9 24.6 %collective-permute-start.3 = (bf16[36,1152]{1,0:T(8,128)(2,1)S(1)}, bf16[36,1152]{1,0:T(8,128)(2,1)S(1)}, u32[]{:S(2)}, u32[]{:S(2)}) collective-permute-start(bf16[36,1152]{1,0:T(8,128)(2,1)S(1)} %broadcast_select_fusion), channel_id=1, source_target_pairs={{0,32},{16,48},{32,0},{48,16},{1,33},{17,49},{33,1},{49,17},{2,34}... | collective-permute-start | bytes 248840 | tf_op jit(solution)/shard_map/ppermute | solution.py:344
  4.6 21.0 %collective-permute-start.2 = (bf16[36,1152]{1,0:T(8,128)(2,1)S(1)}, bf16[36,1152]{1,0:T(8,128)(2,1)S(1)}, u32[]{:S(2)}, u32[]{:S(2)}) collective-permute-start(bf16[36,1152]{1,0:T(8,128)(2,1)S(1)} %broadcast_select_fusion), channel_id=1, source_target_pairs={{0,4},{4,8},{8,12},{12,0},{1,5},{5,9},{9,13},{13,1},{2,6},{6,10},{... | collective-permute-start | bytes 248840 | tf_op jit(solution)/shard_map/ppermute | solution.py:344
  5.9 19.7 %collective-permute-start.1 = (bf16[36,1152]{1,0:T(8,128)(2,1)S(1)}, bf16[36,1152]{1,0:T(8,128)(2,1)S(1)}, u32[]{:S(2)}, u32[]{:S(2)}) collective-permute-start(bf16[36,1152]{1,0:T(8,128)(2,1)S(1)} %broadcast_select_fusion), channel_id=1, source_target_pairs={{0,8},{4,12},{8,0},{12,4},{1,9},{5,13},{9,1},{13,5},{2,10},{6,14},... | collective-permute-start | bytes 248840 | tf_op jit(solution)/shard_map/ppermute | solution.py:344
  8.5 17.1 %collective-permute-start = (bf16[36,1152]{1,0:T(8,128)(2,1)S(1)}, bf16[36,1152]{1,0:T(8,128)(2,1)S(1)}, u32[]{:S(2)}, u32[]{:S(2)}) collective-permute-start(bf16[36,1152]{1,0:T(8,128)(2,1)S(1)} %broadcast_select_fusion), channel_id=1, source_target_pairs={{0,12},{4,0},{8,4},{12,8},{1,13},{5,1},{9,5},{13,9},{2,14},{6,2},{... | collective-permute-start | bytes 248840 | tf_op jit(solution)/shard_map/ppermute | solution.py:344
  9.5 1.3 %copy-start = (bf16[2,256,1152]{2,1,0:T(8,128)(2,1)S(1)}, bf16[2,256,1152]{2,1,0:T(8,128)(2,1)}, u32[]{:S(2)}) copy-start(bf16[2,256,1152]{2,1,0:T(8,128)(2,1)} %param.11) | copy-start | bytes 3538948
  10.8 0.8 copy-start.1
  25.6 10.4 %collective-permute-start.7 = (bf16[36,1152]{1,0:T(8,128)(2,1)S(1)}, bf16[36,1152]{1,0:T(8,128)(2,1)S(1)}, u32[]{:S(2)}, u32[]{:S(2)}) collective-permute-start(bf16[36,1152]{1,0:T(8,128)(2,1)S(1)} %collective-permute-done.3), channel_id=1, source_target_pairs={{0,4},{4,8},{8,12},{12,0},{1,5},{5,9},{9,13},{13,1},{2,6},{6,10},{... | collective-permute-start | bytes 248840 | tf_op jit(solution)/shard_map/ppermute | solution.py:344
  26.0 9.9 %collective-permute-start.6 = (bf16[36,1152]{1,0:T(8,128)(2,1)S(1)}, bf16[36,1152]{1,0:T(8,128)(2,1)S(1)}, u32[]{:S(2)}, u32[]{:S(2)}) collective-permute-start(bf16[36,1152]{1,0:T(8,128)(2,1)S(1)} %collective-permute-done.3), channel_id=1, source_target_pairs={{0,8},{4,12},{8,0},{12,4},{1,9},{5,13},{9,1},{13,5},{2,10},{6,14},... | collective-permute-start | bytes 248840 | tf_op jit(solution)/shard_map/ppermute | solution.py:344
  26.8 9.1 %collective-permute-start.5 = (bf16[36,1152]{1,0:T(8,128)(2,1)S(1)}, bf16[36,1152]{1,0:T(8,128)(2,1)S(1)}, u32[]{:S(2)}, u32[]{:S(2)}) collective-permute-start(bf16[36,1152]{1,0:T(8,128)(2,1)S(1)} %collective-permute-done.3), channel_id=1, source_target_pairs={{0,12},{4,0},{8,4},{12,8},{1,13},{5,1},{9,5},{13,9},{2,14},{6,2},{... | collective-permute-start | bytes 248840 | tf_op jit(solution)/shard_map/ppermute | solution.py:344
  28.8 26.4 %all-to-all-start = ((bf16[32,16,1152]{2,1,0:T(8,128)(2,1)}), bf16[32,16,1152]{2,1,0:T(8,128)(2,1)S(1)}, u32[]{:S(2)}, u32[]{:S(2)}) async-start(bf16[32,16,1152]{2,1,0:T(8,128)(2,1)} %spatial.1), calls=%async_computation | async-start | bytes 2359296 | tf_op jit(solution)/shard_map/all_to_all | solution.py:379
  34.6 20.5 %collective-permute-start.4 = (bf16[144,1152]{1,0:T(8,128)(2,1)S(1)}, bf16[144,1152]{1,0:T(8,128)(2,1)S(1)}, u32[]{:S(2)}, u32[]{:S(2)}) collective-permute-start(bf16[144,1152]{1,0:T(8,128)(2,1)S(1)} %reshape.10), channel_id=1, source_target_pairs={{0,64},{64,0},{1,65},{65,1},{2,66},{66,2},{3,67},{67,3},{4,68},{68... | collective-permute-start | bytes 995336 | tf_op jit(solution)/shard_map/ppermute | solution.py:344
  36.1 23.2 %copy-start.2 = (f32[6,1152]{1,0:T(8,128)S(1)}, f32[6,1152]{1,0:T(8,128)}, u32[]{:S(2)}) copy-start(f32[6,1152]{1,0:T(8,128)} %mod.3) | copy-start | bytes 82948
  55.2 17.8 %collective-permute-start.9 = (bf16[2,144,1152]{2,1,0:T(8,128)(2,1)S(1)}, bf16[2,144,1152]{2,1,0:T(8,128)(2,1)S(1)}, u32[]{:S(2)}, u32[]{:S(2)}) collective-permute-start(bf16[2,144,1152]{2,1,0:T(8,128)(2,1)S(1)} %pad_maximum_fusion.refs_0_), channel_id=1, source_target_pairs={{0,48},{16,0},{32,16},{48,32},{1,49},{17,1},{33,17},{49,33},{2,50}... | collective-permute-start | bytes 1990664 | tf_op jit(solution)/shard_map/ppermute | solution.py:344
  57.6 15.4 %collective-permute-start.8 = (bf16[2,144,1152]{2,1,0:T(8,128)(2,1)S(1)}, bf16[2,144,1152]{2,1,0:T(8,128)(2,1)}, u32[]{:S(2)}, u32[]{:S(2)}) collective-permute-start(bf16[2,144,1152]{2,1,0:T(8,128)(2,1)S(1)} %pad_maximum_fusion.refs_0_), channel_id=1, source_target_pairs={{0,16},{16,32},{32,48},{48,0},{1,17},{17,33},{33,49},{49,1},{2,18}... | collective-permute-start | bytes 1990664 | tf_op jit(solution)/shard_map/ppermute | solution.py:344
  57.6 15.4 %collective-permute-start.10 = (bf16[144,1152]{1,0:T(8,128)(2,1)S(1)}, bf16[144,1152]{1,0:T(8,128)(2,1)}, u32[]{:S(2)}, u32[]{:S(2)}) collective-permute-start(bf16[144,1152]{1,0:T(8,128)(2,1)S(1)} %reshape.11.refs_3_), channel_id=1, source_target_pairs={{0,64},{64,0},{1,65},{65,1},{2,66},{66,2},{3,67},{67,3},{4,68},{68... | collective-permute-start | bytes 995336 | tf_op jit(solution)/shard_map/ppermute | solution.py:344
  73.0 11.5 %copy-start.3 = (bf16[120,1152]{1,0:T(8,128)(2,1)S(1)}, bf16[120,1152]{1,0:T(8,128)(2,1)}, u32[]{:S(2)}) copy-start(bf16[120,1152]{1,0:T(8,128)(2,1)} %param.19) | copy-start | bytes 829444
  73.0 23.1 %all-to-all-start.1 = ((bf16[32,16,1152]{2,1,0:T(8,128)(2,1)}), bf16[32,16,1152]{2,1,0:T(8,128)(2,1)S(1)}, u32[]{:S(2)}, u32[]{:S(2)}) async-start(bf16[32,16,1152]{2,1,0:T(8,128)(2,1)} %temporal.1), calls=%async_computation.1 | async-start | bytes 2359296 | tf_op jit(solution)/shard_map/all_to_all | solution.py:391
  80.7 7.1 %collective-permute-start.11 = (bf16[2,144,1152]{2,1,0:T(8,128)(2,1)S(1)}, bf16[2,144,1152]{2,1,0:T(8,128)(2,1)}, u32[]{:S(2)}, u32[]{:S(2)}) collective-permute-start(bf16[2,144,1152]{2,1,0:T(8,128)(2,1)S(1)} %pad_maximum_fusion.refs_0_), channel_id=1, source_target_pairs={{0,1},{1,0},{2,3},{3,2},{4,5},{5,4},{6,7},{7,6},{8,9},{9,8},{10,11... | collective-permute-start | bytes 1990664 | tf_op jit(solution)/shard_map/ppermute | solution.py:344
  82.8 4.9 %collective-permute-start.12 = (bf16[2,144,1152]{2,1,0:T(8,128)(2,1)}, bf16[2,144,1152]{2,1,0:T(8,128)(2,1)}, u32[]{:S(2)}, u32[]{:S(2)}) collective-permute-start(bf16[2,144,1152]{2,1,0:T(8,128)(2,1)} %collective-permute-done.8.refs_1_), channel_id=1, source_target_pairs={{0,1},{1,0},{2,3},{3,2},{4,5},{5,4},{6,7},{7,6},{8,9},{9,8},{10,11... | collective-permute-start | bytes 1990664 | tf_op jit(solution)/shard_map/ppermute | solution.py:344
  82.9 4.8 %collective-permute-start.13 = (bf16[2,144,1152]{2,1,0:T(8,128)(2,1)S(1)}, bf16[2,144,1152]{2,1,0:T(8,128)(2,1)}, u32[]{:S(2)}, u32[]{:S(2)}) collective-permute-start(bf16[2,144,1152]{2,1,0:T(8,128)(2,1)S(1)} %collective-permute-done.9.refs_2_), channel_id=1, source_target_pairs={{0,1},{1,0},{2,3},{3,2},{4,5},{5,4},{6,7},{7,6},{8,9},{9,8},{10,11... | collective-permute-start | bytes 1990664 | tf_op jit(solution)/shard_map/ppermute | solution.py:344
  83.3 4.2 %collective-permute-start.14 = (bf16[144,1152]{1,0:T(8,128)(2,1)S(1)}, bf16[144,1152]{1,0:T(8,128)(2,1)}, u32[]{:S(2)}, u32[]{:S(2)}) collective-permute-start(bf16[144,1152]{1,0:T(8,128)(2,1)S(1)} %reshape.11.refs_3_), channel_id=1, source_target_pairs={{0,1},{1,0},{2,3},{3,2},{4,5},{5,4},{6,7},{7,6},{8,9},{9,8},{10,11... | collective-permute-start | bytes 995336 | tf_op jit(solution)/shard_map/ppermute | solution.py:344
  83.4 4.3 %collective-permute-start.15 = (bf16[144,1152]{1,0:T(8,128)(2,1)}, bf16[144,1152]{1,0:T(8,128)(2,1)}, u32[]{:S(2)}, u32[]{:S(2)}) collective-permute-start(bf16[144,1152]{1,0:T(8,128)(2,1)} %collective-permute-done.10.refs_4_), channel_id=1, source_target_pairs={{0,1},{1,0},{2,3},{3,2},{4,5},{5,4},{6,7},{7,6},{8,9},{9,8},{10,11... | collective-permute-start | bytes 995336 | tf_op jit(solution)/shard_map/ppermute | solution.py:344

commit v5 on v4

--- a/solution.py
+++ b/solution.py
@@ -20,8 +20,8 @@
 F32 = jnp.float32
 BF16 = jnp.bfloat16
 NT = (((1,), (1,)), ((), ()))
-SEQ = ("z_lo", "x", "y")
-ALL = ("z_hi", "core", "z_lo", "x", "y")
+SEQ = ("z_lo", "x_hi", "x_lo", "y")
+ALL = ("z_hi", "core") + SEQ
 
 
 def mm(a, b):
@@ -214,23 +214,21 @@
 
 
 def cross_kernel(place, x, keys, values, *refs):
-    pieces, (out, w, query, weights, over, v_t, ctx_t, ctx, sems) = refs[:10], refs[10:]
-    length, core, z_lo, x_at = place[0], place[1], place[2], place[3]
-
-    def put(which, src, z, x_from):
-        row = pl.multiple_of(z * (D // 2) + x_from * BLOCK, 16)
+    pieces, (out, w, query, weights, over, v_t, ctx_t, ctx, sems) = refs[:6], refs[6:]
+    length, core, x_lo = place[0], place[1], place[2]
+
+    def put(which, src, z, x):
+        row = pl.multiple_of(z * (D // 2) + x * BLOCK, 16)
         pltpu.make_async_copy(src, w.at[which, pl.ds(row, BLOCK), :], sems.at[which]).start()
 
-    left, right, far = (x_at + 3) % 4, (x_at + 1) % 4, (x_at + 2) % 4
     for own in range(2):
         which = core if own == 0 else 1 - core
-        here, from_left, from_right, far_same, far_other = pieces[5 * own : 5 * own + 5]
-        for n, z in enumerate((z_lo, 1 - z_lo)):
-            put(which, here.at[n], z, x_at)
-            put(which, from_left.at[n], z, left)
-            put(which, from_right.at[n], z, right)
-        put(which, far_same, z_lo, far)
-        put(which, far_other, 1 - z_lo, far)
+        same, other_first, other_last = pieces[3 * own : 3 * own + 3]
+        for z in range(2):
+            put(which, same.at[0, z], z, x_lo)
+            put(which, same.at[1, z], z, 2 + x_lo)
+            put(which, other_first.at[z], z, 1 - x_lo)
+            put(which, other_last.at[z], z, 3 - x_lo)
 
     def whole(which):
         pltpu.make_async_copy(w.at[which], w.at[which], sems.at[which]).wait()
@@ -340,22 +338,15 @@
     return call(cross_kernel, "cross", (2, S, D), scratch, 4_000_000_000, 1_000_000, spaces, *args)
 
 
-def shift(array, axis, by, size):
-    return lax.ppermute(array, axis, [(i, (i + by) % size) for i in range(size)])
-
-
-def over_y(rows):
-    return [shift(rows, "y", by, 4) for by in (3, 2, 1)] + [rows]
-
-
-def in_order(rows):
-    found = jnp.stack(rows + rows[:3])
-    ordered = lax.dynamic_slice_in_dim(found, 3 - lax.axis_index("y"), 4, axis=0)
-    return ordered.reshape(BLOCK, D)
-
-
-def over_core(piece):
-    return shift(piece, "core", 1, 2)
+def shift(array, axes, by, size):
+    return lax.ppermute(array, axes, [(i, (i + by) % size) for i in range(size)])
+
+
+def gather_even(rows):
+    copies = jnp.broadcast_to(rows[None], (16,) + rows.shape)
+    axes = ("x_hi", "z_lo", "y")
+    found = lax.all_to_all(copies, axes, split_axis=0, concat_axis=0, tiled=True)
+    return found
 
 
 def body(
@@ -372,26 +363,21 @@
     text_len,
 ):
     mine = jnp.where(lax.axis_index("core") == 0, cross_query, cross_out)
-    rows = over_y(mine)
-    far_mine = shift(mine, "x", 2, 4)
+    found = gather_even(mine)
     after_spatial = spatial(latent.reshape(T, D), modulation, w_spatial_qkv, w_spatial_out)
-    rows, far_mine, after_spatial = lax.optimization_barrier((rows, far_mine, after_spatial))
+    found, after_spatial = lax.optimization_barrier((found, after_spatial))
     placed = lax.all_to_all(after_spatial, SEQ, split_axis=0, concat_axis=0, tiled=True)
-    block = in_order(rows)
-    far_rows = over_y(far_mine)
-    here = jnp.stack([block, shift(block, "z_lo", 1, 2)])
-    far_same = in_order(far_rows)
-    here, far_same, placed = lax.optimization_barrier((here, far_same, placed))
-    left = shift(here, "x", 1, 4)
-    right = shift(here, "x", -1, 4)
-    far_other = shift(far_same, "z_lo", 1, 2)
+    same = found.reshape(2, 2, BLOCK, D)
+    same, placed = lax.optimization_barrier((same, placed))
+    other_first = shift(same[0], ("x_hi", "x_lo"), 1, 4)
+    other_last = shift(same[1], ("x_hi", "x_lo"), -1, 4)
     after_temporal = temporal(placed, modulation, w_temporal_qkv, w_temporal_out)
-    pieces = [here, left, right, far_same, far_other]
+    pieces = [same, other_first, other_last]
     pieces, after_temporal = lax.optimization_barrier((pieces, after_temporal))
     returned = lax.all_to_all(after_temporal, SEQ, split_axis=0, concat_axis=0, tiled=True)
-    pieces = pieces + [over_core(piece) for piece in pieces]
+    pieces = pieces + [shift(piece, "core", 1, 2) for piece in pieces]
     place = jnp.stack(
-        [text_len[0], lax.axis_index("core"), lax.axis_index("z_lo"), lax.axis_index("x")]
+        [text_len[0], lax.axis_index("core"), lax.axis_index("x_lo")]
     ).astype(jnp.int32)
     fill = ((0, SLOTS - text_keys.shape[0]), (0, 0))
     keys, values = jnp.pad(text_keys, fill), jnp.pad(text_values, fill)
@@ -399,7 +385,7 @@
 
 
 def solution(mesh):
-    fine = Mesh(mesh.devices.reshape(2, 4, 4, 2, 2), ("z_lo", "x", "y", "z_hi", "core"))
+    fine = Mesh(mesh.devices.reshape(2, 2, 2, 4, 2, 2), SEQ + ("z_hi", "core"))
     part = ("z_hi", "core")
     placed = (
         P(ALL, None, None),

time: 108 us -> 105 us (0.972); the launches traced: 106 us -> 105 us
  starting transfers between devices: 33.6 us -> 25.2 us
  waiting for transfers between devices: 29.5 us -> 36.8 us
    ppermute x16 -> x5, waiting for transfers between devices: 21.1 us -> 2.34 us  [shift(): lax.ppermute(array, axes, [(i, (i + by) % size) for i in range(size)])]
    all_to_all x1, waiting for transfers between devices: 0.01 us -> 12.8 us  [body(): lax.all_to_all(after_spatial, SEQ, split_axis=0, concat_axis=0, tiled=True)]
    ppermute x16 -> x5, starting transfers between devices: 20.2 us -> 8.2 us  [shift(): lax.ppermute(array, axes, [(i, (i + by) % size) for i in range(size)])]
    all_to_all x0 -> x1, starting transfers between devices: none -> 9.11 us  [gather_even(): lax.all_to_all(copies, axes, split_axis=0, concat_axis=0, tiled=True)]
    all_to_all x0 -> x1, waiting for transfers between devices: none -> 7.76 us  [gather_even(): lax.all_to_all(copies, axes, split_axis=0, concat_axis=0, tiled=True)]
    all_to_all x1, waiting for transfers between devices: 8.37 us -> 14 us  [body(): lax.all_to_all(after_temporal, SEQ, split_axis=0, concat_axis=0, tiled=True)]
    all_to_all x1, starting transfers between devices: 7.64 us -> 3.96 us  [body(): lax.all_to_all(after_temporal, SEQ, split_axis=0, concat_axis=0, tiled=True)]
    unnamed x20 -> x8, local copies, waits for them, and re-layouts: 2.22 us -> 0.02 us
  transfers between devices with their start and end apart: 18 -> 8, of which waited for: 4 -> 6; matrix products, arithmetic and copies ran while one was open for 2% -> 2% of each run, Pallas kernels for 26% -> 26%
where the time goes in v5:
time: 105 us
  Pallas kernels  37.1 us (35%)
  waiting for transfers between devices  36.8 us (35%)
  starting transfers between devices  25.2 us (24%)
  local copies, waits for them, and re-layouts  3.66 us (3%)
    pallas_call x3, Pallas kernels, call(): pl.pallas_call(kernel, out_shape=jax.ShapeDtypeStruct(shape, BF16), in_sp...  37.1 us
    all_to_all x1, waiting for transfers between devices, body(): lax.all_to_all(after_temporal, SEQ, split_axis=0, concat_axis=0, tiled=True)  14 us
    all_to_all x1, waiting for transfers between devices, body(): lax.all_to_all(after_spatial, SEQ, split_axis=0, concat_axis=0, tiled=True)  12.8 us
    all_to_all x1, starting transfers between devices, gather_even(): lax.all_to_all(copies, axes, split_axis=0, concat_axis=0, tiled=True)  9.11 us
    ppermute x5, starting transfers between devices, shift(): lax.ppermute(array, axes, [(i, (i + by) % size) for i in range(size)])  8.2 us
    all_to_all x1, waiting for transfers between devices, gather_even(): lax.all_to_all(copies, axes, split_axis=0, concat_axis=0, tiled=True)  7.76 us
    all_to_all x1, starting transfers between devices, body(): lax.all_to_all(after_temporal, SEQ, split_axis=0, concat_axis=0, tiled=True)  3.96 us
    all_to_all x1, starting transfers between devices, body(): lax.all_to_all(after_spatial, SEQ, split_axis=0, concat_axis=0, tiled=True)  3.94 us
  transfers between devices with their start and end apart: 8, of which 6 were waited for; matrix products, arithmetic and copies ran while one was open for 2% of the time, Pallas kernels for 26%

profile of v5, /device:TPU:1, one launch (start us, length us, event | category | flops | bytes accessed | tf_op | source)
XLA Modules:
  0.0 104.8 jit_solution(10465929532459213124)
XLA Ops:
  0.0 0.9 broadcast_select_fusion
  0.9 1.2 %broadcast_in_dim.2 = bf16[16,36,1152]{2,1,0:T(8,128)(2,1)} broadcast(bf16[36,1152]{1,0:T(8,128)(2,1)S(1)} %broadcast_select_fusion), dimensions={1,2} | broadcast | bytes 1410048 | tf_op jit(solution)/shard_map/broadcast_in_dim | solution.py:346
  2.1 0.0 copy-start
  2.1 0.0 copy-start.1
  2.1 9.1 %all-to-all-start = ((bf16[16,36,1152]{2,1,0:T(8,128)(2,1)}), bf16[16,36,1152]{2,1,0:T(8,128)(2,1)}, u32[]{:S(2)}, u32[]{:S(2)}) async-start(bf16[16,36,1152]{2,1,0:T(8,128)(2,1)} %broadcast_in_dim.2), calls=%async_computation | async-start | bytes 2949120 | tf_op jit(solution)/shard_map/all_to_all | solution.py:348
  11.3 0.0 copy-done
  11.3 0.0 copy-done.1
  11.3 13.9 %spatial.1 = bf16[32,16,1152]{2,1,0:T(8,128)(2,1)} custom-call(bf16[512,1152]{1,0:T(8,128)(2,1)S(1)} %bitcast.7, f32[6,1152]{1,0:T(8,128)S(1)} %copy-done.1, bf16[1152,3456]{1,0:T(8,128)(2,1)} %w_hbm.2, bf16[1152,1152]{1,0:T(8,128)(2,1)} %wo_hbm.2), custom_call_target="tpu_custom_call" | custom-call | flops 8000000000 | bytes 13000000 | tf_op jit(solution)/shard_map/spatial/pallas_call | solution.py:287
  25.2 7.8 %all-to-all-done = bf16[16,36,1152]{2,1,0:T(8,128)(2,1)} async-done(((bf16[16,36,1152]{2,1,0:T(8,128)(2,1)}), bf16[16,36,1152]{2,1,0:T(8,128)(2,1)}, u32[]{:S(2)}, u32[]{:S(2)}) %all-to-all-start) | async-done | bytes 1327136 | tf_op jit(solution)/shard_map/all_to_all | solution.py:348
  33.0 3.9 %all-to-all-start.1 = ((bf16[32,16,1152]{2,1,0:T(8,128)(2,1)}), bf16[32,16,1152]{2,1,0:T(8,128)(2,1)S(1)}, u32[]{:S(2)}, u32[]{:S(2)}) async-start(bf16[32,16,1152]{2,1,0:T(8,128)(2,1)} %spatial.1), calls=%async_computation.1 | async-start | bytes 2359296 | tf_op jit(solution)/shard_map/all_to_all | solution.py:369
  36.9 2.3 %reshape.8.refs_0_ = bf16[2,2,144,1152]{3,2,1,0:T(8,128)(2,1)S(1)} reshape(bf16[16,36,1152]{2,1,0:T(8,128)(2,1)} %all-to-all-done) | data formatting | bytes 2654208 | tf_op jit(solution)/shard_map/reshape | solution.py:370
  39.2 12.8 %all-to-all-done.1.x = bf16[32,16,1152]{2,1,0:T(8,128)(2,1)S(1)} async-done(((bf16[32,16,1152]{2,1,0:T(8,128)(2,1)}), bf16[32,16,1152]{2,1,0:T(8,128)(2,1)S(1)}, u32[]{:S(2)}, u32[]{:S(2)}) %all-to-all-start.1) | async-done | bytes 1179680 | tf_op jit(solution)/shard_map/all_to_all | solution.py:369
  52.0 0.1 slice_bitcast_fusion
  52.1 2.8 %collective-permute-start.1 = (bf16[2,144,1152]{2,1,0:T(8,128)(2,1)S(1)}, bf16[2,144,1152]{2,1,0:T(8,128)(2,1)}, u32[]{:S(2)}, u32[]{:S(2)}) collective-permute-start(bf16[2,144,1152]{2,1,0:T(8,128)(2,1)S(1)} %get-tuple-element.21), channel_id=1, source_target_pairs={{0,48},{16,0},{32,16},{48,32},{1,49},{17,1},{33,17},{49,33},{2,50}... | collective-permute-start | bytes 1990664 | tf_op jit(solution)/shard_map/ppermute | solution.py:342
  54.9 0.0 collective-permute-start
  54.9 13.6 %temporal.1 = bf16[32,16,1152]{2,1,0:T(8,128)(2,1)} custom-call(bf16[32,16,1152]{2,1,0:T(8,128)(2,1)S(1)} %all-to-all-done.1.x, f32[6,1152]{1,0:T(8,128)S(1)} %copy-done.1, bf16[1152,3456]{1,0:T(8,128)(2,1)} %w_hbm.3, bf16[1152,1152]{1,0:T(8,128)(2,1)} %wo_hbm.3), custom_call_target="tpu_custom_call" | custom-call | flops 8000000000 | bytes 13000000 | tf_op jit(solution)/shard_map/temporal/pallas_call | solution.py:287
  68.5 0.0 copy-start.2
  68.5 0.0 copy-start.3
  68.5 0.0 collective-permute-done.1.refs_2_
  68.5 0.4 collective-permute-done.refs_1_
  69.0 4.5 %collective-permute-start.2 = (bf16[2,2,144,1152]{3,2,1,0:T(8,128)(2,1)S(1)}, bf16[2,2,144,1152]{3,2,1,0:T(8,128)(2,1)}, u32[]{:S(2)}, u32[]{:S(2)}) collective-permute-start(bf16[2,2,144,1152]{3,2,1,0:T(8,128)(2,1)S(1)} %reshape.8.refs_0_), channel_id=1, source_target_pairs={{0,1},{1,0},{2,3},{3,2},{4,5},{5,4},{6,7},{7,6},{8,9},{9,8},{10,11... | collective-permute-start | bytes 3981320 | tf_op jit(solution)/shard_map/ppermute | solution.py:342
  73.5 4.0 %all-to-all-start.2 = ((bf16[32,16,1152]{2,1,0:T(8,128)(2,1)}), bf16[32,16,1152]{2,1,0:T(8,128)(2,1)S(1)}, u32[]{:S(2)}, u32[]{:S(2)}) async-start(bf16[32,16,1152]{2,1,0:T(8,128)(2,1)} %temporal.1), calls=%async_computation.2 | async-start | bytes 2359296 | tf_op jit(solution)/shard_map/all_to_all | solution.py:377
  77.5 0.5 collective-permute-start.3
  78.0 0.3 collective-permute-start.4
  79.0 0.0 copy-done.2
  79.0 0.0 copy-done.3
  79.1 0.1 pad_add_fusion.place
  79.2 0.9 collective-permute-done.3.refs_4_
  80.1 0.9 collective-permute-done.4.refs_5_
  81.0 14.0 %all-to-all-done.2.x = bf16[32,16,1152]{2,1,0:T(8,128)(2,1)S(1)} async-done(((bf16[32,16,1152]{2,1,0:T(8,128)(2,1)}), bf16[32,16,1152]{2,1,0:T(8,128)(2,1)S(1)}, u32[]{:S(2)}, u32[]{:S(2)}) %all-to-all-start.2) | async-done | bytes 1179680 | tf_op jit(solution)/shard_map/all_to_all | solution.py:377
  95.0 0.0 collective-permute-done.2.refs_3_
  95.0 9.6 %cross.1 = bf16[2,256,1152]{2,1,0:T(8,128)(2,1)} custom-call(s32[3]{0:T(128)S(1)} %pad_add_fusion.place, bf16[32,16,1152]{2,1,0:T(8,128)(2,1)S(1)} %all-to-all-done.2.x, bf16[128,1152]{1,0:T(8,128)(2,1)S(1)} %pad.7.keys, bf16[128,1152]{1,0:T(8,128)(2,1)S(1)} %pad.8.values, bf16[2,2,144,1152]{3,2,1,0:T(8,128)(2,1)S(1)} %reshape.8.refs_0_, ...), custom_call_target="tpu_custom_call" | custom-call | flops 4000000000 | bytes 13000000 | tf_op jit(solution)/shard_map/cross/pallas_call | solution.py:287
  (2 shorter events, 0.0 us)
Async XLA Ops:
  2.1 9.1 %copy-start = (bf16[2,256,1152]{2,1,0:T(8,128)(2,1)S(1)}, bf16[2,256,1152]{2,1,0:T(8,128)(2,1)}, u32[]{:S(2)}) copy-start(bf16[2,256,1152]{2,1,0:T(8,128)(2,1)} %param.11) | copy-start | bytes 3538948
  2.1 9.1 %copy-start.1 = (f32[6,1152]{1,0:T(8,128)S(1)}, f32[6,1152]{1,0:T(8,128)}, u32[]{:S(2)}) copy-start(f32[6,1152]{1,0:T(8,128)} %mod.3) | copy-start | bytes 82948
  2.1 30.8 %all-to-all-start = ((bf16[16,36,1152]{2,1,0:T(8,128)(2,1)}), bf16[16,36,1152]{2,1,0:T(8,128)(2,1)}, u32[]{:S(2)}, u32[]{:S(2)}) async-start(bf16[16,36,1152]{2,1,0:T(8,128)(2,1)} %broadcast_in_dim.2), calls=%async_computation | async-start | bytes 2949120 | tf_op jit(solution)/shard_map/all_to_all | solution.py:348
  33.0 19.0 %all-to-all-start.1 = ((bf16[32,16,1152]{2,1,0:T(8,128)(2,1)}), bf16[32,16,1152]{2,1,0:T(8,128)(2,1)S(1)}, u32[]{:S(2)}, u32[]{:S(2)}) async-start(bf16[32,16,1152]{2,1,0:T(8,128)(2,1)} %spatial.1), calls=%async_computation.1 | async-start | bytes 2359296 | tf_op jit(solution)/shard_map/all_to_all | solution.py:369
  52.1 16.5 %collective-permute-start.1 = (bf16[2,144,1152]{2,1,0:T(8,128)(2,1)S(1)}, bf16[2,144,1152]{2,1,0:T(8,128)(2,1)}, u32[]{:S(2)}, u32[]{:S(2)}) collective-permute-start(bf16[2,144,1152]{2,1,0:T(8,128)(2,1)S(1)} %get-tuple-element.21), channel_id=1, source_target_pairs={{0,48},{16,0},{32,16},{48,32},{1,49},{17,1},{33,17},{49,33},{2,50}... | collective-permute-start | bytes 1990664 | tf_op jit(solution)/shard_map/ppermute | solution.py:342
  54.9 14.1 %collective-permute-start = (bf16[2,144,1152]{2,1,0:T(8,128)(2,1)S(1)}, bf16[2,144,1152]{2,1,0:T(8,128)(2,1)}, u32[]{:S(2)}, u32[]{:S(2)}) collective-permute-start(bf16[2,144,1152]{2,1,0:T(8,128)(2,1)S(1)} %get-tuple-element.22), channel_id=1, source_target_pairs={{0,16},{16,32},{32,48},{48,0},{1,17},{17,33},{33,49},{49,1},{2,18}... | collective-permute-start | bytes 1990664 | tf_op jit(solution)/shard_map/ppermute | solution.py:342
  68.5 10.5 %copy-start.2 = (bf16[120,1152]{1,0:T(8,128)(2,1)S(1)}, bf16[120,1152]{1,0:T(8,128)(2,1)}, u32[]{:S(2)}) copy-start(bf16[120,1152]{1,0:T(8,128)(2,1)} %param.19) | copy-start | bytes 829444
  68.5 10.5 %copy-start.3 = (bf16[120,1152]{1,0:T(8,128)(2,1)S(1)}, bf16[120,1152]{1,0:T(8,128)(2,1)}, u32[]{:S(2)}) copy-start(bf16[120,1152]{1,0:T(8,128)(2,1)} %param.20) | copy-start | bytes 829444
  69.0 26.0 %collective-permute-start.2 = (bf16[2,2,144,1152]{3,2,1,0:T(8,128)(2,1)S(1)}, bf16[2,2,144,1152]{3,2,1,0:T(8,128)(2,1)}, u32[]{:S(2)}, u32[]{:S(2)}) collective-permute-start(bf16[2,2,144,1152]{3,2,1,0:T(8,128)(2,1)S(1)} %reshape.8.refs_0_), channel_id=1, source_target_pairs={{0,1},{1,0},{2,3},{3,2},{4,5},{5,4},{6,7},{7,6},{8,9},{9,8},{10,11... | collective-permute-start | bytes 3981320 | tf_op jit(solution)/shard_map/ppermute | solution.py:342
  73.5 21.5 %all-to-all-start.2 = ((bf16[32,16,1152]{2,1,0:T(8,128)(2,1)}), bf16[32,16,1152]{2,1,0:T(8,128)(2,1)S(1)}, u32[]{:S(2)}, u32[]{:S(2)}) async-start(bf16[32,16,1152]{2,1,0:T(8,128)(2,1)} %temporal.1), calls=%async_computation.2 | async-start | bytes 2359296 | tf_op jit(solution)/shard_map/all_to_all | solution.py:377
  77.5 2.6 %collective-permute-start.3 = (bf16[2,144,1152]{2,1,0:T(8,128)(2,1)}, bf16[2,144,1152]{2,1,0:T(8,128)(2,1)}, u32[]{:S(2)}, u32[]{:S(2)}) collective-permute-start(bf16[2,144,1152]{2,1,0:T(8,128)(2,1)} %collective-permute-done.refs_1_), channel_id=1, source_target_pairs={{0,1},{1,0},{2,3},{3,2},{4,5},{5,4},{6,7},{7,6},{8,9},{9,8},{10,11... | collective-permute-start | bytes 1990664 | tf_op jit(solution)/shard_map/ppermute | solution.py:342
  78.0 3.0 %collective-permute-start.4 = (bf16[2,144,1152]{2,1,0:T(8,128)(2,1)}, bf16[2,144,1152]{2,1,0:T(8,128)(2,1)}, u32[]{:S(2)}, u32[]{:S(2)}) collective-permute-start(bf16[2,144,1152]{2,1,0:T(8,128)(2,1)} %collective-permute-done.1.refs_2_), channel_id=1, source_target_pairs={{0,1},{1,0},{2,3},{3,2},{4,5},{5,4},{6,7},{7,6},{8,9},{9,8},{10,11... | collective-permute-start | bytes 1990664 | tf_op jit(solution)/shard_map/ppermute | solution.py:342

commit v6 on v5

--- a/solution.py
+++ b/solution.py
@@ -1,3 +1,5 @@
+import functools
+
 import jax
 import jax.numpy as jnp
 import numpy as np
@@ -83,7 +85,8 @@
 def project_qkv(xn, w, copies, qkv):
     for copy, (at, size) in zip(copies, column_chunks(3 * D, CHUNK)):
         copy.wait()
-        for rows in (slice(0, S), slice(S, T)):
+        for lo in range(0, xn.shape[0], S):
+            rows = slice(lo, lo + S)
             qkv[rows, at : at + size] = mm(xn[rows, :], w[:, at : at + size]).astype(BF16)
 
 
@@ -116,10 +119,8 @@
     return wide.astype(BF16), jnp.concatenate([over_left, over_right], 1)
 
 
-def spatial_kernel(lat, mod, w_hbm, wo_hbm, out, xn, qkv, weights, ctx, w, wo, sem, wsems):
+def spatial_kernel(lat, mod, w_hbm, wo, out, xn, qkv, weights, ctx, w, wsems):
     copies = fetch(w_hbm, w, wsems)
-    last = pltpu.make_async_copy(wo_hbm, wo, sem)
-    last.start()
     shift, scale, gate = mod[0:1, :], mod[1:2, :], mod[2:3, :]
 
     def norm_rows(i, carry):
@@ -127,7 +128,7 @@
         xn[rows, :] = norm_mod(lat[rows, :].astype(F32), shift, scale)
         return carry
 
-    lax.fori_loop(0, T // 64, norm_rows, 0, unroll=2)
+    lax.fori_loop(0, T // 64, norm_rows, 0, unroll=4)
     project_qkv(xn, w, copies, qkv)
 
     def attend(g, rows):
@@ -143,7 +144,6 @@
             ctx[rows, at : at + size] = mixed.astype(BF16)
 
     halves(attend)
-    last.wait()
     for at, size in column_chunks(D, WIN):
         cols = slice(at, at + size)
         parts = []
@@ -154,7 +154,7 @@
 
 
 def temporal_kernel(
-    x, mod, w_hbm, wo_hbm, out, xn, qkv, weights, ctx, rest, over, v_t, ctx_t, wide, w, wo, sem, wsems
+    group, x, mod, w_hbm, wo_hbm, out, xn, qkv, weights, rest, over, v_t, ctx_t, wide, w, wo, wsems, sem
 ):
     copies = fetch(w_hbm, w, wsems)
     last = pltpu.make_async_copy(wo_hbm, wo, sem)
@@ -168,58 +168,48 @@
         return carry
 
     lax.fori_loop(0, 32, widen, 0, unroll=4)
-
-    def norm_rows(p, carry):
-        picked = pl.ds(p, 64, stride=8)
+    for p in range(4):
+        picked = pl.ds(4 * group + p, 64, stride=8)
         values = jnp.concatenate([wide[j, picked, :] for j in range(LANES)], axis=1)
-        rows = pl.ds(pl.multiple_of(p * 64, 64), 64)
+        rows = slice(p * 64, p * 64 + 64)
         rest[rows, :] = values.astype(BF16)
         xn[rows, :] = norm_mod(values, shift, scale)
-        return carry
-
-    lax.fori_loop(0, 8, norm_rows, 0, unroll=2)
     project_qkv(xn, w, copies, qkv)
     eye = identity(WIN)
-
-    def attend(g, rows):
-        for at, size in column_chunks(D, WIN):
-            v_t[at : at + size, :] = mm_nt(eye[:size, :size], qkv[rows, 2 * D + at : 2 * D + at + size])
-        for head in range(H):
-            at = window(head)
-            query = qkv[rows, at : at + WIN] * lane_mask(head, at, WIN)
-            weights[head], over[head] = softmax_blocks(mm_nt(qkv[rows, D + at : D + at + WIN], query))
-        for head in range(H):
-            mine = slice(head * HEAD, head * HEAD + HEAD)
-            ctx_t[mine, :] = mm(v_t[mine, :].astype(BF16), weights[head]) * over[head]
-        ctx[rows, :] = mm_nt(eye, ctx_t[...].astype(BF16)).astype(BF16)
-
-    halves(attend)
+    for at, size in column_chunks(D, WIN):
+        v_t[at : at + size, :] = mm_nt(eye[:size, :size], qkv[:, 2 * D + at : 2 * D + at + size])
+    for head in range(H):
+        at = window(head)
+        query = qkv[:, at : at + WIN] * lane_mask(head, at, WIN)
+        weights[head], over[head] = softmax_blocks(mm_nt(qkv[:, D + at : D + at + WIN], query))
+    for head in range(H):
+        mine = slice(head * HEAD, head * HEAD + HEAD)
+        ctx_t[mine, :] = mm(v_t[mine, :].astype(BF16), weights[head]) * over[head]
+    ctx = mm_nt(eye, ctx_t[...].astype(BF16)).astype(BF16)
     last.wait()
     for at, size in column_chunks(D, WIN):
         cols = slice(at, at + size)
-        for g in range(2):
-            rows = slice(g * S, g * S + S)
-            value = rest[rows, cols].astype(F32) + gate[:, cols] * mm(ctx[rows, :], wo[:, cols])
-            for p in range(4):
-                for j in range(size // 128):
-                    piece = value[p * 64 : p * 64 + 64, j * 128 : j * 128 + 128]
-                    wide[at // 128 + j, pl.ds(g * 4 + p, 64, stride=8), :] = piece
+        value = rest[:, cols].astype(F32) + gate[:, cols] * mm(ctx, wo[:, cols])
+        for p in range(4):
+            for j in range(size // 128):
+                piece = value[p * 64 : p * 64 + 64, j * 128 : j * 128 + 128]
+                wide[at // 128 + j, pl.ds(p, 64, stride=4), :] = piece
 
     def narrow(i, carry):
         rows = pl.ds(pl.multiple_of(i * 16, 16), 16)
-        out[i] = jnp.concatenate([wide[j, rows, :] for j in range(LANES)], axis=1).astype(BF16)
+        out[rows, :] = jnp.concatenate([wide[j, rows, :] for j in range(LANES)], axis=1).astype(BF16)
         return carry
 
-    lax.fori_loop(0, 32, narrow, 0, unroll=4)
-
-
-def cross_kernel(place, x, keys, values, *refs):
-    pieces, (out, w, query, weights, over, v_t, ctx_t, ctx, sems) = refs[:6], refs[6:]
-    length, core, x_lo = place[0], place[1], place[2]
+    lax.fori_loop(0, 16, narrow, 0, unroll=4)
+
+
+def assemble_kernel(place, *refs):
+    pieces, (out, sem) = refs[:6], refs[6:]
+    core, x_lo = place[1], place[2]
 
     def put(which, src, z, x):
         row = pl.multiple_of(z * (D // 2) + x * BLOCK, 16)
-        pltpu.make_async_copy(src, w.at[which, pl.ds(row, BLOCK), :], sems.at[which]).start()
+        pltpu.make_async_copy(src, out.at[which, pl.ds(row, BLOCK), :], sem).start()
 
     for own in range(2):
         which = core if own == 0 else 1 - core
@@ -229,19 +219,21 @@
             put(which, same.at[1, z], z, 2 + x_lo)
             put(which, other_first.at[z], z, 1 - x_lo)
             put(which, other_last.at[z], z, 3 - x_lo)
-
-    def whole(which):
-        pltpu.make_async_copy(w.at[which], w.at[which], sems.at[which]).wait()
-
+    pltpu.make_async_copy(out, out, sem).wait()
+
+
+def cross_kernel(group, place, *refs):
+    if group == 0:
+        first, (x, keys, values, w, out, query, weights, over, v_t, ctx_t) = None, refs
+    else:
+        first, x, keys, values, w, out, query, weights, over, v_t, ctx_t = refs
+    length = place[0]
     eye = identity(WIN)
     for at, size in column_chunks(D, WIN):
         v_t[at : at + size, :] = mm_nt(eye[:size, :size], values[:, at : at + size])
-    whole(0)
     for at, size in column_chunks(D, CHUNK):
-        for g in range(2):
-            rows = x[g * 16 : g * 16 + 16].reshape(S, D)
-            query[g * S : g * S + S, at : at + size] = mm(rows, w[0, :, at : at + size]).astype(BF16)
-    valid = lax.broadcasted_iota(jnp.int32, (SLOTS, T), 0) < length
+        query[:, at : at + size] = mm(x[...], w[0, :, at : at + size]).astype(BF16)
+    valid = lax.broadcasted_iota(jnp.int32, (SLOTS, S), 0) < length
     for head in range(H):
         at = window(head)
         masked = keys[:, at : at + WIN] * lane_mask(head, at, WIN)
@@ -251,32 +243,26 @@
     for head in range(H):
         mine = slice(head * HEAD, head * HEAD + HEAD)
         ctx_t[mine, :] = mm(v_t[mine, :].astype(BF16), weights[head]) * over[head]
-    for g in range(2):
-        rows = slice(g * S, g * S + S)
-        ctx[rows, :] = mm_nt(eye, ctx_t[:, rows].astype(BF16)).astype(BF16)
-    whole(1)
+    ctx = mm_nt(eye, ctx_t[...].astype(BF16)).astype(BF16)
     for at, size in column_chunks(D, WIN):
         cols = slice(at, at + size)
-        for g in range(2):
-            value = x[g * 16 : g * 16 + 16, :, cols].astype(F32).reshape(S, size)
-            value = value + mm(ctx[g * S : g * S + S, :], w[1, :, cols])
-            value = value.reshape(16, 2, 8, size)
-            for f in range(2):
-                out[f, g * 128 : g * 128 + 128, cols] = value[:, f].reshape(128, size).astype(BF16)
+        value = x[:, cols].astype(F32) + mm(ctx, w[1, :, cols])
+        if group == 0:
+            out[:, cols] = value.astype(BF16)
+            continue
+        mine = value.reshape(32, 8, size)
+        before = first[:, cols].astype(F32).reshape(32, 8, size)
+        low = lax.broadcasted_iota(jnp.int32, (32, 8, size), 1) < 4
+        frames = [
+            jnp.where(low, before, pltpu.roll(mine, 4, 1)),
+            jnp.where(low, pltpu.roll(before, 4, 1), mine),
+        ]
+        for f in range(2):
+            out[f, :, cols] = frames[f].reshape(S, size).astype(BF16)
 
 
 def vmem(*shape):
     return pltpu.VMEM(shape, BF16)
-
-
-def weight_scratch():
-    n = len(column_chunks(3 * D, CHUNK))
-    return [
-        vmem(D, 3 * D),
-        vmem(D, D),
-        pltpu.SemaphoreType.DMA,
-        pltpu.SemaphoreType.DMA((n,)),
-    ]
 
 
 def call(kernel, name, shape, scratch, flops, transcendentals, spaces, *args):
@@ -290,7 +276,7 @@
         in_specs=[pl.BlockSpec(memory_space=pl.ANY if space == pltpu.HBM else space) for space in spaces],
         out_specs=pl.BlockSpec(memory_space=pltpu.VMEM),
         scratch_shapes=scratch,
-        compiler_params=pltpu.CompilerParams(vmem_limit_bytes=34 * 1024 * 1024),
+        compiler_params=pltpu.CompilerParams(vmem_limit_bytes=32 * 1024 * 1024),
         cost_estimate=pl.CostEstimate(
             flops=flops, bytes_accessed=13_000_000, transcendentals=transcendentals
         ),
@@ -298,48 +284,66 @@
     )(*args)
 
 
+def chunk_semaphores():
+    return pltpu.SemaphoreType.DMA((len(column_chunks(3 * D, CHUNK)),))
+
+
 def spatial(*args):
-    scratch = [vmem(T, D), vmem(T, 3 * D), vmem(H, S, S), vmem(T, D)]
-    scratch = scratch + weight_scratch()
-    spaces = [pltpu.VMEM, pltpu.VMEM, pltpu.HBM, pltpu.HBM]
+    scratch = [vmem(T, D), vmem(T, 3 * D), vmem(H, S, S), vmem(T, D), vmem(D, 3 * D), chunk_semaphores()]
+    spaces = [pltpu.VMEM, pltpu.VMEM, pltpu.HBM, pltpu.VMEM]
     return call(spatial_kernel, "spatial", (32, 16, D), scratch, 8_000_000_000, 2_100_000, spaces, *args)
 
 
-def temporal(*args):
+def temporal(group, *args):
     scratch = [
-        vmem(T, D),
-        vmem(T, 3 * D),
+        vmem(S, D),
+        vmem(S, 3 * D),
         vmem(H, S, S),
-        vmem(T, D),
-        vmem(T, D),
+        vmem(S, D),
         pltpu.VMEM((H, 1, S), F32),
         pltpu.VMEM((D, S), F32),
         pltpu.VMEM((D, S), F32),
         pltpu.VMEM((LANES, T, 128), F32),
+        vmem(D, 3 * D),
+        vmem(D, D),
+        chunk_semaphores(),
+        pltpu.SemaphoreType.DMA,
     ]
-    scratch = scratch + weight_scratch()
     spaces = [pltpu.VMEM, pltpu.VMEM, pltpu.HBM, pltpu.HBM]
-    return call(temporal_kernel, "temporal", (32, 16, D), scratch, 8_000_000_000, 600_000, spaces, *args)
-
-
-def cross(place, x, keys, values, pieces):
+    kernel = functools.partial(temporal_kernel, group)
+    name = f"temporal_{group}"
+    return call(kernel, name, (S, D), scratch, 4_000_000_000, 300_000, spaces, *args)
+
+
+def assemble(place, pieces):
+    spaces = [pltpu.SMEM] + [pl.ANY] * len(pieces)
+    scratch = [pltpu.SemaphoreType.DMA]
+    return call(assemble_kernel, "assemble", (2, D, D), scratch, 0, 0, spaces, place, *pieces)
+
+
+def cross(group, place, first, x, keys, values, w):
     scratch = [
-        vmem(2, D, D),
-        vmem(T, D),
-        vmem(H, SLOTS, T),
-        pltpu.VMEM((H, 1, T), F32),
+        vmem(S, D),
+        vmem(H, SLOTS, S),
+        pltpu.VMEM((H, 1, S), F32),
         pltpu.VMEM((D, SLOTS), F32),
-        pltpu.VMEM((D, T), F32),
-        vmem(T, D),
-        pltpu.SemaphoreType.DMA((2,)),
+        pltpu.VMEM((D, S), F32),
     ]
-    args = (place, x, keys, values, *pieces)
-    spaces = [pltpu.SMEM] + [pltpu.VMEM] * 3 + [pl.ANY] * len(pieces)
-    return call(cross_kernel, "cross", (2, S, D), scratch, 4_000_000_000, 1_000_000, spaces, *args)
+    lead = [] if group == 0 else [first]
+    args = [place, *lead, x, keys, values, w]
+    spaces = [pltpu.SMEM] + [pltpu.VMEM] * (len(args) - 1)
+    shape = (S, D) if group == 0 else (2, S, D)
+    kernel = functools.partial(cross_kernel, group)
+    name = f"cross_{group}"
+    return call(kernel, name, shape, scratch, 2_000_000_000, 500_000, spaces, *args)
 
 
 def shift(array, axes, by, size):
     return lax.ppermute(array, axes, [(i, (i + by) % size) for i in range(size)])
+
+
+def over_seq(blocks):
+    return lax.all_to_all(blocks, SEQ, split_axis=0, concat_axis=0, tiled=True)
 
 
 def gather_even(rows):
@@ -366,22 +370,25 @@
     found = gather_even(mine)
     after_spatial = spatial(latent.reshape(T, D), modulation, w_spatial_qkv, w_spatial_out)
     found, after_spatial = lax.optimization_barrier((found, after_spatial))
-    placed = lax.all_to_all(after_spatial, SEQ, split_axis=0, concat_axis=0, tiled=True)
+    placed = over_seq(after_spatial)
     same = found.reshape(2, 2, BLOCK, D)
     same, placed = lax.optimization_barrier((same, placed))
     other_first = shift(same[0], ("x_hi", "x_lo"), 1, 4)
     other_last = shift(same[1], ("x_hi", "x_lo"), -1, 4)
-    after_temporal = temporal(placed, modulation, w_temporal_qkv, w_temporal_out)
+    halves = [temporal(0, placed, modulation, w_temporal_qkv, w_temporal_out)]
+    returned = [over_seq(halves[0].reshape(32, 8, D)).reshape(S, D)]
+    placed, halves[0] = lax.optimization_barrier((placed, halves[0]))
+    halves.append(temporal(1, placed, modulation, w_temporal_qkv, w_temporal_out))
     pieces = [same, other_first, other_last]
-    pieces, after_temporal = lax.optimization_barrier((pieces, after_temporal))
-    returned = lax.all_to_all(after_temporal, SEQ, split_axis=0, concat_axis=0, tiled=True)
+    pieces, halves[1] = lax.optimization_barrier((pieces, halves[1]))
+    returned.append(over_seq(halves[1].reshape(32, 8, D)).reshape(S, D))
     pieces = pieces + [shift(piece, "core", 1, 2) for piece in pieces]
-    place = jnp.stack(
-        [text_len[0], lax.axis_index("core"), lax.axis_index("x_lo")]
-    ).astype(jnp.int32)
+    place = jnp.stack([text_len[0], lax.axis_index("core"), lax.axis_index("x_lo")]).astype(jnp.int32)
     fill = ((0, SLOTS - text_keys.shape[0]), (0, 0))
     keys, values = jnp.pad(text_keys, fill), jnp.pad(text_values, fill)
-    return cross(place, returned, keys, values, pieces)
+    whole = assemble(place, pieces)
+    first = cross(0, place, None, returned[0], keys, values, whole)
+    return cross(1, place, first, returned[1], keys, values, whole)
 
 
 def solution(mesh):

time: 105 us -> 117 us (1.11)
  local copies, waits for them, and re-layouts: 3.66 us -> 15.1 us
  waiting for transfers between devices: 36.8 us -> 30.2 us
  starting transfers between devices: 25.2 us -> 29.9 us
  Pallas kernels: 37.1 us -> 39.6 us
    unnamed x8 -> x22, local copies, waits for them, and re-layouts: 0.02 us -> 9.55 us
    all_to_all x2 -> x3, starting transfers between devices: 7.91 us -> 12.7 us  [over_seq(): return lax.all_to_all(blocks, SEQ, split_axis=0, concat_axis=0, tiled=True)]
    all_to_all x2 -> x3, waiting for transfers between devices: 26.7 us -> 23.7 us  [over_seq(): return lax.all_to_all(blocks, SEQ, split_axis=0, concat_axis=0, tiled=True)]
    pallas_call x3 -> x6, Pallas kernels: 37.1 us -> 39.6 us  [call(): pl.pallas_call(kernel, out_shape=jax.ShapeDtypeStruct(shape, BF16), in_sp...]
    ppermute x5, waiting for transfers between devices: 2.34 us -> 0.01 us  [shift(): lax.ppermute(array, axes, [(i, (i + by) % size) for i in range(size)])]
    pad x2, local copies, waits for them, and re-layouts: 0.05 us -> 1.96 us  [body(): keys, values = (jnp.pad(text_keys, fill), jnp.pad(text_values, fill))]
    all_to_all x1, waiting for transfers between devices: 7.76 us -> 6.5 us  [gather_even(): lax.all_to_all(copies, axes, split_axis=0, concat_axis=0, tiled=True)]
  transfers between devices with their start and end apart: 8 -> 9, of which waited for: 6 -> 3; matrix products, arithmetic and copies ran while one was open for 2% -> 4% of each run, Pallas kernels for 26% -> 30%
where the time goes in v6:
time: 117 us
  Pallas kernels  39.6 us (34%)
  waiting for transfers between devices  30.2 us (26%)
  starting transfers between devices  29.9 us (26%)
  local copies, waits for them, and re-layouts  15.1 us (13%)
    pallas_call x6, Pallas kernels, call(): pl.pallas_call(kernel, out_shape=jax.ShapeDtypeStruct(shape, BF16), in_sp...  39.6 us
    all_to_all x3, waiting for transfers between devices, over_seq(): return lax.all_to_all(blocks, SEQ, split_axis=0, concat_axis=0, tiled=True)  23.7 us
    all_to_all x3, starting transfers between devices, over_seq(): return lax.all_to_all(blocks, SEQ, split_axis=0, concat_axis=0, tiled=True)  12.7 us
    unnamed x22, local copies, waits for them, and re-layouts  9.55 us
    all_to_all x1, starting transfers between devices, gather_even(): lax.all_to_all(copies, axes, split_axis=0, concat_axis=0, tiled=True)  9.25 us
    ppermute x5, starting transfers between devices, shift(): lax.ppermute(array, axes, [(i, (i + by) % size) for i in range(size)])  7.95 us
    all_to_all x1, waiting for transfers between devices, gather_even(): lax.all_to_all(copies, axes, split_axis=0, concat_axis=0, tiled=True)  6.5 us
  transfers between devices with their start and end apart: 9, of which 3 were waited for; matrix products, arithmetic and copies ran while one was open for 4% of the time, Pallas kernels for 30%

profile of v6, /device:TPU:1, one launch (start us, length us, event | category | flops | bytes accessed | tf_op | source)
XLA Modules:
  0.0 116.6 jit_solution(8700431090774119527)
XLA Ops:
  0.0 0.9 broadcast_select_fusion
  0.9 1.2 %broadcast_in_dim.2 = bf16[16,36,1152]{2,1,0:T(8,128)(2,1)} broadcast(bf16[36,1152]{1,0:T(8,128)(2,1)S(1)} %broadcast_select_fusion), dimensions={1,2} | broadcast | bytes 1410048 | tf_op jit(solution)/shard_map/broadcast_in_dim | solution.py:350
  2.1 0.0 copy-start.8
  2.1 9.2 %all-to-all-start = ((bf16[16,36,1152]{2,1,0:T(8,128)(2,1)}), bf16[16,36,1152]{2,1,0:T(8,128)(2,1)}, u32[]{:S(2)}, u32[]{:S(2)}) async-start(bf16[16,36,1152]{2,1,0:T(8,128)(2,1)} %broadcast_in_dim.2), calls=%async_computation | async-start | bytes 2949120 | tf_op jit(solution)/shard_map/all_to_all | solution.py:352
  11.4 0.0 copy-done.8
  11.4 0.0 copy-done.10
  11.4 0.0 copy-start.9
  11.4 1.3 %copy-done.9 = bf16[2,256,1152]{2,1,0:T(8,128)(2,1)S(1)} copy-done((bf16[2,256,1152]{2,1,0:T(8,128)(2,1)S(1)}, bf16[2,256,1152]{2,1,0:T(8,128)(2,1)}, u32[]{:S(2)}) %copy-start.9) | copy-done | bytes 1179672
  12.7 13.9 %spatial.1 = bf16[32,16,1152]{2,1,0:T(8,128)(2,1)} custom-call(bf16[512,1152]{1,0:T(8,128)(2,1)S(1)} %bitcast.15, f32[6,1152]{1,0:T(8,128)S(1)} %copy-done.10, bf16[1152,3456]{1,0:T(8,128)(2,1)} %w_hbm.3, bf16[1152,1152]{1,0:T(8,128)(2,1)S(1)} %copy-done.8), custom_call_target="tpu_custom_call" | custom-call | flops 8000000000 | bytes 13000000 | tf_op jit(solution)/shard_map/spatial/pallas_call | solution.py:273
  26.6 6.5 %all-to-all-done = bf16[16,36,1152]{2,1,0:T(8,128)(2,1)} async-done(((bf16[16,36,1152]{2,1,0:T(8,128)(2,1)}), bf16[16,36,1152]{2,1,0:T(8,128)(2,1)}, u32[]{:S(2)}, u32[]{:S(2)}) %all-to-all-start) | async-done | bytes 1327136 | tf_op jit(solution)/shard_map/all_to_all | solution.py:352
  33.1 3.9 %all-to-all-start.1 = ((bf16[32,16,1152]{2,1,0:T(8,128)(2,1)}), bf16[32,16,1152]{2,1,0:T(8,128)(2,1)S(1)}, u32[]{:S(2)}, u32[]{:S(2)}) async-start(bf16[32,16,1152]{2,1,0:T(8,128)(2,1)} %spatial.1), calls=%async_computation.1 | async-start | bytes 2359296 | tf_op jit(solution)/shard_map/all_to_all | solution.py:346
  37.1 2.3 %reshape.20.refs_0_ = bf16[2,2,144,1152]{3,2,1,0:T(8,128)(2,1)S(1)} reshape(bf16[16,36,1152]{2,1,0:T(8,128)(2,1)} %all-to-all-done) | data formatting | bytes 2654208 | tf_op jit(solution)/shard_map/reshape | solution.py:374
  39.3 12.8 %all-to-all-done.1.x = bf16[32,16,1152]{2,1,0:T(8,128)(2,1)S(1)} async-done(((bf16[32,16,1152]{2,1,0:T(8,128)(2,1)}), bf16[32,16,1152]{2,1,0:T(8,128)(2,1)S(1)}, u32[]{:S(2)}, u32[]{:S(2)}) %all-to-all-start.1) | async-done | bytes 1179680 | tf_op jit(solution)/shard_map/all_to_all | solution.py:346
  52.1 0.1 slice_bitcast_fusion
  52.2 1.3 %collective-permute-start = (bf16[2,144,1152]{2,1,0:T(8,128)(2,1)S(1)}, bf16[2,144,1152]{2,1,0:T(8,128)(2,1)}, u32[]{:S(2)}, u32[]{:S(2)}) collective-permute-start(bf16[2,144,1152]{2,1,0:T(8,128)(2,1)S(1)} %get-tuple-element.24), channel_id=1, source_target_pairs={{0,16},{16,32},{32,48},{48,0},{1,17},{17,33},{33,49},{49,1},{2,18}... | collective-permute-start | bytes 1990664 | tf_op jit(solution)/shard_map/ppermute | solution.py:342
  53.5 1.8 %collective-permute-start.1 = (bf16[2,144,1152]{2,1,0:T(8,128)(2,1)S(1)}, bf16[2,144,1152]{2,1,0:T(8,128)(2,1)}, u32[]{:S(2)}, u32[]{:S(2)}) collective-permute-start(bf16[2,144,1152]{2,1,0:T(8,128)(2,1)S(1)} %get-tuple-element.23), channel_id=1, source_target_pairs={{0,48},{16,0},{32,16},{48,32},{1,49},{17,1},{33,17},{49,33},{2,50}... | collective-permute-start | bytes 1990664 | tf_op jit(solution)/shard_map/ppermute | solution.py:342
  55.3 7.3 %temporal_0.1 = bf16[256,1152]{1,0:T(8,128)(2,1)S(1)} custom-call(bf16[32,16,1152]{2,1,0:T(8,128)(2,1)S(1)} %all-to-all-done.1.x, f32[6,1152]{1,0:T(8,128)S(1)} %copy-done.10, bf16[1152,3456]{1,0:T(8,128)(2,1)} %w_hbm.5, bf16[1152,1152]{1,0:T(8,128)(2,1)} %wo_hbm.3), custom_call_target="tpu_custom_call" | custom-call | flops 4000000000 | bytes 13000000 | tf_op jit(solution)/shard_map/temporal_0/pallas_call | solution.py:273
  62.6 0.0 copy-start.7
  62.6 0.8 copy-done.7
  63.4 7.3 %temporal_1.1 = bf16[256,1152]{1,0:T(8,128)(2,1)S(1)} custom-call(bf16[32,16,1152]{2,1,0:T(8,128)(2,1)S(1)} %all-to-all-done.1.x, f32[6,1152]{1,0:T(8,128)S(1)} %copy-done.10, bf16[1152,3456]{1,0:T(8,128)(2,1)} %w_hbm.5, bf16[1152,1152]{1,0:T(8,128)(2,1)} %wo_hbm.3), custom_call_target="tpu_custom_call" | custom-call | flops 4000000000 | bytes 13000000 | tf_op jit(solution)/shard_map/temporal_1/pallas_call | solution.py:273
  70.7 0.0 copy-start.4
  70.7 0.8 copy-done.4
  71.5 0.0 collective-permute-done.refs_1_
  71.5 0.0 collective-permute-done.1.refs_2_
  71.5 4.3 %collective-permute-start.2 = (bf16[2,2,144,1152]{3,2,1,0:T(8,128)(2,1)S(1)}, bf16[2,2,144,1152]{3,2,1,0:T(8,128)(2,1)S(1)}, u32[]{:S(2)}, u32[]{:S(2)}) collective-permute-start(bf16[2,2,144,1152]{3,2,1,0:T(8,128)(2,1)S(1)} %reshape.20.refs_0_), channel_id=1, source_target_pairs={{0,1},{1,0},{2,3},{3,2},{4,5},{5,4},{6,7},{7,6},{8,9},{9,8},{10,11... | collective-permute-start | bytes 3981320 | tf_op jit(solution)/shard_map/ppermute | solution.py:342
  75.8 3.9 %all-to-all-start.2 = ((bf16[32,8,1152]{2,1,0:T(8,128)(2,1)}), bf16[32,8,1152]{2,1,0:T(8,128)(2,1)S(1)}, u32[]{:S(2)}, u32[]{:S(2)}) async-start(bf16[32,8,1152]{2,1,0:T(8,128)(2,1)} %bitcast.14), calls=%async_computation.2 | async-start | bytes 1179648 | tf_op jit(solution)/shard_map/all_to_all | solution.py:346
  79.7 0.2 collective-permute-start.3
  79.9 0.4 collective-permute-start.4
  80.3 10.9 %all-to-all-done.2 = bf16[32,8,1152]{2,1,0:T(8,128)(2,1)S(1)} async-done(((bf16[32,8,1152]{2,1,0:T(8,128)(2,1)}), bf16[32,8,1152]{2,1,0:T(8,128)(2,1)S(1)}, u32[]{:S(2)}, u32[]{:S(2)}) %all-to-all-start.2) | async-done | bytes 589856 | tf_op jit(solution)/shard_map/all_to_all | solution.py:346
  91.2 0.8 copy-done.5
  92.0 4.9 %all-to-all-start.3 = ((bf16[32,8,1152]{2,1,0:T(8,128)(2,1)}), bf16[32,8,1152]{2,1,0:T(8,128)(2,1)S(1)}, u32[]{:S(2)}, u32[]{:S(2)}) async-start(bf16[32,8,1152]{2,1,0:T(8,128)(2,1)} %bitcast.12), calls=%async_computation.3 | async-start | bytes 1179648 | tf_op jit(solution)/shard_map/all_to_all | solution.py:346
  97.5 1.0 pad.7.refs_1_.refs_2_
  98.5 1.0 pad.8.refs_2_.refs_3_
  99.5 0.0 copy-start.2
  99.5 0.1 pad_add_fusion.place
  99.6 0.0 collective-permute-done.3.refs_4_
  99.6 0.0 collective-permute-done.4.refs_5_
  99.6 0.0 collective-permute-done.2.refs_3_
  99.6 2.7 %assemble.1.refs_3_.refs_4_ = bf16[2,1152,1152]{2,1,0:T(8,128)(2,1)S(1)} custom-call(s32[3]{0:T(128)S(1)} %pad_add_fusion.place, bf16[2,2,144,1152]{3,2,1,0:T(8,128)(2,1)S(1)} %reshape.20.refs_0_, bf16[2,144,1152]{2,1,0:T(8,128)(2,1)} %collective-permute-done.refs_1_, bf16[2,144,1152]{2,1,0:T(8,128)(2,1)} %collective-permute-done.1.refs_2_, ...), custom_call_target="tpu_custom_call" | custom-call | bytes 13000000 | tf_op jit(solution)/shard_map/assemble/pallas_call | solution.py:273
  102.3 0.0 copy-done.2
  102.3 0.0 copy-done.6
  102.3 3.7 %cross_0.1.refs_0_ = bf16[256,1152]{1,0:T(8,128)(2,1)S(1)} custom-call(s32[3]{0:T(128)S(1)} %pad_add_fusion.place, bf16[256,1152]{1,0:T(8,128)(2,1)S(1)} %bitcast.13, bf16[128,1152]{1,0:T(8,128)(2,1)S(1)} %pad.7.refs_1_.refs_2_, bf16[128,1152]{1,0:T(8,128)(2,1)S(1)} %pad.8.refs_2_.refs_3_, bf16[2,1152,1152]{2,1,0:T(8,128)(2,1)S(1)} %assemble.1.refs_3_.refs_4_), custom_call_target="tpu_custom_call" | custom-call | flops 2000000000 | bytes 13000000 | tf_op jit(solution)/shard_map/cross_0/pallas_call | solution.py:273
  106.0 0.0 copy-start
  106.0 2.3 %copy-done = bf16[2,1152,1152]{2,1,0:T(8,128)(2,1)} copy-done((bf16[2,1152,1152]{2,1,0:T(8,128)(2,1)}, bf16[2,1152,1152]{2,1,0:T(8,128)(2,1)S(1)}, u32[]{:S(2)}) %copy-start) | copy-done | bytes 5308440
  108.3 0.0 all-to-all-done.3
  108.3 2.5 %copy-done.1 = bf16[2,1152,1152]{2,1,0:T(8,128)(2,1)S(1)} copy-done((bf16[2,1152,1152]{2,1,0:T(8,128)(2,1)S(1)}, bf16[2,1152,1152]{2,1,0:T(8,128)(2,1)}, u32[]{:S(2)}) %copy-start.1) | copy-done | bytes 5308440
  110.9 1.0 copy-done.3
  111.8 4.8 %cross_1.1 = bf16[2,256,1152]{2,1,0:T(8,128)(2,1)} custom-call(s32[3]{0:T(128)S(1)} %pad_add_fusion.place, bf16[256,1152]{1,0:T(8,128)(2,1)S(1)} %cross_0.1.refs_0_, bf16[256,1152]{1,0:T(8,128)(2,1)S(1)} %bitcast.11, bf16[128,1152]{1,0:T(8,128)(2,1)S(1)} %pad.7.refs_1_.refs_2_, bf16[128,1152]{1,0:T(8,128)(2,1)S(1)} %copy-done.3, ...), custom_call_target="tpu_custom_call" | custom-call | flops 2000000000 | bytes 13000000 | tf_op jit(solution)/shard_map/cross_1/pallas_call | solution.py:273
  (5 shorter events, 0.0 us)
Async XLA Ops:
  2.1 9.3 %copy-start.8 = (bf16[1152,1152]{1,0:T(8,128)(2,1)S(1)}, bf16[1152,1152]{1,0:T(8,128)(2,1)}, u32[]{:S(2)}) copy-start(bf16[1152,1152]{1,0:T(8,128)(2,1)} %wo.1) | copy-start | bytes 7962628
  2.1 9.3 %copy-start.10 = (f32[6,1152]{1,0:T(8,128)S(1)}, f32[6,1152]{1,0:T(8,128)}, u32[]{:S(2)}) copy-start(f32[6,1152]{1,0:T(8,128)} %mod.5) | copy-start | bytes 82948
  2.1 31.0 %all-to-all-start = ((bf16[16,36,1152]{2,1,0:T(8,128)(2,1)}), bf16[16,36,1152]{2,1,0:T(8,128)(2,1)}, u32[]{:S(2)}, u32[]{:S(2)}) async-start(bf16[16,36,1152]{2,1,0:T(8,128)(2,1)} %broadcast_in_dim.2), calls=%async_computation | async-start | bytes 2949120 | tf_op jit(solution)/shard_map/all_to_all | solution.py:352
  11.4 1.3 %copy-start.9 = (bf16[2,256,1152]{2,1,0:T(8,128)(2,1)S(1)}, bf16[2,256,1152]{2,1,0:T(8,128)(2,1)}, u32[]{:S(2)}) copy-start(bf16[2,256,1152]{2,1,0:T(8,128)(2,1)} %param.11) | copy-start | bytes 3538948
  33.1 19.0 %all-to-all-start.1 = ((bf16[32,16,1152]{2,1,0:T(8,128)(2,1)}), bf16[32,16,1152]{2,1,0:T(8,128)(2,1)S(1)}, u32[]{:S(2)}, u32[]{:S(2)}) async-start(bf16[32,16,1152]{2,1,0:T(8,128)(2,1)} %spatial.1), calls=%async_computation.1 | async-start | bytes 2359296 | tf_op jit(solution)/shard_map/all_to_all | solution.py:346
  52.2 19.3 %collective-permute-start = (bf16[2,144,1152]{2,1,0:T(8,128)(2,1)S(1)}, bf16[2,144,1152]{2,1,0:T(8,128)(2,1)}, u32[]{:S(2)}, u32[]{:S(2)}) collective-permute-start(bf16[2,144,1152]{2,1,0:T(8,128)(2,1)S(1)} %get-tuple-element.24), channel_id=1, source_target_pairs={{0,16},{16,32},{32,48},{48,0},{1,17},{17,33},{33,49},{49,1},{2,18}... | collective-permute-start | bytes 1990664 | tf_op jit(solution)/shard_map/ppermute | solution.py:342
  53.5 18.0 %collective-permute-start.1 = (bf16[2,144,1152]{2,1,0:T(8,128)(2,1)S(1)}, bf16[2,144,1152]{2,1,0:T(8,128)(2,1)}, u32[]{:S(2)}, u32[]{:S(2)}) collective-permute-start(bf16[2,144,1152]{2,1,0:T(8,128)(2,1)S(1)} %get-tuple-element.23), channel_id=1, source_target_pairs={{0,48},{16,0},{32,16},{48,32},{1,49},{17,1},{33,17},{49,33},{2,50}... | collective-permute-start | bytes 1990664 | tf_op jit(solution)/shard_map/ppermute | solution.py:342
  62.6 0.8 copy-start.7
  70.7 0.8 copy-start.4
  71.5 28.1 %collective-permute-start.2 = (bf16[2,2,144,1152]{3,2,1,0:T(8,128)(2,1)S(1)}, bf16[2,2,144,1152]{3,2,1,0:T(8,128)(2,1)S(1)}, u32[]{:S(2)}, u32[]{:S(2)}) collective-permute-start(bf16[2,2,144,1152]{3,2,1,0:T(8,128)(2,1)S(1)} %reshape.20.refs_0_), channel_id=1, source_target_pairs={{0,1},{1,0},{2,3},{3,2},{4,5},{5,4},{6,7},{7,6},{8,9},{9,8},{10,11... | collective-permute-start | bytes 3981320 | tf_op jit(solution)/shard_map/ppermute | solution.py:342
  75.8 15.4 %all-to-all-start.2 = ((bf16[32,8,1152]{2,1,0:T(8,128)(2,1)}), bf16[32,8,1152]{2,1,0:T(8,128)(2,1)S(1)}, u32[]{:S(2)}, u32[]{:S(2)}) async-start(bf16[32,8,1152]{2,1,0:T(8,128)(2,1)} %bitcast.14), calls=%async_computation.2 | async-start | bytes 1179648 | tf_op jit(solution)/shard_map/all_to_all | solution.py:346
  79.7 19.9 %collective-permute-start.3 = (bf16[2,144,1152]{2,1,0:T(8,128)(2,1)}, bf16[2,144,1152]{2,1,0:T(8,128)(2,1)}, u32[]{:S(2)}, u32[]{:S(2)}) collective-permute-start(bf16[2,144,1152]{2,1,0:T(8,128)(2,1)} %collective-permute-done.refs_1_), channel_id=1, source_target_pairs={{0,1},{1,0},{2,3},{3,2},{4,5},{5,4},{6,7},{7,6},{8,9},{9,8},{10,11... | collective-permute-start | bytes 1990664 | tf_op jit(solution)/shard_map/ppermute | solution.py:342
  79.9 19.7 %collective-permute-start.4 = (bf16[2,144,1152]{2,1,0:T(8,128)(2,1)}, bf16[2,144,1152]{2,1,0:T(8,128)(2,1)}, u32[]{:S(2)}, u32[]{:S(2)}) collective-permute-start(bf16[2,144,1152]{2,1,0:T(8,128)(2,1)} %collective-permute-done.1.refs_2_), channel_id=1, source_target_pairs={{0,1},{1,0},{2,3},{3,2},{4,5},{5,4},{6,7},{7,6},{8,9},{9,8},{10,11... | collective-permute-start | bytes 1990664 | tf_op jit(solution)/shard_map/ppermute | solution.py:342
  91.2 0.8 copy-start.5
  92.0 16.3 %all-to-all-start.3 = ((bf16[32,8,1152]{2,1,0:T(8,128)(2,1)}), bf16[32,8,1152]{2,1,0:T(8,128)(2,1)S(1)}, u32[]{:S(2)}, u32[]{:S(2)}) async-start(bf16[32,8,1152]{2,1,0:T(8,128)(2,1)} %bitcast.12), calls=%async_computation.3 | async-start | bytes 1179648 | tf_op jit(solution)/shard_map/all_to_all | solution.py:346
  99.5 2.8 %copy-start.2 = (bf16[128,1152]{1,0:T(8,128)(2,1)}, bf16[128,1152]{1,0:T(8,128)(2,1)S(1)}, u32[]{:S(2)}) copy-start(bf16[128,1152]{1,0:T(8,128)(2,1)S(1)} %pad.8.refs_2_.refs_3_) | copy-start | bytes 884740
  99.6 2.7 %copy-start.6 = (bf16[32,8,1152]{2,1,0:T(8,128)(2,1)S(1)}, bf16[32,8,1152]{2,1,0:T(8,128)(2,1)}, u32[]{:S(2)}) copy-start(bf16[32,8,1152]{2,1,0:T(8,128)(2,1)} %copy-done.5) | copy-start | bytes 1769476
  106.0 2.4 %copy-start = (bf16[2,1152,1152]{2,1,0:T(8,128)(2,1)}, bf16[2,1152,1152]{2,1,0:T(8,128)(2,1)S(1)}, u32[]{:S(2)}) copy-start(bf16[2,1152,1152]{2,1,0:T(8,128)(2,1)S(1)} %assemble.1.refs_3_.refs_4_) | copy-start | bytes 15925252
  108.3 2.5 %copy-start.1 = (bf16[2,1152,1152]{2,1,0:T(8,128)(2,1)S(1)}, bf16[2,1152,1152]{2,1,0:T(8,128)(2,1)}, u32[]{:S(2)}) copy-start(bf16[2,1152,1152]{2,1,0:T(8,128)(2,1)} %copy-done) | copy-start | bytes 15925252
  110.9 1.0 copy-start.3

commit v7 on v5

--- a/solution.py
+++ b/solution.py
@@ -127,7 +127,7 @@
         xn[rows, :] = norm_mod(lat[rows, :].astype(F32), shift, scale)
         return carry
 
-    lax.fori_loop(0, T // 64, norm_rows, 0, unroll=2)
+    lax.fori_loop(0, T // 64, norm_rows, 0, unroll=4)
     project_qkv(xn, w, copies, qkv)
 
     def attend(g, rows):
@@ -177,7 +177,7 @@
         xn[rows, :] = norm_mod(values, shift, scale)
         return carry
 
-    lax.fori_loop(0, 8, norm_rows, 0, unroll=2)
+    lax.fori_loop(0, 8, norm_rows, 0, unroll=4)
     project_qkv(xn, w, copies, qkv)
     eye = identity(WIN)
 
@@ -214,21 +214,23 @@
 
 
 def cross_kernel(place, x, keys, values, *refs):
-    pieces, (out, w, query, weights, over, v_t, ctx_t, ctx, sems) = refs[:6], refs[6:]
-    length, core, x_lo = place[0], place[1], place[2]
-
-    def put(which, src, z, x):
-        row = pl.multiple_of(z * (D // 2) + x * BLOCK, 16)
-        pltpu.make_async_copy(src, w.at[which, pl.ds(row, BLOCK), :], sems.at[which]).start()
-
-    for own in range(2):
-        which = core if own == 0 else 1 - core
-        same, other_first, other_last = pieces[3 * own : 3 * own + 3]
-        for z in range(2):
-            put(which, same.at[0, z], z, x_lo)
-            put(which, same.at[1, z], z, 2 + x_lo)
-            put(which, other_first.at[z], z, 1 - x_lo)
-            put(which, other_last.at[z], z, 3 - x_lo)
+    pieces, (out, w, query, weights, over, v_t, ctx_t, ctx, sems) = refs[:16], refs[16:]
+    length, core, z_lo, x_lo = place[0], place[1], place[2], place[3]
+
+    def put_whole(which, source):
+        for n, src in enumerate(pieces[8 * source : 8 * source + 8]):
+            x_hi, side, z = n % 2, n // 4, n // 2 % 2
+            x = 2 * x_hi + (x_lo if side == 0 else 1 - x_lo)
+            row = (z_lo if z == 0 else 1 - z_lo) * (D // 2) + x * BLOCK
+            rows = pl.ds(pl.multiple_of(row, 16), BLOCK)
+            pltpu.make_async_copy(src, w.at[which, rows, :], sems.at[which]).start()
+
+    for one in range(2):
+
+        @pl.when(core == one)
+        def _():
+            put_whole(0, one)
+            put_whole(1, 1 - one)
 
     def whole(which):
         pltpu.make_async_copy(w.at[which], w.at[which], sems.at[which]).wait()
@@ -334,7 +336,7 @@
         pltpu.SemaphoreType.DMA((2,)),
     ]
     args = (place, x, keys, values, *pieces)
-    spaces = [pltpu.SMEM] + [pltpu.VMEM] * 3 + [pl.ANY] * len(pieces)
+    spaces = [pltpu.SMEM] + [pltpu.VMEM] * 3 + [pltpu.HBM] * len(pieces)
     return call(cross_kernel, "cross", (2, S, D), scratch, 4_000_000_000, 1_000_000, spaces, *args)
 
 
@@ -342,11 +344,18 @@
     return lax.ppermute(array, axes, [(i, (i + by) % size) for i in range(size)])
 
 
-def gather_even(rows):
-    copies = jnp.broadcast_to(rows[None], (16,) + rows.shape)
-    axes = ("x_hi", "z_lo", "y")
-    found = lax.all_to_all(copies, axes, split_axis=0, concat_axis=0, tiled=True)
-    return found
+def gather_even(first, last):
+    shape = (8,) + first.shape
+    copies = jnp.where(
+        lax.axis_index("core") == 0,
+        jnp.broadcast_to(first[None], shape),
+        jnp.broadcast_to(last[None], shape),
+    )
+    return lax.all_to_all(copies, ("x_hi", "y"), split_axis=0, concat_axis=0, tiled=True)
+
+
+def over_z(block):
+    return lax.ppermute(block, ("z_lo", "z_hi"), [(i, 3 - i) for i in range(4)])
 
 
 def body(
@@ -362,22 +371,22 @@
     text_values,
     text_len,
 ):
-    mine = jnp.where(lax.axis_index("core") == 0, cross_query, cross_out)
-    found = gather_even(mine)
+    found = gather_even(cross_query, cross_out)
     after_spatial = spatial(latent.reshape(T, D), modulation, w_spatial_qkv, w_spatial_out)
     found, after_spatial = lax.optimization_barrier((found, after_spatial))
     placed = lax.all_to_all(after_spatial, SEQ, split_axis=0, concat_axis=0, tiled=True)
-    same = found.reshape(2, 2, BLOCK, D)
-    same, placed = lax.optimization_barrier((same, placed))
-    other_first = shift(same[0], ("x_hi", "x_lo"), 1, 4)
-    other_last = shift(same[1], ("x_hi", "x_lo"), -1, 4)
+    own = [found[:4].reshape(BLOCK, D), found[4:].reshape(BLOCK, D)]
+    others = [over_z(block) for block in own]
+    own, others, placed = lax.optimization_barrier((own, others, placed))
+    sides = [shift(own[n], ("x_hi", "x_lo"), (1, -1)[n], 4) for n in range(2)]
+    far_side = shift(others[0], ("x_hi", "x_lo"), 1, 4)
     after_temporal = temporal(placed, modulation, w_temporal_qkv, w_temporal_out)
-    pieces = [same, other_first, other_last]
-    pieces, after_temporal = lax.optimization_barrier((pieces, after_temporal))
+    sides, far_side, after_temporal = lax.optimization_barrier((sides, far_side, after_temporal))
     returned = lax.all_to_all(after_temporal, SEQ, split_axis=0, concat_axis=0, tiled=True)
+    pieces = own + others + sides + [far_side, over_z(sides[1])]
     pieces = pieces + [shift(piece, "core", 1, 2) for piece in pieces]
     place = jnp.stack(
-        [text_len[0], lax.axis_index("core"), lax.axis_index("x_lo")]
+        [text_len[0], lax.axis_index("core"), lax.axis_index("z_lo"), lax.axis_index("x_lo")]
     ).astype(jnp.int32)
     fill = ((0, SLOTS - text_keys.shape[0]), (0, 0))
     keys, values = jnp.pad(text_keys, fill), jnp.pad(text_values, fill)

time: 105 us -> 101 us (0.962)
  waiting for transfers between devices: 36.8 us -> 21.2 us
  starting transfers between devices: 25.2 us -> 38.7 us
  local copies, waits for them, and re-layouts: 3.66 us -> 2.08 us
    ppermute x0 -> x3, waiting for transfers between devices: none -> 20.5 us  [over_z(): return lax.ppermute(block, ('z_lo', 'z_hi'), [(i, 3 - i) for i in range(4)])]
    all_to_all x1, waiting for transfers between devices: 14 us -> 0.01 us  [body(): lax.all_to_all(after_temporal, SEQ, split_axis=0, concat_axis=0, tiled=True)]
    all_to_all x1, waiting for transfers between devices: 12.8 us -> 0.01 us  [body(): lax.all_to_all(after_spatial, SEQ, split_axis=0, concat_axis=0, tiled=True)]
    all_to_all x1, waiting for transfers between devices: 7.76 us -> 0.01 us  [gather_even(): lax.all_to_all(copies, ('x_hi', 'y'), split_axis=0, concat_axis=0, tiled=...]
    ppermute x0 -> x3, starting transfers between devices: none -> 7.45 us  [over_z(): return lax.ppermute(block, ('z_lo', 'z_hi'), [(i, 3 - i) for i in range(4)])]
    all_to_all x1, starting transfers between devices: 3.94 us -> 8.4 us  [body(): lax.all_to_all(after_spatial, SEQ, split_axis=0, concat_axis=0, tiled=True)]
    all_to_all x1, starting transfers between devices: 3.96 us -> 6.75 us  [body(): lax.all_to_all(after_temporal, SEQ, split_axis=0, concat_axis=0, tiled=True)]
    reshape x1 -> x2, local copies, waits for them, and re-layouts: 2.25 us -> 0.14 us  [body(): own = [found[:4].reshape(BLOCK, D), found[4:].reshape(BLOCK, D)]]
  transfers between devices with their start and end apart: 8 -> 17, of which waited for: 6 -> 4; matrix products, arithmetic and copies ran while one was open for 2% -> 0% of each run, Pallas kernels for 26% -> 27%
where the time goes in v7:
time: 101 us; the launch traced here: 100 us
  starting transfers between devices  38.7 us (38%)
  Pallas kernels  36.4 us (36%)
  waiting for transfers between devices  21.2 us (21%)
  local copies, waits for them, and re-layouts  2.08 us (2%)
  between operations  1.07 us (1%)
    pallas_call x3, Pallas kernels, call(): pl.pallas_call(kernel, out_shape=jax.ShapeDtypeStruct(shape, BF16), in_sp...  36.4 us
    ppermute x3, waiting for transfers between devices, over_z(): return lax.ppermute(block, ('z_lo', 'z_hi'), [(i, 3 - i) for i in range(4)])  20.5 us
    ppermute x11, starting transfers between devices, shift(): lax.ppermute(array, axes, [(i, (i + by) % size) for i in range(size)])  8.6 us
    all_to_all x1, starting transfers between devices, body(): lax.all_to_all(after_spatial, SEQ, split_axis=0, concat_axis=0, tiled=True)  8.4 us
    all_to_all x1, starting transfers between devices, gather_even(): lax.all_to_all(copies, ('x_hi', 'y'), split_axis=0, concat_axis=0, tiled=...  7.48 us
    ppermute x3, starting transfers between devices, over_z(): return lax.ppermute(block, ('z_lo', 'z_hi'), [(i, 3 - i) for i in range(4)])  7.45 us
    all_to_all x1, starting transfers between devices, body(): lax.all_to_all(after_temporal, SEQ, split_axis=0, concat_axis=0, tiled=True)  6.75 us
  transfers between devices with their start and end apart: 17, of which 4 were waited for; matrix products, arithmetic and copies ran while one was open for 0% of the time, Pallas kernels for 27%

profile of v7, /device:TPU:1, one launch (start us, length us, event | category | flops | bytes accessed | tf_op | source)
XLA Modules:
  0.0 100.5 jit_solution(10788495852155385186)
XLA Ops:
  0.0 0.9 broadcast_select_fusion
  0.9 0.0 copy-start
  0.9 0.0 copy-start.1
  0.9 0.9 broadcast_in_dim.2
  1.9 7.5 %all-to-all-start = ((bf16[8,36,1152]{2,1,0:T(8,128)(2,1)}), bf16[8,36,1152]{2,1,0:T(8,128)(2,1)S(1)}, u32[]{:S(2)}, u32[]{:S(2)}) async-start(bf16[8,36,1152]{2,1,0:T(8,128)(2,1)} %broadcast_in_dim.2), calls=%async_computation | async-start | bytes 1474560 | tf_op jit(solution)/shard_map/all_to_all | solution.py:354
  9.4 13.9 %spatial.1 = bf16[32,16,1152]{2,1,0:T(8,128)(2,1)} custom-call(bf16[512,1152]{1,0:T(8,128)(2,1)S(1)} %bitcast.4, f32[6,1152]{1,0:T(8,128)S(1)} %copy-done.1, bf16[1152,3456]{1,0:T(8,128)(2,1)} %w_hbm.2, bf16[1152,1152]{1,0:T(8,128)(2,1)} %wo_hbm.2), custom_call_target="tpu_custom_call" | custom-call | flops 8000000000 | bytes 13000000 | tf_op jit(solution)/shard_map/spatial/pallas_call | solution.py:289
  23.3 0.0 all-to-all-done
  23.3 8.4 %all-to-all-start.1 = ((bf16[32,16,1152]{2,1,0:T(8,128)(2,1)}), bf16[32,16,1152]{2,1,0:T(8,128)(2,1)S(1)}, u32[]{:S(2)}, u32[]{:S(2)}) async-start(bf16[32,16,1152]{2,1,0:T(8,128)(2,1)} %spatial.1), calls=%async_computation.1 | async-start | bytes 2359296 | tf_op jit(solution)/shard_map/all_to_all | solution.py:377
  31.7 0.1 fusion
  31.8 0.1 reshape.13.refs_1_
  31.9 0.1 reshape.12.refs_0_
  32.0 3.4 %collective-permute-start = (bf16[144,1152]{1,0:T(8,128)(2,1)S(1)}, bf16[144,1152]{1,0:T(8,128)(2,1)S(1)}, u32[]{:S(2)}, u32[]{:S(2)}) collective-permute-start(bf16[144,1152]{1,0:T(8,128)(2,1)S(1)} %reshape.12.refs_0_), channel_id=1, source_target_pairs={{0,66},{2,64},{64,2},{66,0},{1,67},{3,65},{65,3},{67,1},{4,70},{6,... | collective-permute-start | bytes 995336 | tf_op jit(solution)/shard_map/ppermute | solution.py:358
  35.4 0.1 collective-permute-start.1
  35.5 6.2 %collective-permute-done.refs_2_ = bf16[144,1152]{1,0:T(8,128)(2,1)S(1)} collective-permute-done((bf16[144,1152]{1,0:T(8,128)(2,1)S(1)}, bf16[144,1152]{1,0:T(8,128)(2,1)S(1)}, u32[]{:S(2)}, u32[]{:S(2)}) %collective-permute-start) | collective-permute-done | bytes 331808 | tf_op jit(solution)/shard_map/ppermute | solution.py:358
  41.7 7.1 %collective-permute-done.1.refs_3_ = bf16[144,1152]{1,0:T(8,128)(2,1)S(1)} collective-permute-done((bf16[144,1152]{1,0:T(8,128)(2,1)S(1)}, bf16[144,1152]{1,0:T(8,128)(2,1)S(1)}, u32[]{:S(2)}, u32[]{:S(2)}) %collective-permute-start.1) | collective-permute-done | bytes 331808 | tf_op jit(solution)/shard_map/ppermute | solution.py:358
  48.8 0.0 all-to-all-done.1.x
  48.8 1.2 %collective-permute-start.2 = (bf16[144,1152]{1,0:T(8,128)(2,1)S(1)}, bf16[144,1152]{1,0:T(8,128)(2,1)S(1)}, u32[]{:S(2)}, u32[]{:S(2)}) collective-permute-start(bf16[144,1152]{1,0:T(8,128)(2,1)S(1)} %reshape.12.refs_0_), channel_id=1, source_target_pairs={{0,16},{16,32},{32,48},{48,0},{1,17},{17,33},{33,49},{49,1},{2,18}... | collective-permute-start | bytes 995336 | tf_op jit(solution)/shard_map/ppermute | solution.py:344
  50.0 1.5 %collective-permute-start.3 = (bf16[144,1152]{1,0:T(8,128)(2,1)S(1)}, bf16[144,1152]{1,0:T(8,128)(2,1)S(1)}, u32[]{:S(2)}, u32[]{:S(2)}) collective-permute-start(bf16[144,1152]{1,0:T(8,128)(2,1)S(1)} %reshape.13.refs_1_), channel_id=1, source_target_pairs={{0,48},{16,0},{32,16},{48,32},{1,49},{17,1},{33,17},{49,33},{2,50}... | collective-permute-start | bytes 995336 | tf_op jit(solution)/shard_map/ppermute | solution.py:344
  51.5 0.0 collective-permute-start.4
  51.5 13.5 %temporal.1 = bf16[32,16,1152]{2,1,0:T(8,128)(2,1)} custom-call(bf16[32,16,1152]{2,1,0:T(8,128)(2,1)S(1)} %all-to-all-done.1.x, f32[6,1152]{1,0:T(8,128)S(1)} %copy-done.1, bf16[1152,3456]{1,0:T(8,128)(2,1)} %w_hbm.3, bf16[1152,1152]{1,0:T(8,128)(2,1)} %wo_hbm.3), custom_call_target="tpu_custom_call" | custom-call | flops 8000000000 | bytes 13000000 | tf_op jit(solution)/shard_map/temporal/pallas_call | solution.py:289
  65.0 0.0 copy-start.4
  65.0 0.0 copy-start.5
  65.0 0.0 collective-permute-done.2.refs_4_
  65.0 0.0 collective-permute-done.3.refs_5_
  65.1 0.7 copy-done.9
  65.8 0.0 collective-permute-done.4.refs_6_
  65.8 6.8 %all-to-all-start.2 = ((bf16[32,16,1152]{2,1,0:T(8,128)(2,1)}), bf16[32,16,1152]{2,1,0:T(8,128)(2,1)S(1)}, u32[]{:S(2)}, u32[]{:S(2)}) async-start(bf16[32,16,1152]{2,1,0:T(8,128)(2,1)} %temporal.1), calls=%async_computation.2 | async-start | bytes 2359296 | tf_op jit(solution)/shard_map/all_to_all | solution.py:385
  72.5 3.6 %collective-permute-start.9 = (bf16[144,1152]{1,0:T(8,128)(2,1)S(1)}, bf16[144,1152]{1,0:T(8,128)(2,1)S(1)}, u32[]{:S(2)}, u32[]{:S(2)}) collective-permute-start(bf16[144,1152]{1,0:T(8,128)(2,1)S(1)} %collective-permute-done.1.refs_3_), channel_id=1, source_target_pairs={{0,1},{1,0},{2,3},{3,2},{4,5},{5,4},{6,7},{7,6},{8,9},{9,8},{10,11... | collective-permute-start | bytes 995336 | tf_op jit(solution)/shard_map/ppermute | solution.py:344
  76.2 0.1 collective-permute-start.6
  76.3 0.4 collective-permute-start.7
  76.7 3.9 %collective-permute-start.5 = (bf16[144,1152]{1,0:T(8,128)(2,1)}, bf16[144,1152]{1,0:T(8,128)(2,1)}, u32[]{:S(2)}, u32[]{:S(2)}) collective-permute-start(bf16[144,1152]{1,0:T(8,128)(2,1)} %copy-done.9), channel_id=1, source_target_pairs={{0,66},{2,64},{64,2},{66,0},{1,67},{3,65},{65,3},{67,1},{4,70},{6,... | collective-permute-start | bytes 995336 | tf_op jit(solution)/shard_map/ppermute | solution.py:358
  80.6 0.4 collective-permute-start.8
  81.0 0.0 collective-permute-done.9.refs_11_
  81.0 0.1 collective-permute-start.11
  81.1 0.0 collective-permute-done.6.refs_8_
  81.1 0.4 collective-permute-start.10
  81.6 0.0 collective-permute-done.7.refs_9_
  81.6 0.1 copy-done.10
  81.7 0.1 collective-permute-start.12
  81.9 7.1 %collective-permute-done.5.refs_7_ = bf16[144,1152]{1,0:T(8,128)(2,1)} collective-permute-done((bf16[144,1152]{1,0:T(8,128)(2,1)}, bf16[144,1152]{1,0:T(8,128)(2,1)}, u32[]{:S(2)}, u32[]{:S(2)}) %collective-permute-start.5) | collective-permute-done | bytes 331808 | tf_op jit(solution)/shard_map/ppermute | solution.py:358
  89.0 0.7 collective-permute-start.13
  90.4 0.1 pad_add_fusion.place
  90.5 0.0 collective-permute-done.8.refs_10_
  90.5 0.0 collective-permute-done.10.refs_12_
  90.5 0.0 collective-permute-done.11.refs_13_
  90.5 0.8 collective-permute-done.13.refs_15_
  91.3 0.0 all-to-all-done.2.x
  91.3 9.0 %cross.1 = bf16[2,256,1152]{2,1,0:T(8,128)(2,1)} custom-call(s32[4]{0:T(128)S(1)} %pad_add_fusion.place, bf16[32,16,1152]{2,1,0:T(8,128)(2,1)S(1)} %all-to-all-done.2.x, bf16[128,1152]{1,0:T(8,128)(2,1)S(1)} %pad.7.keys, bf16[128,1152]{1,0:T(8,128)(2,1)S(1)} %pad.8.values, bf16[144,1152]{1,0:T(8,128)(2,1)} %copy-done.3, bf16[144,1152]{1,0:T(8,128)(2,1)} %copy-done.2, ...), custom_call_target="tpu_custom_call" | custom-call | flops 4000000000 | bytes 13000000 | tf_op jit(solution)/shard_map/cross/pallas_call | solution.py:289
  (25 shorter events, 0.1 us)
Async XLA Ops:
  0.9 8.4 %copy-start = (bf16[2,256,1152]{2,1,0:T(8,128)(2,1)S(1)}, bf16[2,256,1152]{2,1,0:T(8,128)(2,1)}, u32[]{:S(2)}) copy-start(bf16[2,256,1152]{2,1,0:T(8,128)(2,1)} %param.11) | copy-start | bytes 3538948
  0.9 8.4 %copy-start.1 = (f32[6,1152]{1,0:T(8,128)S(1)}, f32[6,1152]{1,0:T(8,128)}, u32[]{:S(2)}) copy-start(f32[6,1152]{1,0:T(8,128)} %mod.3) | copy-start | bytes 82948
  1.9 21.4 %all-to-all-start = ((bf16[8,36,1152]{2,1,0:T(8,128)(2,1)}), bf16[8,36,1152]{2,1,0:T(8,128)(2,1)S(1)}, u32[]{:S(2)}, u32[]{:S(2)}) async-start(bf16[8,36,1152]{2,1,0:T(8,128)(2,1)} %broadcast_in_dim.2), calls=%async_computation | async-start | bytes 1474560 | tf_op jit(solution)/shard_map/all_to_all | solution.py:354
  23.3 25.5 %all-to-all-start.1 = ((bf16[32,16,1152]{2,1,0:T(8,128)(2,1)}), bf16[32,16,1152]{2,1,0:T(8,128)(2,1)S(1)}, u32[]{:S(2)}, u32[]{:S(2)}) async-start(bf16[32,16,1152]{2,1,0:T(8,128)(2,1)} %spatial.1), calls=%async_computation.1 | async-start | bytes 2359296 | tf_op jit(solution)/shard_map/all_to_all | solution.py:377
  31.9 44.4 %copy-start.2 = (bf16[144,1152]{1,0:T(8,128)(2,1)}, bf16[144,1152]{1,0:T(8,128)(2,1)S(1)}, u32[]{:S(2)}) copy-start(bf16[144,1152]{1,0:T(8,128)(2,1)S(1)} %reshape.13.refs_1_) | copy-start | bytes 995332
  31.9 44.2 %copy-start.3 = (bf16[144,1152]{1,0:T(8,128)(2,1)}, bf16[144,1152]{1,0:T(8,128)(2,1)S(1)}, u32[]{:S(2)}) copy-start(bf16[144,1152]{1,0:T(8,128)(2,1)S(1)} %reshape.12.refs_0_) | copy-start | bytes 995332
  32.0 9.8 %collective-permute-start = (bf16[144,1152]{1,0:T(8,128)(2,1)S(1)}, bf16[144,1152]{1,0:T(8,128)(2,1)S(1)}, u32[]{:S(2)}, u32[]{:S(2)}) collective-permute-start(bf16[144,1152]{1,0:T(8,128)(2,1)S(1)} %reshape.12.refs_0_), channel_id=1, source_target_pairs={{0,66},{2,64},{64,2},{66,0},{1,67},{3,65},{65,3},{67,1},{4,70},{6,... | collective-permute-start | bytes 995336 | tf_op jit(solution)/shard_map/ppermute | solution.py:358
  35.4 13.4 %collective-permute-start.1 = (bf16[144,1152]{1,0:T(8,128)(2,1)S(1)}, bf16[144,1152]{1,0:T(8,128)(2,1)S(1)}, u32[]{:S(2)}, u32[]{:S(2)}) collective-permute-start(bf16[144,1152]{1,0:T(8,128)(2,1)S(1)} %reshape.13.refs_1_), channel_id=1, source_target_pairs={{0,66},{2,64},{64,2},{66,0},{1,67},{3,65},{65,3},{67,1},{4,70},{6,... | collective-permute-start | bytes 995336 | tf_op jit(solution)/shard_map/ppermute | solution.py:358
  41.7 38.9 %copy-start.6 = (bf16[144,1152]{1,0:T(8,128)(2,1)}, bf16[144,1152]{1,0:T(8,128)(2,1)S(1)}, u32[]{:S(2)}) copy-start(bf16[144,1152]{1,0:T(8,128)(2,1)S(1)} %collective-permute-done.refs_2_) | copy-start | bytes 995332
  48.8 23.7 %copy-start.7 = (bf16[144,1152]{1,0:T(8,128)(2,1)}, bf16[144,1152]{1,0:T(8,128)(2,1)S(1)}, u32[]{:S(2)}) copy-start(bf16[144,1152]{1,0:T(8,128)(2,1)S(1)} %collective-permute-done.1.refs_3_) | copy-start | bytes 995332
  48.8 16.2 %collective-permute-start.2 = (bf16[144,1152]{1,0:T(8,128)(2,1)S(1)}, bf16[144,1152]{1,0:T(8,128)(2,1)S(1)}, u32[]{:S(2)}, u32[]{:S(2)}) collective-permute-start(bf16[144,1152]{1,0:T(8,128)(2,1)S(1)} %reshape.12.refs_0_), channel_id=1, source_target_pairs={{0,16},{16,32},{32,48},{48,0},{1,17},{17,33},{33,49},{49,1},{2,18}... | collective-permute-start | bytes 995336 | tf_op jit(solution)/shard_map/ppermute | solution.py:344
  50.0 15.0 %collective-permute-start.3 = (bf16[144,1152]{1,0:T(8,128)(2,1)S(1)}, bf16[144,1152]{1,0:T(8,128)(2,1)S(1)}, u32[]{:S(2)}, u32[]{:S(2)}) collective-permute-start(bf16[144,1152]{1,0:T(8,128)(2,1)S(1)} %reshape.13.refs_1_), channel_id=1, source_target_pairs={{0,48},{16,0},{32,16},{48,32},{1,49},{17,1},{33,17},{49,33},{2,50}... | collective-permute-start | bytes 995336 | tf_op jit(solution)/shard_map/ppermute | solution.py:344
  51.5 14.3 %collective-permute-start.4 = (bf16[144,1152]{1,0:T(8,128)(2,1)S(1)}, bf16[144,1152]{1,0:T(8,128)(2,1)}, u32[]{:S(2)}, u32[]{:S(2)}) collective-permute-start(bf16[144,1152]{1,0:T(8,128)(2,1)S(1)} %collective-permute-done.refs_2_), channel_id=1, source_target_pairs={{0,16},{16,32},{32,48},{48,0},{1,17},{17,33},{33,49},{49,1},{2,18}... | collective-permute-start | bytes 995336 | tf_op jit(solution)/shard_map/ppermute | solution.py:344
  65.0 25.3 %copy-start.4 = (bf16[120,1152]{1,0:T(8,128)(2,1)S(1)}, bf16[120,1152]{1,0:T(8,128)(2,1)}, u32[]{:S(2)}) copy-start(bf16[120,1152]{1,0:T(8,128)(2,1)} %param.19) | copy-start | bytes 829444
  65.0 25.4 %copy-start.5 = (bf16[120,1152]{1,0:T(8,128)(2,1)S(1)}, bf16[120,1152]{1,0:T(8,128)(2,1)}, u32[]{:S(2)}) copy-start(bf16[120,1152]{1,0:T(8,128)(2,1)} %param.20) | copy-start | bytes 829444
  65.0 16.1 %copy-start.8 = (bf16[144,1152]{1,0:T(8,128)(2,1)}, bf16[144,1152]{1,0:T(8,128)(2,1)S(1)}, u32[]{:S(2)}) copy-start(bf16[144,1152]{1,0:T(8,128)(2,1)S(1)} %collective-permute-done.2.refs_4_) | copy-start | bytes 995332
  65.0 0.7 copy-start.9
  65.8 25.5 %all-to-all-start.2 = ((bf16[32,16,1152]{2,1,0:T(8,128)(2,1)}), bf16[32,16,1152]{2,1,0:T(8,128)(2,1)S(1)}, u32[]{:S(2)}, u32[]{:S(2)}) async-start(bf16[32,16,1152]{2,1,0:T(8,128)(2,1)} %temporal.1), calls=%async_computation.2 | async-start | bytes 2359296 | tf_op jit(solution)/shard_map/all_to_all | solution.py:385
  72.5 8.4 %collective-permute-start.9 = (bf16[144,1152]{1,0:T(8,128)(2,1)S(1)}, bf16[144,1152]{1,0:T(8,128)(2,1)S(1)}, u32[]{:S(2)}, u32[]{:S(2)}) collective-permute-start(bf16[144,1152]{1,0:T(8,128)(2,1)S(1)} %collective-permute-done.1.refs_3_), channel_id=1, source_target_pairs={{0,1},{1,0},{2,3},{3,2},{4,5},{5,4},{6,7},{7,6},{8,9},{9,8},{10,11... | collective-permute-start | bytes 995336 | tf_op jit(solution)/shard_map/ppermute | solution.py:344
  76.2 5.0 %collective-permute-start.6 = (bf16[144,1152]{1,0:T(8,128)(2,1)S(1)}, bf16[144,1152]{1,0:T(8,128)(2,1)S(1)}, u32[]{:S(2)}, u32[]{:S(2)}) collective-permute-start(bf16[144,1152]{1,0:T(8,128)(2,1)S(1)} %reshape.12.refs_0_), channel_id=1, source_target_pairs={{0,1},{1,0},{2,3},{3,2},{4,5},{5,4},{6,7},{7,6},{8,9},{9,8},{10,11... | collective-permute-start | bytes 995336 | tf_op jit(solution)/shard_map/ppermute | solution.py:344
  76.3 5.3 %collective-permute-start.7 = (bf16[144,1152]{1,0:T(8,128)(2,1)S(1)}, bf16[144,1152]{1,0:T(8,128)(2,1)S(1)}, u32[]{:S(2)}, u32[]{:S(2)}) collective-permute-start(bf16[144,1152]{1,0:T(8,128)(2,1)S(1)} %reshape.13.refs_1_), channel_id=1, source_target_pairs={{0,1},{1,0},{2,3},{3,2},{4,5},{5,4},{6,7},{7,6},{8,9},{9,8},{10,11... | collective-permute-start | bytes 995336 | tf_op jit(solution)/shard_map/ppermute | solution.py:344
  76.7 12.3 %collective-permute-start.5 = (bf16[144,1152]{1,0:T(8,128)(2,1)}, bf16[144,1152]{1,0:T(8,128)(2,1)}, u32[]{:S(2)}, u32[]{:S(2)}) collective-permute-start(bf16[144,1152]{1,0:T(8,128)(2,1)} %copy-done.9), channel_id=1, source_target_pairs={{0,66},{2,64},{64,2},{66,0},{1,67},{3,65},{65,3},{67,1},{4,70},{6,... | collective-permute-start | bytes 995336 | tf_op jit(solution)/shard_map/ppermute | solution.py:358
  80.6 9.9 %collective-permute-start.8 = (bf16[144,1152]{1,0:T(8,128)(2,1)S(1)}, bf16[144,1152]{1,0:T(8,128)(2,1)}, u32[]{:S(2)}, u32[]{:S(2)}) collective-permute-start(bf16[144,1152]{1,0:T(8,128)(2,1)S(1)} %collective-permute-done.refs_2_), channel_id=1, source_target_pairs={{0,1},{1,0},{2,3},{3,2},{4,5},{5,4},{6,7},{7,6},{8,9},{9,8},{10,11... | collective-permute-start | bytes 995336 | tf_op jit(solution)/shard_map/ppermute | solution.py:344
  81.0 0.7 copy-start.10
  81.0 9.5 %collective-permute-start.11 = (bf16[144,1152]{1,0:T(8,128)(2,1)}, bf16[144,1152]{1,0:T(8,128)(2,1)S(1)}, u32[]{:S(2)}, u32[]{:S(2)}) collective-permute-start(bf16[144,1152]{1,0:T(8,128)(2,1)} %copy-done.9), channel_id=1, source_target_pairs={{0,1},{1,0},{2,3},{3,2},{4,5},{5,4},{6,7},{7,6},{8,9},{9,8},{10,11... | collective-permute-start | bytes 995336 | tf_op jit(solution)/shard_map/ppermute | solution.py:344
  81.1 0.7 copy-start.11
  81.1 9.3 %collective-permute-start.10 = (bf16[144,1152]{1,0:T(8,128)(2,1)S(1)}, bf16[144,1152]{1,0:T(8,128)(2,1)}, u32[]{:S(2)}, u32[]{:S(2)}) collective-permute-start(bf16[144,1152]{1,0:T(8,128)(2,1)S(1)} %collective-permute-done.2.refs_4_), channel_id=1, source_target_pairs={{0,1},{1,0},{2,3},{3,2},{4,5},{5,4},{6,7},{7,6},{8,9},{9,8},{10,11... | collective-permute-start | bytes 995336 | tf_op jit(solution)/shard_map/ppermute | solution.py:344
  81.7 7.3 %copy-start.12 = (bf16[144,1152]{1,0:T(8,128)(2,1)}, bf16[144,1152]{1,0:T(8,128)(2,1)S(1)}, u32[]{:S(2)}) copy-start(bf16[144,1152]{1,0:T(8,128)(2,1)S(1)} %collective-permute-done.7.refs_9_) | copy-start | bytes 995332
  81.7 8.8 %collective-permute-start.12 = (bf16[144,1152]{1,0:T(8,128)(2,1)}, bf16[144,1152]{1,0:T(8,128)(2,1)}, u32[]{:S(2)}, u32[]{:S(2)}) collective-permute-start(bf16[144,1152]{1,0:T(8,128)(2,1)} %collective-permute-done.4.refs_6_), channel_id=1, source_target_pairs={{0,1},{1,0},{2,3},{3,2},{4,5},{5,4},{6,7},{7,6},{8,9},{9,8},{10,11... | collective-permute-start | bytes 995336 | tf_op jit(solution)/shard_map/ppermute | solution.py:344
  89.0 2.3 %collective-permute-start.13 = (bf16[144,1152]{1,0:T(8,128)(2,1)}, bf16[144,1152]{1,0:T(8,128)(2,1)}, u32[]{:S(2)}, u32[]{:S(2)}) collective-permute-start(bf16[144,1152]{1,0:T(8,128)(2,1)} %collective-permute-done.5.refs_7_), channel_id=1, source_target_pairs={{0,1},{1,0},{2,3},{3,2},{4,5},{5,4},{6,7},{7,6},{8,9},{9,8},{10,11... | collective-permute-start | bytes 995336 | tf_op jit(solution)/shard_map/ppermute | solution.py:344
  90.5 0.8 copy-start.13

commit v8 on v7

--- a/solution.py
+++ b/solution.py
@@ -64,11 +64,8 @@
 
 
 def halves(body):
-    def step(g, carry):
-        body(g, pl.ds(pl.multiple_of(g * S, S), S))
-        return carry
-
-    lax.fori_loop(0, 2, step, 0)
+    for rows in (slice(0, S), slice(S, T)):
+        body(rows)
 
 
 def fetch(src, dst, sems):
@@ -130,7 +127,7 @@
     lax.fori_loop(0, T // 64, norm_rows, 0, unroll=4)
     project_qkv(xn, w, copies, qkv)
 
-    def attend(g, rows):
+    def attend(rows):
         for head in range(H):
             at = window(head)
             query = qkv[rows, at : at + WIN] * lane_mask(head, at, WIN)
@@ -181,7 +178,7 @@
     project_qkv(xn, w, copies, qkv)
     eye = identity(WIN)
 
-    def attend(g, rows):
+    def attend(rows):
         for at, size in column_chunks(D, WIN):
             v_t[at : at + size, :] = mm_nt(eye[:size, :size], qkv[rows, 2 * D + at : 2 * D + at + size])
         for head in range(H):
@@ -281,7 +278,7 @@
     ]
 
 
-def call(kernel, name, shape, scratch, flops, transcendentals, spaces, *args):
+def call(kernel, name, shape, scratch, mebibytes, flops, transcendentals, spaces, *args):
     args = [
         pltpu.with_memory_space_constraint(arg, space) if space == pltpu.HBM else arg
         for arg, space in zip(args, spaces)
@@ -292,7 +289,7 @@
         in_specs=[pl.BlockSpec(memory_space=pl.ANY if space == pltpu.HBM else space) for space in spaces],
         out_specs=pl.BlockSpec(memory_space=pltpu.VMEM),
         scratch_shapes=scratch,
-        compiler_params=pltpu.CompilerParams(vmem_limit_bytes=34 * 1024 * 1024),
+        compiler_params=pltpu.CompilerParams(vmem_limit_bytes=mebibytes * 1024 * 1024),
         cost_estimate=pl.CostEstimate(
             flops=flops, bytes_accessed=13_000_000, transcendentals=transcendentals
         ),
@@ -304,7 +301,7 @@
     scratch = [vmem(T, D), vmem(T, 3 * D), vmem(H, S, S), vmem(T, D)]
     scratch = scratch + weight_scratch()
     spaces = [pltpu.VMEM, pltpu.VMEM, pltpu.HBM, pltpu.HBM]
-    return call(spatial_kernel, "spatial", (32, 16, D), scratch, 8_000_000_000, 2_100_000, spaces, *args)
+    return call(spatial_kernel, "spatial", (32, 16, D), scratch, 22, 8_000_000_000, 2_100_000, spaces, *args)
 
 
 def temporal(*args):
@@ -321,7 +318,7 @@
     ]
     scratch = scratch + weight_scratch()
     spaces = [pltpu.VMEM, pltpu.VMEM, pltpu.HBM, pltpu.HBM]
-    return call(temporal_kernel, "temporal", (32, 16, D), scratch, 8_000_000_000, 600_000, spaces, *args)
+    return call(temporal_kernel, "temporal", (32, 16, D), scratch, 28, 8_000_000_000, 600_000, spaces, *args)
 
 
 def cross(place, x, keys, values, pieces):
@@ -337,7 +334,7 @@
     ]
     args = (place, x, keys, values, *pieces)
     spaces = [pltpu.SMEM] + [pltpu.VMEM] * 3 + [pltpu.HBM] * len(pieces)
-    return call(cross_kernel, "cross", (2, S, D), scratch, 4_000_000_000, 1_000_000, spaces, *args)
+    return call(cross_kernel, "cross", (2, S, D), scratch, 16, 4_000_000_000, 1_000_000, spaces, *args)
 
 
 def shift(array, axes, by, size):
@@ -352,6 +349,10 @@
         jnp.broadcast_to(last[None], shape),
     )
     return lax.all_to_all(copies, ("x_hi", "y"), split_axis=0, concat_axis=0, tiled=True)
+
+
+def over_core(block):
+    return shift(block, "core", 1, 2)
 
 
 def over_z(block):
@@ -377,14 +378,15 @@
     placed = lax.all_to_all(after_spatial, SEQ, split_axis=0, concat_axis=0, tiled=True)
     own = [found[:4].reshape(BLOCK, D), found[4:].reshape(BLOCK, D)]
     others = [over_z(block) for block in own]
-    own, others, placed = lax.optimization_barrier((own, others, placed))
+    own_swapped = [over_core(block) for block in own]
+    own, own_swapped, others, placed = lax.optimization_barrier((own, own_swapped, others, placed))
     sides = [shift(own[n], ("x_hi", "x_lo"), (1, -1)[n], 4) for n in range(2)]
     far_side = shift(others[0], ("x_hi", "x_lo"), 1, 4)
     after_temporal = temporal(placed, modulation, w_temporal_qkv, w_temporal_out)
     sides, far_side, after_temporal = lax.optimization_barrier((sides, far_side, after_temporal))
     returned = lax.all_to_all(after_temporal, SEQ, split_axis=0, concat_axis=0, tiled=True)
-    pieces = own + others + sides + [far_side, over_z(sides[1])]
-    pieces = pieces + [shift(piece, "core", 1, 2) for piece in pieces]
+    later = others + sides + [far_side, over_z(sides[1])]
+    pieces = own + later + own_swapped + [over_core(block) for block in later]
     place = jnp.stack(
         [text_len[0], lax.axis_index("core"), lax.axis_index("z_lo"), lax.axis_index("x_lo")]
     ).astype(jnp.int32)

time: 101 us -> 99.8 us (0.988)
  waiting for transfers between devices: 21.2 us -> 18.5 us
  starting transfers between devices: 38.7 us -> 40.4 us
    ppermute x3, waiting for transfers between devices: 20.5 us -> 17.7 us  [over_z(): return lax.ppermute(block, ('z_lo', 'z_hi'), [(i, 3 - i) for i in range(4)])]
    ppermute x11, starting transfers between devices: 8.6 us -> 10.3 us  [shift(): lax.ppermute(array, axes, [(i, (i + by) % size) for i in range(size)])]
where the time goes in v8:
time: 99.8 us; the launch traced here: 99.3 us
  starting transfers between devices  40.4 us (40%)
  Pallas kernels  35.7 us (36%)
  waiting for transfers between devices  18.5 us (19%)
  local copies, waits for them, and re-layouts  2.67 us (3%)
  between operations  1.1 us (1%)
    pallas_call x3, Pallas kernels, call(): pl.pallas_call(kernel, out_shape=jax.ShapeDtypeStruct(shape, BF16), in_sp...  35.7 us
    ppermute x3, waiting for transfers between devices, over_z(): return lax.ppermute(block, ('z_lo', 'z_hi'), [(i, 3 - i) for i in range(4)])  17.7 us
    ppermute x11, starting transfers between devices, shift(): lax.ppermute(array, axes, [(i, (i + by) % size) for i in range(size)])  10.3 us
    all_to_all x1, starting transfers between devices, body(): lax.all_to_all(after_spatial, SEQ, split_axis=0, concat_axis=0, tiled=True)  8.39 us
    all_to_all x1, starting transfers between devices, gather_even(): lax.all_to_all(copies, ('x_hi', 'y'), split_axis=0, concat_axis=0, tiled=...  7.48 us
    ppermute x3, starting transfers between devices, over_z(): return lax.ppermute(block, ('z_lo', 'z_hi'), [(i, 3 - i) for i in range(4)])  7.44 us
    all_to_all x1, starting transfers between devices, body(): lax.all_to_all(after_temporal, SEQ, split_axis=0, concat_axis=0, tiled=True)  6.88 us
  transfers between devices with their start and end apart: 17, of which 4 were waited for; matrix products, arithmetic and copies ran while one was open for 0% of the time, Pallas kernels for 27%

profile of v8, /device:TPU:1, one launch (start us, length us, event | category | flops | bytes accessed | tf_op | source)
XLA Modules:
  0.0 99.3 jit_solution(17336669287690034608)
XLA Ops:
  0.0 0.9 broadcast_select_fusion
  0.9 0.0 copy-start
  0.9 0.0 copy-start.1
  0.9 0.9 broadcast_in_dim.2
  1.9 7.5 %all-to-all-start = ((bf16[8,36,1152]{2,1,0:T(8,128)(2,1)}), bf16[8,36,1152]{2,1,0:T(8,128)(2,1)S(1)}, u32[]{:S(2)}, u32[]{:S(2)}) async-start(bf16[8,36,1152]{2,1,0:T(8,128)(2,1)} %broadcast_in_dim.2), calls=%async_computation | async-start | bytes 1474560 | tf_op jit(solution)/shard_map/all_to_all | solution.py:351
  9.4 13.7 %spatial.1 = bf16[32,16,1152]{2,1,0:T(8,128)(2,1)} custom-call(bf16[512,1152]{1,0:T(8,128)(2,1)S(1)} %bitcast.4, f32[6,1152]{1,0:T(8,128)S(1)} %copy-done.1, bf16[1152,3456]{1,0:T(8,128)(2,1)} %w_hbm.2, bf16[1152,1152]{1,0:T(8,128)(2,1)} %wo_hbm.2), custom_call_target="tpu_custom_call" | custom-call | flops 8000000000 | bytes 13000000 | tf_op jit(solution)/shard_map/spatial/pallas_call | solution.py:286
  23.1 0.0 all-to-all-done
  23.1 8.4 %all-to-all-start.1 = ((bf16[32,16,1152]{2,1,0:T(8,128)(2,1)}), bf16[32,16,1152]{2,1,0:T(8,128)(2,1)S(1)}, u32[]{:S(2)}, u32[]{:S(2)}) async-start(bf16[32,16,1152]{2,1,0:T(8,128)(2,1)} %spatial.1), calls=%async_computation.1 | async-start | bytes 2359296 | tf_op jit(solution)/shard_map/all_to_all | solution.py:378
  31.5 0.1 fusion
  31.6 0.1 reshape.12.refs_0_
  31.6 3.4 %collective-permute-start.2 = (bf16[144,1152]{1,0:T(8,128)(2,1)S(1)}, bf16[144,1152]{1,0:T(8,128)(2,1)S(1)}, u32[]{:S(2)}, u32[]{:S(2)}) collective-permute-start(bf16[144,1152]{1,0:T(8,128)(2,1)S(1)} %reshape.12.refs_0_), channel_id=1, source_target_pairs={{0,66},{2,64},{64,2},{66,0},{1,67},{3,65},{65,3},{67,1},{4,70},{6,... | collective-permute-start | bytes 995336 | tf_op jit(solution)/shard_map/ppermute | solution.py:359
  35.1 2.1 %collective-permute-start = (bf16[144,1152]{1,0:T(8,128)(2,1)S(1)}, bf16[144,1152]{1,0:T(8,128)(2,1)S(1)}, u32[]{:S(2)}, u32[]{:S(2)}) collective-permute-start(bf16[144,1152]{1,0:T(8,128)(2,1)S(1)} %reshape.12.refs_0_), channel_id=1, source_target_pairs={{0,1},{1,0},{2,3},{3,2},{4,5},{5,4},{6,7},{7,6},{8,9},{9,8},{10,11... | collective-permute-start | bytes 995336 | tf_op jit(solution)/shard_map/ppermute | solution.py:341
  37.2 0.1 reshape.13.refs_1_
  37.2 0.1 collective-permute-start.3
  37.3 0.1 collective-permute-start.1
  37.4 4.0 %collective-permute-done.2.refs_2_ = bf16[144,1152]{1,0:T(8,128)(2,1)S(1)} collective-permute-done((bf16[144,1152]{1,0:T(8,128)(2,1)S(1)}, bf16[144,1152]{1,0:T(8,128)(2,1)S(1)}, u32[]{:S(2)}, u32[]{:S(2)}) %collective-permute-start.2) | collective-permute-done | bytes 331808 | tf_op jit(solution)/shard_map/ppermute | solution.py:359
  41.4 0.0 collective-permute-done.refs_8_
  41.4 7.1 %collective-permute-done.3.refs_3_ = bf16[144,1152]{1,0:T(8,128)(2,1)S(1)} collective-permute-done((bf16[144,1152]{1,0:T(8,128)(2,1)S(1)}, bf16[144,1152]{1,0:T(8,128)(2,1)S(1)}, u32[]{:S(2)}, u32[]{:S(2)}) %collective-permute-start.3) | collective-permute-done | bytes 331808 | tf_op jit(solution)/shard_map/ppermute | solution.py:359
  48.5 0.0 collective-permute-done.1.refs_9_
  48.5 0.0 all-to-all-done.1.x
  48.5 1.3 %collective-permute-start.4 = (bf16[144,1152]{1,0:T(8,128)(2,1)S(1)}, bf16[144,1152]{1,0:T(8,128)(2,1)S(1)}, u32[]{:S(2)}, u32[]{:S(2)}) collective-permute-start(bf16[144,1152]{1,0:T(8,128)(2,1)S(1)} %reshape.12.refs_0_), channel_id=1, source_target_pairs={{0,16},{16,32},{32,48},{48,0},{1,17},{17,33},{33,49},{49,1},{2,18}... | collective-permute-start | bytes 995336 | tf_op jit(solution)/shard_map/ppermute | solution.py:341
  49.8 1.5 %collective-permute-start.5 = (bf16[144,1152]{1,0:T(8,128)(2,1)S(1)}, bf16[144,1152]{1,0:T(8,128)(2,1)}, u32[]{:S(2)}, u32[]{:S(2)}) collective-permute-start(bf16[144,1152]{1,0:T(8,128)(2,1)S(1)} %reshape.13.refs_1_), channel_id=1, source_target_pairs={{0,48},{16,0},{32,16},{48,32},{1,49},{17,1},{33,17},{49,33},{2,50}... | collective-permute-start | bytes 995336 | tf_op jit(solution)/shard_map/ppermute | solution.py:341
  51.3 0.0 collective-permute-start.6
  51.3 13.0 %temporal.1 = bf16[32,16,1152]{2,1,0:T(8,128)(2,1)} custom-call(bf16[32,16,1152]{2,1,0:T(8,128)(2,1)S(1)} %all-to-all-done.1.x, f32[6,1152]{1,0:T(8,128)S(1)} %copy-done.1, bf16[1152,3456]{1,0:T(8,128)(2,1)} %w_hbm.3, bf16[1152,1152]{1,0:T(8,128)(2,1)} %wo_hbm.3), custom_call_target="tpu_custom_call" | custom-call | flops 8000000000 | bytes 13000000 | tf_op jit(solution)/shard_map/temporal/pallas_call | solution.py:286
  64.4 0.0 copy-start.4
  64.4 0.0 copy-start.5
  64.4 0.0 collective-permute-done.4.refs_4_
  64.4 0.0 collective-permute-done.5.refs_5_
  64.4 0.7 copy-done.11
  65.1 0.0 collective-permute-done.6.refs_6_
  65.1 6.9 %all-to-all-start.2 = ((bf16[32,16,1152]{2,1,0:T(8,128)(2,1)}), bf16[32,16,1152]{2,1,0:T(8,128)(2,1)S(1)}, u32[]{:S(2)}, u32[]{:S(2)}) async-start(bf16[32,16,1152]{2,1,0:T(8,128)(2,1)} %temporal.1), calls=%async_computation.2 | async-start | bytes 2359296 | tf_op jit(solution)/shard_map/all_to_all | solution.py:387
  72.0 3.6 %collective-permute-start.9 = (bf16[144,1152]{1,0:T(8,128)(2,1)S(1)}, bf16[144,1152]{1,0:T(8,128)(2,1)S(1)}, u32[]{:S(2)}, u32[]{:S(2)}) collective-permute-start(bf16[144,1152]{1,0:T(8,128)(2,1)S(1)} %copy-done.9), channel_id=1, source_target_pairs={{0,1},{1,0},{2,3},{3,2},{4,5},{5,4},{6,7},{7,6},{8,9},{9,8},{10,11... | collective-permute-start | bytes 995336 | tf_op jit(solution)/shard_map/ppermute | solution.py:341
  75.6 3.9 %collective-permute-start.7 = (bf16[144,1152]{1,0:T(8,128)(2,1)}, bf16[144,1152]{1,0:T(8,128)(2,1)}, u32[]{:S(2)}, u32[]{:S(2)}) collective-permute-start(bf16[144,1152]{1,0:T(8,128)(2,1)} %collective-permute-done.5.refs_5_), channel_id=1, source_target_pairs={{0,66},{2,64},{64,2},{66,0},{1,67},{3,65},{65,3},{67,1},{4,70},{6,... | collective-permute-start | bytes 995336 | tf_op jit(solution)/shard_map/ppermute | solution.py:359
  79.5 0.4 collective-permute-start.8
  79.9 0.2 collective-permute-start.11
  80.1 0.4 collective-permute-start.10
  80.4 0.0 collective-permute-done.9.refs_11_
  80.4 0.7 copy-done.13
  81.2 0.2 collective-permute-start.12
  81.3 6.6 %collective-permute-done.7.refs_7_ = bf16[144,1152]{1,0:T(8,128)(2,1)} collective-permute-done((bf16[144,1152]{1,0:T(8,128)(2,1)}, bf16[144,1152]{1,0:T(8,128)(2,1)}, u32[]{:S(2)}, u32[]{:S(2)}) %collective-permute-start.7) | collective-permute-done | bytes 331808 | tf_op jit(solution)/shard_map/ppermute | solution.py:359
  87.9 0.7 collective-permute-start.13
  89.3 0.1 pad_add_fusion.place
  89.4 0.0 collective-permute-done.8.refs_10_
  89.4 0.0 collective-permute-done.10.refs_12_
  89.4 0.0 collective-permute-done.11.refs_13_
  89.4 0.8 collective-permute-done.13.refs_15_
  90.2 0.0 all-to-all-done.2.x
  90.2 9.0 %cross.1 = bf16[2,256,1152]{2,1,0:T(8,128)(2,1)} custom-call(s32[4]{0:T(128)S(1)} %pad_add_fusion.place, bf16[32,16,1152]{2,1,0:T(8,128)(2,1)S(1)} %all-to-all-done.2.x, bf16[128,1152]{1,0:T(8,128)(2,1)S(1)} %pad.7.keys, bf16[128,1152]{1,0:T(8,128)(2,1)S(1)} %pad.8.values, bf16[144,1152]{1,0:T(8,128)(2,1)} %copy-done.2, bf16[144,1152]{1,0:T(8,128)(2,1)} %copy-done.3, ...), custom_call_target="tpu_custom_call" | custom-call | flops 4000000000 | bytes 13000000 | tf_op jit(solution)/shard_map/cross/pallas_call | solution.py:286
  (27 shorter events, 0.1 us)
Async XLA Ops:
  0.9 8.4 %copy-start = (bf16[2,256,1152]{2,1,0:T(8,128)(2,1)S(1)}, bf16[2,256,1152]{2,1,0:T(8,128)(2,1)}, u32[]{:S(2)}) copy-start(bf16[2,256,1152]{2,1,0:T(8,128)(2,1)} %param.11) | copy-start | bytes 3538948
  0.9 8.4 %copy-start.1 = (f32[6,1152]{1,0:T(8,128)S(1)}, f32[6,1152]{1,0:T(8,128)}, u32[]{:S(2)}) copy-start(f32[6,1152]{1,0:T(8,128)} %mod.3) | copy-start | bytes 82948
  1.9 21.2 %all-to-all-start = ((bf16[8,36,1152]{2,1,0:T(8,128)(2,1)}), bf16[8,36,1152]{2,1,0:T(8,128)(2,1)S(1)}, u32[]{:S(2)}, u32[]{:S(2)}) async-start(bf16[8,36,1152]{2,1,0:T(8,128)(2,1)} %broadcast_in_dim.2), calls=%async_computation | async-start | bytes 1474560 | tf_op jit(solution)/shard_map/all_to_all | solution.py:351
  23.1 25.4 %all-to-all-start.1 = ((bf16[32,16,1152]{2,1,0:T(8,128)(2,1)}), bf16[32,16,1152]{2,1,0:T(8,128)(2,1)S(1)}, u32[]{:S(2)}, u32[]{:S(2)}) async-start(bf16[32,16,1152]{2,1,0:T(8,128)(2,1)} %spatial.1), calls=%async_computation.1 | async-start | bytes 2359296 | tf_op jit(solution)/shard_map/all_to_all | solution.py:378
  31.6 32.7 %copy-start.2 = (bf16[144,1152]{1,0:T(8,128)(2,1)}, bf16[144,1152]{1,0:T(8,128)(2,1)S(1)}, u32[]{:S(2)}) copy-start(bf16[144,1152]{1,0:T(8,128)(2,1)S(1)} %reshape.12.refs_0_) | copy-start | bytes 995332
  31.6 9.8 %collective-permute-start.2 = (bf16[144,1152]{1,0:T(8,128)(2,1)S(1)}, bf16[144,1152]{1,0:T(8,128)(2,1)S(1)}, u32[]{:S(2)}, u32[]{:S(2)}) collective-permute-start(bf16[144,1152]{1,0:T(8,128)(2,1)S(1)} %reshape.12.refs_0_), channel_id=1, source_target_pairs={{0,66},{2,64},{64,2},{66,0},{1,67},{3,65},{65,3},{67,1},{4,70},{6,... | collective-permute-start | bytes 995336 | tf_op jit(solution)/shard_map/ppermute | solution.py:359
  35.1 6.3 %collective-permute-start = (bf16[144,1152]{1,0:T(8,128)(2,1)S(1)}, bf16[144,1152]{1,0:T(8,128)(2,1)S(1)}, u32[]{:S(2)}, u32[]{:S(2)}) collective-permute-start(bf16[144,1152]{1,0:T(8,128)(2,1)S(1)} %reshape.12.refs_0_), channel_id=1, source_target_pairs={{0,1},{1,0},{2,3},{3,2},{4,5},{5,4},{6,7},{7,6},{8,9},{9,8},{10,11... | collective-permute-start | bytes 995336 | tf_op jit(solution)/shard_map/ppermute | solution.py:341
  37.2 27.1 %copy-start.3 = (bf16[144,1152]{1,0:T(8,128)(2,1)}, bf16[144,1152]{1,0:T(8,128)(2,1)S(1)}, u32[]{:S(2)}) copy-start(bf16[144,1152]{1,0:T(8,128)(2,1)S(1)} %reshape.13.refs_1_) | copy-start | bytes 995332
  37.2 11.3 %collective-permute-start.3 = (bf16[144,1152]{1,0:T(8,128)(2,1)S(1)}, bf16[144,1152]{1,0:T(8,128)(2,1)S(1)}, u32[]{:S(2)}, u32[]{:S(2)}) collective-permute-start(bf16[144,1152]{1,0:T(8,128)(2,1)S(1)} %reshape.13.refs_1_), channel_id=1, source_target_pairs={{0,66},{2,64},{64,2},{66,0},{1,67},{3,65},{65,3},{67,1},{4,70},{6,... | collective-permute-start | bytes 995336 | tf_op jit(solution)/shard_map/ppermute | solution.py:359
  37.3 11.2 %collective-permute-start.1 = (bf16[144,1152]{1,0:T(8,128)(2,1)S(1)}, bf16[144,1152]{1,0:T(8,128)(2,1)S(1)}, u32[]{:S(2)}, u32[]{:S(2)}) collective-permute-start(bf16[144,1152]{1,0:T(8,128)(2,1)S(1)} %reshape.13.refs_1_), channel_id=1, source_target_pairs={{0,1},{1,0},{2,3},{3,2},{4,5},{5,4},{6,7},{7,6},{8,9},{9,8},{10,11... | collective-permute-start | bytes 995336 | tf_op jit(solution)/shard_map/ppermute | solution.py:341
  41.4 38.2 %copy-start.6 = (bf16[144,1152]{1,0:T(8,128)(2,1)}, bf16[144,1152]{1,0:T(8,128)(2,1)S(1)}, u32[]{:S(2)}) copy-start(bf16[144,1152]{1,0:T(8,128)(2,1)S(1)} %collective-permute-done.2.refs_2_) | copy-start | bytes 995332
  41.4 9.9 %copy-start.7 = (bf16[144,1152]{1,0:T(8,128)(2,1)}, bf16[144,1152]{1,0:T(8,128)(2,1)S(1)}, u32[]{:S(2)}) copy-start(bf16[144,1152]{1,0:T(8,128)(2,1)S(1)} %collective-permute-done.refs_8_) | copy-start | bytes 995332
  48.5 2.8 %copy-start.8 = (bf16[144,1152]{1,0:T(8,128)(2,1)}, bf16[144,1152]{1,0:T(8,128)(2,1)S(1)}, u32[]{:S(2)}) copy-start(bf16[144,1152]{1,0:T(8,128)(2,1)S(1)} %collective-permute-done.3.refs_3_) | copy-start | bytes 995332
  48.5 2.8 %copy-start.10 = (bf16[144,1152]{1,0:T(8,128)(2,1)}, bf16[144,1152]{1,0:T(8,128)(2,1)S(1)}, u32[]{:S(2)}) copy-start(bf16[144,1152]{1,0:T(8,128)(2,1)S(1)} %collective-permute-done.1.refs_9_) | copy-start | bytes 995332
  48.5 15.9 %collective-permute-start.4 = (bf16[144,1152]{1,0:T(8,128)(2,1)S(1)}, bf16[144,1152]{1,0:T(8,128)(2,1)S(1)}, u32[]{:S(2)}, u32[]{:S(2)}) collective-permute-start(bf16[144,1152]{1,0:T(8,128)(2,1)S(1)} %reshape.12.refs_0_), channel_id=1, source_target_pairs={{0,16},{16,32},{32,48},{48,0},{1,17},{17,33},{33,49},{49,1},{2,18}... | collective-permute-start | bytes 995336 | tf_op jit(solution)/shard_map/ppermute | solution.py:341
  49.8 14.6 %collective-permute-start.5 = (bf16[144,1152]{1,0:T(8,128)(2,1)S(1)}, bf16[144,1152]{1,0:T(8,128)(2,1)}, u32[]{:S(2)}, u32[]{:S(2)}) collective-permute-start(bf16[144,1152]{1,0:T(8,128)(2,1)S(1)} %reshape.13.refs_1_), channel_id=1, source_target_pairs={{0,48},{16,0},{32,16},{48,32},{1,49},{17,1},{33,17},{49,33},{2,50}... | collective-permute-start | bytes 995336 | tf_op jit(solution)/shard_map/ppermute | solution.py:341
  51.3 13.8 %collective-permute-start.6 = (bf16[144,1152]{1,0:T(8,128)(2,1)S(1)}, bf16[144,1152]{1,0:T(8,128)(2,1)}, u32[]{:S(2)}, u32[]{:S(2)}) collective-permute-start(bf16[144,1152]{1,0:T(8,128)(2,1)S(1)} %collective-permute-done.2.refs_2_), channel_id=1, source_target_pairs={{0,16},{16,32},{32,48},{48,0},{1,17},{17,33},{33,49},{49,1},{2,18}... | collective-permute-start | bytes 995336 | tf_op jit(solution)/shard_map/ppermute | solution.py:341
  64.4 24.9 %copy-start.4 = (bf16[120,1152]{1,0:T(8,128)(2,1)S(1)}, bf16[120,1152]{1,0:T(8,128)(2,1)}, u32[]{:S(2)}) copy-start(bf16[120,1152]{1,0:T(8,128)(2,1)} %param.19) | copy-start | bytes 829444
  64.4 24.9 %copy-start.5 = (bf16[120,1152]{1,0:T(8,128)(2,1)S(1)}, bf16[120,1152]{1,0:T(8,128)(2,1)}, u32[]{:S(2)}) copy-start(bf16[120,1152]{1,0:T(8,128)(2,1)} %param.20) | copy-start | bytes 829444
  64.4 0.7 copy-start.11
  64.4 7.6 %copy-start.9 = (bf16[144,1152]{1,0:T(8,128)(2,1)S(1)}, bf16[144,1152]{1,0:T(8,128)(2,1)}, u32[]{:S(2)}) copy-start(bf16[144,1152]{1,0:T(8,128)(2,1)} %copy-done.8) | copy-start | bytes 995332
  65.1 14.9 %copy-start.12 = (bf16[144,1152]{1,0:T(8,128)(2,1)S(1)}, bf16[144,1152]{1,0:T(8,128)(2,1)}, u32[]{:S(2)}) copy-start(bf16[144,1152]{1,0:T(8,128)(2,1)} %copy-done.11) | copy-start | bytes 995332
  65.1 25.1 %all-to-all-start.2 = ((bf16[32,16,1152]{2,1,0:T(8,128)(2,1)}), bf16[32,16,1152]{2,1,0:T(8,128)(2,1)S(1)}, u32[]{:S(2)}, u32[]{:S(2)}) async-start(bf16[32,16,1152]{2,1,0:T(8,128)(2,1)} %temporal.1), calls=%async_computation.2 | async-start | bytes 2359296 | tf_op jit(solution)/shard_map/all_to_all | solution.py:387
  72.0 8.4 %collective-permute-start.9 = (bf16[144,1152]{1,0:T(8,128)(2,1)S(1)}, bf16[144,1152]{1,0:T(8,128)(2,1)S(1)}, u32[]{:S(2)}, u32[]{:S(2)}) collective-permute-start(bf16[144,1152]{1,0:T(8,128)(2,1)S(1)} %copy-done.9), channel_id=1, source_target_pairs={{0,1},{1,0},{2,3},{3,2},{4,5},{5,4},{6,7},{7,6},{8,9},{9,8},{10,11... | collective-permute-start | bytes 995336 | tf_op jit(solution)/shard_map/ppermute | solution.py:341
  75.6 12.3 %collective-permute-start.7 = (bf16[144,1152]{1,0:T(8,128)(2,1)}, bf16[144,1152]{1,0:T(8,128)(2,1)}, u32[]{:S(2)}, u32[]{:S(2)}) collective-permute-start(bf16[144,1152]{1,0:T(8,128)(2,1)} %collective-permute-done.5.refs_5_), channel_id=1, source_target_pairs={{0,66},{2,64},{64,2},{66,0},{1,67},{3,65},{65,3},{67,1},{4,70},{6,... | collective-permute-start | bytes 995336 | tf_op jit(solution)/shard_map/ppermute | solution.py:359
  79.5 9.9 %collective-permute-start.8 = (bf16[144,1152]{1,0:T(8,128)(2,1)S(1)}, bf16[144,1152]{1,0:T(8,128)(2,1)}, u32[]{:S(2)}, u32[]{:S(2)}) collective-permute-start(bf16[144,1152]{1,0:T(8,128)(2,1)S(1)} %collective-permute-done.2.refs_2_), channel_id=1, source_target_pairs={{0,1},{1,0},{2,3},{3,2},{4,5},{5,4},{6,7},{7,6},{8,9},{9,8},{10,11... | collective-permute-start | bytes 995336 | tf_op jit(solution)/shard_map/ppermute | solution.py:341
  79.9 9.5 %collective-permute-start.11 = (bf16[144,1152]{1,0:T(8,128)(2,1)}, bf16[144,1152]{1,0:T(8,128)(2,1)}, u32[]{:S(2)}, u32[]{:S(2)}) collective-permute-start(bf16[144,1152]{1,0:T(8,128)(2,1)} %collective-permute-done.5.refs_5_), channel_id=1, source_target_pairs={{0,1},{1,0},{2,3},{3,2},{4,5},{5,4},{6,7},{7,6},{8,9},{9,8},{10,11... | collective-permute-start | bytes 995336 | tf_op jit(solution)/shard_map/ppermute | solution.py:341
  80.1 9.4 %collective-permute-start.10 = (bf16[144,1152]{1,0:T(8,128)(2,1)S(1)}, bf16[144,1152]{1,0:T(8,128)(2,1)}, u32[]{:S(2)}, u32[]{:S(2)}) collective-permute-start(bf16[144,1152]{1,0:T(8,128)(2,1)S(1)} %copy-done.12), channel_id=1, source_target_pairs={{0,1},{1,0},{2,3},{3,2},{4,5},{5,4},{6,7},{7,6},{8,9},{9,8},{10,11... | collective-permute-start | bytes 995336 | tf_op jit(solution)/shard_map/ppermute | solution.py:341
  80.4 0.7 copy-start.13
  81.2 8.3 %collective-permute-start.12 = (bf16[144,1152]{1,0:T(8,128)(2,1)}, bf16[144,1152]{1,0:T(8,128)(2,1)S(1)}, u32[]{:S(2)}, u32[]{:S(2)}) collective-permute-start(bf16[144,1152]{1,0:T(8,128)(2,1)} %collective-permute-done.6.refs_6_), channel_id=1, source_target_pairs={{0,1},{1,0},{2,3},{3,2},{4,5},{5,4},{6,7},{7,6},{8,9},{9,8},{10,11... | collective-permute-start | bytes 995336 | tf_op jit(solution)/shard_map/ppermute | solution.py:341
  87.9 2.3 %collective-permute-start.13 = (bf16[144,1152]{1,0:T(8,128)(2,1)}, bf16[144,1152]{1,0:T(8,128)(2,1)}, u32[]{:S(2)}, u32[]{:S(2)}) collective-permute-start(bf16[144,1152]{1,0:T(8,128)(2,1)} %collective-permute-done.7.refs_7_), channel_id=1, source_target_pairs={{0,1},{1,0},{2,3},{3,2},{4,5},{5,4},{6,7},{7,6},{8,9},{9,8},{10,11... | collective-permute-start | bytes 995336 | tf_op jit(solution)/shard_map/ppermute | solution.py:341
  89.4 0.8 copy-start.14

commit v9 on v8

--- a/solution.py
+++ b/solution.py
@@ -314,7 +314,7 @@
         pltpu.VMEM((H, 1, S), F32),
         pltpu.VMEM((D, S), F32),
         pltpu.VMEM((D, S), F32),
-        pltpu.VMEM((LANES, T, 128), F32),
+        pltpu.VMEM((LANES, T + 8, 128), F32),
     ]
     scratch = scratch + weight_scratch()
     spaces = [pltpu.VMEM, pltpu.VMEM, pltpu.HBM, pltpu.HBM]

time: 99.8 us -> 99.8 us (level)
  no operation moved by 1% of the time
where the time goes in v9:
time: 99.8 us; the launch traced here: 99.3 us
  starting transfers between devices  40.4 us (40%)
  Pallas kernels  35.7 us (36%)
  waiting for transfers between devices  18.5 us (19%)
  local copies, waits for them, and re-layouts  2.67 us (3%)
  between operations  1.1 us (1%)
    pallas_call x3, Pallas kernels, call(): pl.pallas_call(kernel, out_shape=jax.ShapeDtypeStruct(shape, BF16), in_sp...  35.7 us
    ppermute x3, waiting for transfers between devices, over_z(): return lax.ppermute(block, ('z_lo', 'z_hi'), [(i, 3 - i) for i in range(4)])  17.7 us
    ppermute x11, starting transfers between devices, shift(): lax.ppermute(array, axes, [(i, (i + by) % size) for i in range(size)])  10.3 us
    all_to_all x1, starting transfers between devices, body(): lax.all_to_all(after_spatial, SEQ, split_axis=0, concat_axis=0, tiled=True)  8.39 us
    all_to_all x1, starting transfers between devices, gather_even(): lax.all_to_all(copies, ('x_hi', 'y'), split_axis=0, concat_axis=0, tiled=...  7.48 us
    ppermute x3, starting transfers between devices, over_z(): return lax.ppermute(block, ('z_lo', 'z_hi'), [(i, 3 - i) for i in range(4)])  7.44 us
    all_to_all x1, starting transfers between devices, body(): lax.all_to_all(after_temporal, SEQ, split_axis=0, concat_axis=0, tiled=True)  6.88 us
  transfers between devices with their start and end apart: 17, of which 4 were waited for; matrix products, arithmetic and copies ran while one was open for 0% of the time, Pallas kernels for 27%

profile of v9, /device:TPU:1, one launch (start us, length us, event | category | flops | bytes accessed | tf_op | source)
XLA Modules:
  0.0 99.3 jit_solution(4616774476670203142)
XLA Ops:
  0.0 0.9 broadcast_select_fusion
  0.9 0.0 copy-start
  0.9 0.0 copy-start.1
  0.9 0.9 broadcast_in_dim.2
  1.9 7.5 %all-to-all-start = ((bf16[8,36,1152]{2,1,0:T(8,128)(2,1)}), bf16[8,36,1152]{2,1,0:T(8,128)(2,1)S(1)}, u32[]{:S(2)}, u32[]{:S(2)}) async-start(bf16[8,36,1152]{2,1,0:T(8,128)(2,1)} %broadcast_in_dim.2), calls=%async_computation | async-start | bytes 1474560 | tf_op jit(solution)/shard_map/all_to_all | solution.py:351
  9.4 13.7 %spatial.1 = bf16[32,16,1152]{2,1,0:T(8,128)(2,1)} custom-call(bf16[512,1152]{1,0:T(8,128)(2,1)S(1)} %bitcast.4, f32[6,1152]{1,0:T(8,128)S(1)} %copy-done.1, bf16[1152,3456]{1,0:T(8,128)(2,1)} %w_hbm.2, bf16[1152,1152]{1,0:T(8,128)(2,1)} %wo_hbm.2), custom_call_target="tpu_custom_call" | custom-call | flops 8000000000 | bytes 13000000 | tf_op jit(solution)/shard_map/spatial/pallas_call | solution.py:286
  23.1 0.0 all-to-all-done
  23.1 8.4 %all-to-all-start.1 = ((bf16[32,16,1152]{2,1,0:T(8,128)(2,1)}), bf16[32,16,1152]{2,1,0:T(8,128)(2,1)S(1)}, u32[]{:S(2)}, u32[]{:S(2)}) async-start(bf16[32,16,1152]{2,1,0:T(8,128)(2,1)} %spatial.1), calls=%async_computation.1 | async-start | bytes 2359296 | tf_op jit(solution)/shard_map/all_to_all | solution.py:378
  31.5 0.1 fusion
  31.6 0.1 reshape.12.refs_0_
  31.6 3.4 %collective-permute-start.2 = (bf16[144,1152]{1,0:T(8,128)(2,1)S(1)}, bf16[144,1152]{1,0:T(8,128)(2,1)S(1)}, u32[]{:S(2)}, u32[]{:S(2)}) collective-permute-start(bf16[144,1152]{1,0:T(8,128)(2,1)S(1)} %reshape.12.refs_0_), channel_id=1, source_target_pairs={{0,66},{2,64},{64,2},{66,0},{1,67},{3,65},{65,3},{67,1},{4,70},{6,... | collective-permute-start | bytes 995336 | tf_op jit(solution)/shard_map/ppermute | solution.py:359
  35.1 2.1 %collective-permute-start = (bf16[144,1152]{1,0:T(8,128)(2,1)S(1)}, bf16[144,1152]{1,0:T(8,128)(2,1)S(1)}, u32[]{:S(2)}, u32[]{:S(2)}) collective-permute-start(bf16[144,1152]{1,0:T(8,128)(2,1)S(1)} %reshape.12.refs_0_), channel_id=1, source_target_pairs={{0,1},{1,0},{2,3},{3,2},{4,5},{5,4},{6,7},{7,6},{8,9},{9,8},{10,11... | collective-permute-start | bytes 995336 | tf_op jit(solution)/shard_map/ppermute | solution.py:341
  37.2 0.1 reshape.13.refs_1_
  37.2 0.1 collective-permute-start.3
  37.3 0.1 collective-permute-start.1
  37.4 4.0 %collective-permute-done.2.refs_2_ = bf16[144,1152]{1,0:T(8,128)(2,1)S(1)} collective-permute-done((bf16[144,1152]{1,0:T(8,128)(2,1)S(1)}, bf16[144,1152]{1,0:T(8,128)(2,1)S(1)}, u32[]{:S(2)}, u32[]{:S(2)}) %collective-permute-start.2) | collective-permute-done | bytes 331808 | tf_op jit(solution)/shard_map/ppermute | solution.py:359
  41.4 0.0 collective-permute-done.refs_8_
  41.4 7.1 %collective-permute-done.3.refs_3_ = bf16[144,1152]{1,0:T(8,128)(2,1)S(1)} collective-permute-done((bf16[144,1152]{1,0:T(8,128)(2,1)S(1)}, bf16[144,1152]{1,0:T(8,128)(2,1)S(1)}, u32[]{:S(2)}, u32[]{:S(2)}) %collective-permute-start.3) | collective-permute-done | bytes 331808 | tf_op jit(solution)/shard_map/ppermute | solution.py:359
  48.5 0.0 collective-permute-done.1.refs_9_
  48.5 0.0 all-to-all-done.1.x
  48.5 1.3 %collective-permute-start.4 = (bf16[144,1152]{1,0:T(8,128)(2,1)S(1)}, bf16[144,1152]{1,0:T(8,128)(2,1)S(1)}, u32[]{:S(2)}, u32[]{:S(2)}) collective-permute-start(bf16[144,1152]{1,0:T(8,128)(2,1)S(1)} %reshape.12.refs_0_), channel_id=1, source_target_pairs={{0,16},{16,32},{32,48},{48,0},{1,17},{17,33},{33,49},{49,1},{2,18}... | collective-permute-start | bytes 995336 | tf_op jit(solution)/shard_map/ppermute | solution.py:341
  49.8 1.5 %collective-permute-start.5 = (bf16[144,1152]{1,0:T(8,128)(2,1)S(1)}, bf16[144,1152]{1,0:T(8,128)(2,1)}, u32[]{:S(2)}, u32[]{:S(2)}) collective-permute-start(bf16[144,1152]{1,0:T(8,128)(2,1)S(1)} %reshape.13.refs_1_), channel_id=1, source_target_pairs={{0,48},{16,0},{32,16},{48,32},{1,49},{17,1},{33,17},{49,33},{2,50}... | collective-permute-start | bytes 995336 | tf_op jit(solution)/shard_map/ppermute | solution.py:341
  51.3 0.0 collective-permute-start.6
  51.3 13.0 %temporal.1 = bf16[32,16,1152]{2,1,0:T(8,128)(2,1)} custom-call(bf16[32,16,1152]{2,1,0:T(8,128)(2,1)S(1)} %all-to-all-done.1.x, f32[6,1152]{1,0:T(8,128)S(1)} %copy-done.1, bf16[1152,3456]{1,0:T(8,128)(2,1)} %w_hbm.3, bf16[1152,1152]{1,0:T(8,128)(2,1)} %wo_hbm.3), custom_call_target="tpu_custom_call" | custom-call | flops 8000000000 | bytes 13000000 | tf_op jit(solution)/shard_map/temporal/pallas_call | solution.py:286
  64.4 0.0 copy-start.4
  64.4 0.0 copy-start.5
  64.4 0.0 collective-permute-done.4.refs_4_
  64.4 0.0 collective-permute-done.5.refs_5_
  64.4 0.7 copy-done.11
  65.1 0.0 collective-permute-done.6.refs_6_
  65.1 6.9 %all-to-all-start.2 = ((bf16[32,16,1152]{2,1,0:T(8,128)(2,1)}), bf16[32,16,1152]{2,1,0:T(8,128)(2,1)S(1)}, u32[]{:S(2)}, u32[]{:S(2)}) async-start(bf16[32,16,1152]{2,1,0:T(8,128)(2,1)} %temporal.1), calls=%async_computation.2 | async-start | bytes 2359296 | tf_op jit(solution)/shard_map/all_to_all | solution.py:387
  72.0 3.6 %collective-permute-start.9 = (bf16[144,1152]{1,0:T(8,128)(2,1)S(1)}, bf16[144,1152]{1,0:T(8,128)(2,1)S(1)}, u32[]{:S(2)}, u32[]{:S(2)}) collective-permute-start(bf16[144,1152]{1,0:T(8,128)(2,1)S(1)} %copy-done.9), channel_id=1, source_target_pairs={{0,1},{1,0},{2,3},{3,2},{4,5},{5,4},{6,7},{7,6},{8,9},{9,8},{10,11... | collective-permute-start | bytes 995336 | tf_op jit(solution)/shard_map/ppermute | solution.py:341
  75.6 3.9 %collective-permute-start.7 = (bf16[144,1152]{1,0:T(8,128)(2,1)}, bf16[144,1152]{1,0:T(8,128)(2,1)}, u32[]{:S(2)}, u32[]{:S(2)}) collective-permute-start(bf16[144,1152]{1,0:T(8,128)(2,1)} %collective-permute-done.5.refs_5_), channel_id=1, source_target_pairs={{0,66},{2,64},{64,2},{66,0},{1,67},{3,65},{65,3},{67,1},{4,70},{6,... | collective-permute-start | bytes 995336 | tf_op jit(solution)/shard_map/ppermute | solution.py:359
  79.5 0.4 collective-permute-start.8
  79.9 0.2 collective-permute-start.11
  80.1 0.4 collective-permute-start.10
  80.4 0.0 collective-permute-done.9.refs_11_
  80.4 0.7 copy-done.13
  81.1 0.2 collective-permute-start.12
  81.3 6.6 %collective-permute-done.7.refs_7_ = bf16[144,1152]{1,0:T(8,128)(2,1)} collective-permute-done((bf16[144,1152]{1,0:T(8,128)(2,1)}, bf16[144,1152]{1,0:T(8,128)(2,1)}, u32[]{:S(2)}, u32[]{:S(2)}) %collective-permute-start.7) | collective-permute-done | bytes 331808 | tf_op jit(solution)/shard_map/ppermute | solution.py:359
  87.9 0.7 collective-permute-start.13
  89.3 0.1 pad_add_fusion.place
  89.4 0.0 collective-permute-done.8.refs_10_
  89.4 0.0 collective-permute-done.10.refs_12_
  89.4 0.0 collective-permute-done.12.refs_14_
  89.4 0.0 collective-permute-done.11.refs_13_
  89.4 0.8 collective-permute-done.13.refs_15_
  90.2 9.0 %cross.1 = bf16[2,256,1152]{2,1,0:T(8,128)(2,1)} custom-call(s32[4]{0:T(128)S(1)} %pad_add_fusion.place, bf16[32,16,1152]{2,1,0:T(8,128)(2,1)S(1)} %all-to-all-done.2.x, bf16[128,1152]{1,0:T(8,128)(2,1)S(1)} %pad.7.keys, bf16[128,1152]{1,0:T(8,128)(2,1)S(1)} %pad.8.values, bf16[144,1152]{1,0:T(8,128)(2,1)} %copy-done.2, bf16[144,1152]{1,0:T(8,128)(2,1)} %copy-done.3, ...), custom_call_target="tpu_custom_call" | custom-call | flops 4000000000 | bytes 13000000 | tf_op jit(solution)/shard_map/cross/pallas_call | solution.py:286
  (27 shorter events, 0.1 us)
Async XLA Ops:
  0.9 8.4 %copy-start = (bf16[2,256,1152]{2,1,0:T(8,128)(2,1)S(1)}, bf16[2,256,1152]{2,1,0:T(8,128)(2,1)}, u32[]{:S(2)}) copy-start(bf16[2,256,1152]{2,1,0:T(8,128)(2,1)} %param.11) | copy-start | bytes 3538948
  0.9 8.4 %copy-start.1 = (f32[6,1152]{1,0:T(8,128)S(1)}, f32[6,1152]{1,0:T(8,128)}, u32[]{:S(2)}) copy-start(f32[6,1152]{1,0:T(8,128)} %mod.3) | copy-start | bytes 82948
  1.9 21.2 %all-to-all-start = ((bf16[8,36,1152]{2,1,0:T(8,128)(2,1)}), bf16[8,36,1152]{2,1,0:T(8,128)(2,1)S(1)}, u32[]{:S(2)}, u32[]{:S(2)}) async-start(bf16[8,36,1152]{2,1,0:T(8,128)(2,1)} %broadcast_in_dim.2), calls=%async_computation | async-start | bytes 1474560 | tf_op jit(solution)/shard_map/all_to_all | solution.py:351
  23.1 25.4 %all-to-all-start.1 = ((bf16[32,16,1152]{2,1,0:T(8,128)(2,1)}), bf16[32,16,1152]{2,1,0:T(8,128)(2,1)S(1)}, u32[]{:S(2)}, u32[]{:S(2)}) async-start(bf16[32,16,1152]{2,1,0:T(8,128)(2,1)} %spatial.1), calls=%async_computation.1 | async-start | bytes 2359296 | tf_op jit(solution)/shard_map/all_to_all | solution.py:378
  31.6 32.7 %copy-start.2 = (bf16[144,1152]{1,0:T(8,128)(2,1)}, bf16[144,1152]{1,0:T(8,128)(2,1)S(1)}, u32[]{:S(2)}) copy-start(bf16[144,1152]{1,0:T(8,128)(2,1)S(1)} %reshape.12.refs_0_) | copy-start | bytes 995332
  31.6 9.8 %collective-permute-start.2 = (bf16[144,1152]{1,0:T(8,128)(2,1)S(1)}, bf16[144,1152]{1,0:T(8,128)(2,1)S(1)}, u32[]{:S(2)}, u32[]{:S(2)}) collective-permute-start(bf16[144,1152]{1,0:T(8,128)(2,1)S(1)} %reshape.12.refs_0_), channel_id=1, source_target_pairs={{0,66},{2,64},{64,2},{66,0},{1,67},{3,65},{65,3},{67,1},{4,70},{6,... | collective-permute-start | bytes 995336 | tf_op jit(solution)/shard_map/ppermute | solution.py:359
  35.1 6.3 %collective-permute-start = (bf16[144,1152]{1,0:T(8,128)(2,1)S(1)}, bf16[144,1152]{1,0:T(8,128)(2,1)S(1)}, u32[]{:S(2)}, u32[]{:S(2)}) collective-permute-start(bf16[144,1152]{1,0:T(8,128)(2,1)S(1)} %reshape.12.refs_0_), channel_id=1, source_target_pairs={{0,1},{1,0},{2,3},{3,2},{4,5},{5,4},{6,7},{7,6},{8,9},{9,8},{10,11... | collective-permute-start | bytes 995336 | tf_op jit(solution)/shard_map/ppermute | solution.py:341
  37.2 27.1 %copy-start.3 = (bf16[144,1152]{1,0:T(8,128)(2,1)}, bf16[144,1152]{1,0:T(8,128)(2,1)S(1)}, u32[]{:S(2)}) copy-start(bf16[144,1152]{1,0:T(8,128)(2,1)S(1)} %reshape.13.refs_1_) | copy-start | bytes 995332
  37.2 11.3 %collective-permute-start.3 = (bf16[144,1152]{1,0:T(8,128)(2,1)S(1)}, bf16[144,1152]{1,0:T(8,128)(2,1)S(1)}, u32[]{:S(2)}, u32[]{:S(2)}) collective-permute-start(bf16[144,1152]{1,0:T(8,128)(2,1)S(1)} %reshape.13.refs_1_), channel_id=1, source_target_pairs={{0,66},{2,64},{64,2},{66,0},{1,67},{3,65},{65,3},{67,1},{4,70},{6,... | collective-permute-start | bytes 995336 | tf_op jit(solution)/shard_map/ppermute | solution.py:359
  37.3 11.2 %collective-permute-start.1 = (bf16[144,1152]{1,0:T(8,128)(2,1)S(1)}, bf16[144,1152]{1,0:T(8,128)(2,1)S(1)}, u32[]{:S(2)}, u32[]{:S(2)}) collective-permute-start(bf16[144,1152]{1,0:T(8,128)(2,1)S(1)} %reshape.13.refs_1_), channel_id=1, source_target_pairs={{0,1},{1,0},{2,3},{3,2},{4,5},{5,4},{6,7},{7,6},{8,9},{9,8},{10,11... | collective-permute-start | bytes 995336 | tf_op jit(solution)/shard_map/ppermute | solution.py:341
  41.4 38.2 %copy-start.6 = (bf16[144,1152]{1,0:T(8,128)(2,1)}, bf16[144,1152]{1,0:T(8,128)(2,1)S(1)}, u32[]{:S(2)}) copy-start(bf16[144,1152]{1,0:T(8,128)(2,1)S(1)} %collective-permute-done.2.refs_2_) | copy-start | bytes 995332
  41.4 9.9 %copy-start.7 = (bf16[144,1152]{1,0:T(8,128)(2,1)}, bf16[144,1152]{1,0:T(8,128)(2,1)S(1)}, u32[]{:S(2)}) copy-start(bf16[144,1152]{1,0:T(8,128)(2,1)S(1)} %collective-permute-done.refs_8_) | copy-start | bytes 995332
  48.5 2.8 %copy-start.8 = (bf16[144,1152]{1,0:T(8,128)(2,1)}, bf16[144,1152]{1,0:T(8,128)(2,1)S(1)}, u32[]{:S(2)}) copy-start(bf16[144,1152]{1,0:T(8,128)(2,1)S(1)} %collective-permute-done.3.refs_3_) | copy-start | bytes 995332
  48.5 2.8 %copy-start.10 = (bf16[144,1152]{1,0:T(8,128)(2,1)}, bf16[144,1152]{1,0:T(8,128)(2,1)S(1)}, u32[]{:S(2)}) copy-start(bf16[144,1152]{1,0:T(8,128)(2,1)S(1)} %collective-permute-done.1.refs_9_) | copy-start | bytes 995332
  48.5 15.9 %collective-permute-start.4 = (bf16[144,1152]{1,0:T(8,128)(2,1)S(1)}, bf16[144,1152]{1,0:T(8,128)(2,1)S(1)}, u32[]{:S(2)}, u32[]{:S(2)}) collective-permute-start(bf16[144,1152]{1,0:T(8,128)(2,1)S(1)} %reshape.12.refs_0_), channel_id=1, source_target_pairs={{0,16},{16,32},{32,48},{48,0},{1,17},{17,33},{33,49},{49,1},{2,18}... | collective-permute-start | bytes 995336 | tf_op jit(solution)/shard_map/ppermute | solution.py:341
  49.8 14.6 %collective-permute-start.5 = (bf16[144,1152]{1,0:T(8,128)(2,1)S(1)}, bf16[144,1152]{1,0:T(8,128)(2,1)}, u32[]{:S(2)}, u32[]{:S(2)}) collective-permute-start(bf16[144,1152]{1,0:T(8,128)(2,1)S(1)} %reshape.13.refs_1_), channel_id=1, source_target_pairs={{0,48},{16,0},{32,16},{48,32},{1,49},{17,1},{33,17},{49,33},{2,50}... | collective-permute-start | bytes 995336 | tf_op jit(solution)/shard_map/ppermute | solution.py:341
  51.3 13.8 %collective-permute-start.6 = (bf16[144,1152]{1,0:T(8,128)(2,1)S(1)}, bf16[144,1152]{1,0:T(8,128)(2,1)}, u32[]{:S(2)}, u32[]{:S(2)}) collective-permute-start(bf16[144,1152]{1,0:T(8,128)(2,1)S(1)} %collective-permute-done.2.refs_2_), channel_id=1, source_target_pairs={{0,16},{16,32},{32,48},{48,0},{1,17},{17,33},{33,49},{49,1},{2,18}... | collective-permute-start | bytes 995336 | tf_op jit(solution)/shard_map/ppermute | solution.py:341
  64.4 24.9 %copy-start.4 = (bf16[120,1152]{1,0:T(8,128)(2,1)S(1)}, bf16[120,1152]{1,0:T(8,128)(2,1)}, u32[]{:S(2)}) copy-start(bf16[120,1152]{1,0:T(8,128)(2,1)} %param.19) | copy-start | bytes 829444
  64.4 24.9 %copy-start.5 = (bf16[120,1152]{1,0:T(8,128)(2,1)S(1)}, bf16[120,1152]{1,0:T(8,128)(2,1)}, u32[]{:S(2)}) copy-start(bf16[120,1152]{1,0:T(8,128)(2,1)} %param.20) | copy-start | bytes 829444
  64.4 0.7 copy-start.11
  64.4 7.6 %copy-start.9 = (bf16[144,1152]{1,0:T(8,128)(2,1)S(1)}, bf16[144,1152]{1,0:T(8,128)(2,1)}, u32[]{:S(2)}) copy-start(bf16[144,1152]{1,0:T(8,128)(2,1)} %copy-done.8) | copy-start | bytes 995332
  65.1 14.9 %copy-start.12 = (bf16[144,1152]{1,0:T(8,128)(2,1)S(1)}, bf16[144,1152]{1,0:T(8,128)(2,1)}, u32[]{:S(2)}) copy-start(bf16[144,1152]{1,0:T(8,128)(2,1)} %copy-done.11) | copy-start | bytes 995332
  65.1 25.1 %all-to-all-start.2 = ((bf16[32,16,1152]{2,1,0:T(8,128)(2,1)}), bf16[32,16,1152]{2,1,0:T(8,128)(2,1)S(1)}, u32[]{:S(2)}, u32[]{:S(2)}) async-start(bf16[32,16,1152]{2,1,0:T(8,128)(2,1)} %temporal.1), calls=%async_computation.2 | async-start | bytes 2359296 | tf_op jit(solution)/shard_map/all_to_all | solution.py:387
  72.0 8.4 %collective-permute-start.9 = (bf16[144,1152]{1,0:T(8,128)(2,1)S(1)}, bf16[144,1152]{1,0:T(8,128)(2,1)S(1)}, u32[]{:S(2)}, u32[]{:S(2)}) collective-permute-start(bf16[144,1152]{1,0:T(8,128)(2,1)S(1)} %copy-done.9), channel_id=1, source_target_pairs={{0,1},{1,0},{2,3},{3,2},{4,5},{5,4},{6,7},{7,6},{8,9},{9,8},{10,11... | collective-permute-start | bytes 995336 | tf_op jit(solution)/shard_map/ppermute | solution.py:341
  75.6 12.3 %collective-permute-start.7 = (bf16[144,1152]{1,0:T(8,128)(2,1)}, bf16[144,1152]{1,0:T(8,128)(2,1)}, u32[]{:S(2)}, u32[]{:S(2)}) collective-permute-start(bf16[144,1152]{1,0:T(8,128)(2,1)} %collective-permute-done.5.refs_5_), channel_id=1, source_target_pairs={{0,66},{2,64},{64,2},{66,0},{1,67},{3,65},{65,3},{67,1},{4,70},{6,... | collective-permute-start | bytes 995336 | tf_op jit(solution)/shard_map/ppermute | solution.py:359
  79.5 9.9 %collective-permute-start.8 = (bf16[144,1152]{1,0:T(8,128)(2,1)S(1)}, bf16[144,1152]{1,0:T(8,128)(2,1)}, u32[]{:S(2)}, u32[]{:S(2)}) collective-permute-start(bf16[144,1152]{1,0:T(8,128)(2,1)S(1)} %collective-permute-done.2.refs_2_), channel_id=1, source_target_pairs={{0,1},{1,0},{2,3},{3,2},{4,5},{5,4},{6,7},{7,6},{8,9},{9,8},{10,11... | collective-permute-start | bytes 995336 | tf_op jit(solution)/shard_map/ppermute | solution.py:341
  79.9 9.5 %collective-permute-start.11 = (bf16[144,1152]{1,0:T(8,128)(2,1)}, bf16[144,1152]{1,0:T(8,128)(2,1)}, u32[]{:S(2)}, u32[]{:S(2)}) collective-permute-start(bf16[144,1152]{1,0:T(8,128)(2,1)} %collective-permute-done.5.refs_5_), channel_id=1, source_target_pairs={{0,1},{1,0},{2,3},{3,2},{4,5},{5,4},{6,7},{7,6},{8,9},{9,8},{10,11... | collective-permute-start | bytes 995336 | tf_op jit(solution)/shard_map/ppermute | solution.py:341
  80.1 9.4 %collective-permute-start.10 = (bf16[144,1152]{1,0:T(8,128)(2,1)S(1)}, bf16[144,1152]{1,0:T(8,128)(2,1)}, u32[]{:S(2)}, u32[]{:S(2)}) collective-permute-start(bf16[144,1152]{1,0:T(8,128)(2,1)S(1)} %copy-done.12), channel_id=1, source_target_pairs={{0,1},{1,0},{2,3},{3,2},{4,5},{5,4},{6,7},{7,6},{8,9},{9,8},{10,11... | collective-permute-start | bytes 995336 | tf_op jit(solution)/shard_map/ppermute | solution.py:341
  80.4 0.7 copy-start.13
  81.1 8.3 %collective-permute-start.12 = (bf16[144,1152]{1,0:T(8,128)(2,1)}, bf16[144,1152]{1,0:T(8,128)(2,1)S(1)}, u32[]{:S(2)}, u32[]{:S(2)}) collective-permute-start(bf16[144,1152]{1,0:T(8,128)(2,1)} %collective-permute-done.6.refs_6_), channel_id=1, source_target_pairs={{0,1},{1,0},{2,3},{3,2},{4,5},{5,4},{6,7},{7,6},{8,9},{9,8},{10,11... | collective-permute-start | bytes 995336 | tf_op jit(solution)/shard_map/ppermute | solution.py:341
  87.9 2.3 %collective-permute-start.13 = (bf16[144,1152]{1,0:T(8,128)(2,1)}, bf16[144,1152]{1,0:T(8,128)(2,1)}, u32[]{:S(2)}, u32[]{:S(2)}) collective-permute-start(bf16[144,1152]{1,0:T(8,128)(2,1)} %collective-permute-done.7.refs_7_), channel_id=1, source_target_pairs={{0,1},{1,0},{2,3},{3,2},{4,5},{5,4},{6,7},{7,6},{8,9},{9,8},{10,11... | collective-permute-start | bytes 995336 | tf_op jit(solution)/shard_map/ppermute | solution.py:341
  89.4 0.8 copy-start.14

commit v10 on v9

--- a/solution.py
+++ b/solution.py
@@ -15,7 +15,7 @@
 WIN = 256
 SLOTS = 128
 BLOCK = 144
-CHUNK = 512
+CHUNK = 768
 EXP_SCALE = float(np.log2(np.e) / np.sqrt(72.0))
 F32 = jnp.float32
 BF16 = jnp.bfloat16

time: 99.8 us -> 99.4 us (level)
  no operation moved by 1% of the time
where the time goes in v10:
time: 99.4 us; the launch traced here: 98.9 us
  starting transfers between devices  40.4 us (41%)
  Pallas kernels  35.3 us (36%)
  waiting for transfers between devices  18.5 us (19%)
  local copies, waits for them, and re-layouts  2.67 us (3%)
  between operations  1.1 us (1%)
    pallas_call x3, Pallas kernels, call(): pl.pallas_call(kernel, out_shape=jax.ShapeDtypeStruct(shape, BF16), in_sp...  35.3 us
    ppermute x3, waiting for transfers between devices, over_z(): return lax.ppermute(block, ('z_lo', 'z_hi'), [(i, 3 - i) for i in range(4)])  17.7 us
    ppermute x11, starting transfers between devices, shift(): lax.ppermute(array, axes, [(i, (i + by) % size) for i in range(size)])  10.2 us
    all_to_all x1, starting transfers between devices, body(): lax.all_to_all(after_spatial, SEQ, split_axis=0, concat_axis=0, tiled=True)  8.4 us
    all_to_all x1, starting transfers between devices, gather_even(): lax.all_to_all(copies, ('x_hi', 'y'), split_axis=0, concat_axis=0, tiled=...  7.48 us
    ppermute x3, starting transfers between devices, over_z(): return lax.ppermute(block, ('z_lo', 'z_hi'), [(i, 3 - i) for i in range(4)])  7.44 us
    all_to_all x1, starting transfers between devices, body(): lax.all_to_all(after_temporal, SEQ, split_axis=0, concat_axis=0, tiled=True)  6.87 us
  transfers between devices with their start and end apart: 17, of which 4 were waited for; matrix products, arithmetic and copies ran while one was open for 0% of the time, Pallas kernels for 27%

profile of v10, /device:TPU:1, one launch (start us, length us, event | category | flops | bytes accessed | tf_op | source)
XLA Modules:
  0.0 98.9 jit_solution(2440797856292657545)
XLA Ops:
  0.0 0.9 broadcast_select_fusion
  0.9 0.0 copy-start
  0.9 0.0 copy-start.1
  0.9 0.9 broadcast_in_dim.2
  1.9 7.5 %all-to-all-start = ((bf16[8,36,1152]{2,1,0:T(8,128)(2,1)}), bf16[8,36,1152]{2,1,0:T(8,128)(2,1)S(1)}, u32[]{:S(2)}, u32[]{:S(2)}) async-start(bf16[8,36,1152]{2,1,0:T(8,128)(2,1)} %broadcast_in_dim.2), calls=%async_computation | async-start | bytes 1474560 | tf_op jit(solution)/shard_map/all_to_all | solution.py:351
  9.4 13.6 %spatial.1 = bf16[32,16,1152]{2,1,0:T(8,128)(2,1)} custom-call(bf16[512,1152]{1,0:T(8,128)(2,1)S(1)} %bitcast.4, f32[6,1152]{1,0:T(8,128)S(1)} %copy-done.1, bf16[1152,3456]{1,0:T(8,128)(2,1)} %w_hbm.2, bf16[1152,1152]{1,0:T(8,128)(2,1)} %wo_hbm.2), custom_call_target="tpu_custom_call" | custom-call | flops 8000000000 | bytes 13000000 | tf_op jit(solution)/shard_map/spatial/pallas_call | solution.py:286
  22.9 0.0 all-to-all-done
  22.9 8.4 %all-to-all-start.1 = ((bf16[32,16,1152]{2,1,0:T(8,128)(2,1)}), bf16[32,16,1152]{2,1,0:T(8,128)(2,1)S(1)}, u32[]{:S(2)}, u32[]{:S(2)}) async-start(bf16[32,16,1152]{2,1,0:T(8,128)(2,1)} %spatial.1), calls=%async_computation.1 | async-start | bytes 2359296 | tf_op jit(solution)/shard_map/all_to_all | solution.py:378
  31.3 0.1 fusion
  31.4 0.1 reshape.12.refs_0_
  31.5 3.4 %collective-permute-start.2 = (bf16[144,1152]{1,0:T(8,128)(2,1)S(1)}, bf16[144,1152]{1,0:T(8,128)(2,1)S(1)}, u32[]{:S(2)}, u32[]{:S(2)}) collective-permute-start(bf16[144,1152]{1,0:T(8,128)(2,1)S(1)} %reshape.12.refs_0_), channel_id=1, source_target_pairs={{0,66},{2,64},{64,2},{66,0},{1,67},{3,65},{65,3},{67,1},{4,70},{6,... | collective-permute-start | bytes 995336 | tf_op jit(solution)/shard_map/ppermute | solution.py:359
  34.9 2.1 %collective-permute-start = (bf16[144,1152]{1,0:T(8,128)(2,1)S(1)}, bf16[144,1152]{1,0:T(8,128)(2,1)S(1)}, u32[]{:S(2)}, u32[]{:S(2)}) collective-permute-start(bf16[144,1152]{1,0:T(8,128)(2,1)S(1)} %reshape.12.refs_0_), channel_id=1, source_target_pairs={{0,1},{1,0},{2,3},{3,2},{4,5},{5,4},{6,7},{7,6},{8,9},{9,8},{10,11... | collective-permute-start | bytes 995336 | tf_op jit(solution)/shard_map/ppermute | solution.py:341
  37.0 0.1 reshape.13.refs_1_
  37.1 0.1 collective-permute-start.3
  37.2 0.1 collective-permute-start.1
  37.3 4.0 %collective-permute-done.2.refs_2_ = bf16[144,1152]{1,0:T(8,128)(2,1)S(1)} collective-permute-done((bf16[144,1152]{1,0:T(8,128)(2,1)S(1)}, bf16[144,1152]{1,0:T(8,128)(2,1)S(1)}, u32[]{:S(2)}, u32[]{:S(2)}) %collective-permute-start.2) | collective-permute-done | bytes 331808 | tf_op jit(solution)/shard_map/ppermute | solution.py:359
  41.2 0.0 collective-permute-done.refs_8_
  41.3 7.1 %collective-permute-done.3.refs_3_ = bf16[144,1152]{1,0:T(8,128)(2,1)S(1)} collective-permute-done((bf16[144,1152]{1,0:T(8,128)(2,1)S(1)}, bf16[144,1152]{1,0:T(8,128)(2,1)S(1)}, u32[]{:S(2)}, u32[]{:S(2)}) %collective-permute-start.3) | collective-permute-done | bytes 331808 | tf_op jit(solution)/shard_map/ppermute | solution.py:359
  48.4 0.0 collective-permute-done.1.refs_9_
  48.4 0.0 all-to-all-done.1.x
  48.4 1.3 %collective-permute-start.4 = (bf16[144,1152]{1,0:T(8,128)(2,1)S(1)}, bf16[144,1152]{1,0:T(8,128)(2,1)S(1)}, u32[]{:S(2)}, u32[]{:S(2)}) collective-permute-start(bf16[144,1152]{1,0:T(8,128)(2,1)S(1)} %reshape.12.refs_0_), channel_id=1, source_target_pairs={{0,16},{16,32},{32,48},{48,0},{1,17},{17,33},{33,49},{49,1},{2,18}... | collective-permute-start | bytes 995336 | tf_op jit(solution)/shard_map/ppermute | solution.py:341
  49.6 1.5 %collective-permute-start.5 = (bf16[144,1152]{1,0:T(8,128)(2,1)S(1)}, bf16[144,1152]{1,0:T(8,128)(2,1)}, u32[]{:S(2)}, u32[]{:S(2)}) collective-permute-start(bf16[144,1152]{1,0:T(8,128)(2,1)S(1)} %reshape.13.refs_1_), channel_id=1, source_target_pairs={{0,48},{16,0},{32,16},{48,32},{1,49},{17,1},{33,17},{49,33},{2,50}... | collective-permute-start | bytes 995336 | tf_op jit(solution)/shard_map/ppermute | solution.py:341
  51.2 0.0 collective-permute-start.6
  51.2 12.7 %temporal.1 = bf16[32,16,1152]{2,1,0:T(8,128)(2,1)} custom-call(bf16[32,16,1152]{2,1,0:T(8,128)(2,1)S(1)} %all-to-all-done.1.x, f32[6,1152]{1,0:T(8,128)S(1)} %copy-done.1, bf16[1152,3456]{1,0:T(8,128)(2,1)} %w_hbm.3, bf16[1152,1152]{1,0:T(8,128)(2,1)} %wo_hbm.3), custom_call_target="tpu_custom_call" | custom-call | flops 8000000000 | bytes 13000000 | tf_op jit(solution)/shard_map/temporal/pallas_call | solution.py:286
  63.9 0.0 copy-start.4
  63.9 0.0 copy-start.5
  63.9 0.0 collective-permute-done.4.refs_4_
  64.0 0.0 collective-permute-done.5.refs_5_
  64.0 0.7 copy-done.11
  64.7 0.0 collective-permute-done.6.refs_6_
  64.7 6.9 %all-to-all-start.2 = ((bf16[32,16,1152]{2,1,0:T(8,128)(2,1)}), bf16[32,16,1152]{2,1,0:T(8,128)(2,1)S(1)}, u32[]{:S(2)}, u32[]{:S(2)}) async-start(bf16[32,16,1152]{2,1,0:T(8,128)(2,1)} %temporal.1), calls=%async_computation.2 | async-start | bytes 2359296 | tf_op jit(solution)/shard_map/all_to_all | solution.py:387
  71.6 3.6 %collective-permute-start.9 = (bf16[144,1152]{1,0:T(8,128)(2,1)S(1)}, bf16[144,1152]{1,0:T(8,128)(2,1)S(1)}, u32[]{:S(2)}, u32[]{:S(2)}) collective-permute-start(bf16[144,1152]{1,0:T(8,128)(2,1)S(1)} %copy-done.9), channel_id=1, source_target_pairs={{0,1},{1,0},{2,3},{3,2},{4,5},{5,4},{6,7},{7,6},{8,9},{9,8},{10,11... | collective-permute-start | bytes 995336 | tf_op jit(solution)/shard_map/ppermute | solution.py:341
  75.2 3.9 %collective-permute-start.7 = (bf16[144,1152]{1,0:T(8,128)(2,1)}, bf16[144,1152]{1,0:T(8,128)(2,1)}, u32[]{:S(2)}, u32[]{:S(2)}) collective-permute-start(bf16[144,1152]{1,0:T(8,128)(2,1)} %collective-permute-done.5.refs_5_), channel_id=1, source_target_pairs={{0,66},{2,64},{64,2},{66,0},{1,67},{3,65},{65,3},{67,1},{4,70},{6,... | collective-permute-start | bytes 995336 | tf_op jit(solution)/shard_map/ppermute | solution.py:359
  79.1 0.4 collective-permute-start.8
  79.4 0.2 collective-permute-start.11
  79.6 0.4 collective-permute-start.10
  80.0 0.0 collective-permute-done.9.refs_11_
  80.0 0.7 copy-done.13
  80.7 0.2 collective-permute-start.12
  80.8 6.6 %collective-permute-done.7.refs_7_ = bf16[144,1152]{1,0:T(8,128)(2,1)} collective-permute-done((bf16[144,1152]{1,0:T(8,128)(2,1)}, bf16[144,1152]{1,0:T(8,128)(2,1)}, u32[]{:S(2)}, u32[]{:S(2)}) %collective-permute-start.7) | collective-permute-done | bytes 331808 | tf_op jit(solution)/shard_map/ppermute | solution.py:359
  87.5 0.7 collective-permute-start.13
  88.9 0.1 pad_add_fusion.place
  88.9 0.0 collective-permute-done.8.refs_10_
  89.0 0.0 collective-permute-done.10.refs_12_
  89.0 0.0 collective-permute-done.11.refs_13_
  89.0 0.8 collective-permute-done.13.refs_15_
  89.7 0.0 all-to-all-done.2.x
  89.7 9.0 %cross.1 = bf16[2,256,1152]{2,1,0:T(8,128)(2,1)} custom-call(s32[4]{0:T(128)S(1)} %pad_add_fusion.place, bf16[32,16,1152]{2,1,0:T(8,128)(2,1)S(1)} %all-to-all-done.2.x, bf16[128,1152]{1,0:T(8,128)(2,1)S(1)} %pad.7.keys, bf16[128,1152]{1,0:T(8,128)(2,1)S(1)} %pad.8.values, bf16[144,1152]{1,0:T(8,128)(2,1)} %copy-done.2, bf16[144,1152]{1,0:T(8,128)(2,1)} %copy-done.3, ...), custom_call_target="tpu_custom_call" | custom-call | flops 4000000000 | bytes 13000000 | tf_op jit(solution)/shard_map/cross/pallas_call | solution.py:286
  (27 shorter events, 0.1 us)
Async XLA Ops:
  0.9 8.4 %copy-start = (bf16[2,256,1152]{2,1,0:T(8,128)(2,1)S(1)}, bf16[2,256,1152]{2,1,0:T(8,128)(2,1)}, u32[]{:S(2)}) copy-start(bf16[2,256,1152]{2,1,0:T(8,128)(2,1)} %param.11) | copy-start | bytes 3538948
  0.9 8.4 %copy-start.1 = (f32[6,1152]{1,0:T(8,128)S(1)}, f32[6,1152]{1,0:T(8,128)}, u32[]{:S(2)}) copy-start(f32[6,1152]{1,0:T(8,128)} %mod.3) | copy-start | bytes 82948
  1.9 21.1 %all-to-all-start = ((bf16[8,36,1152]{2,1,0:T(8,128)(2,1)}), bf16[8,36,1152]{2,1,0:T(8,128)(2,1)S(1)}, u32[]{:S(2)}, u32[]{:S(2)}) async-start(bf16[8,36,1152]{2,1,0:T(8,128)(2,1)} %broadcast_in_dim.2), calls=%async_computation | async-start | bytes 1474560 | tf_op jit(solution)/shard_map/all_to_all | solution.py:351
  22.9 25.4 %all-to-all-start.1 = ((bf16[32,16,1152]{2,1,0:T(8,128)(2,1)}), bf16[32,16,1152]{2,1,0:T(8,128)(2,1)S(1)}, u32[]{:S(2)}, u32[]{:S(2)}) async-start(bf16[32,16,1152]{2,1,0:T(8,128)(2,1)} %spatial.1), calls=%async_computation.1 | async-start | bytes 2359296 | tf_op jit(solution)/shard_map/all_to_all | solution.py:378
  31.5 32.4 %copy-start.2 = (bf16[144,1152]{1,0:T(8,128)(2,1)}, bf16[144,1152]{1,0:T(8,128)(2,1)S(1)}, u32[]{:S(2)}) copy-start(bf16[144,1152]{1,0:T(8,128)(2,1)S(1)} %reshape.12.refs_0_) | copy-start | bytes 995332
  31.5 9.8 %collective-permute-start.2 = (bf16[144,1152]{1,0:T(8,128)(2,1)S(1)}, bf16[144,1152]{1,0:T(8,128)(2,1)S(1)}, u32[]{:S(2)}, u32[]{:S(2)}) collective-permute-start(bf16[144,1152]{1,0:T(8,128)(2,1)S(1)} %reshape.12.refs_0_), channel_id=1, source_target_pairs={{0,66},{2,64},{64,2},{66,0},{1,67},{3,65},{65,3},{67,1},{4,70},{6,... | collective-permute-start | bytes 995336 | tf_op jit(solution)/shard_map/ppermute | solution.py:359
  34.9 6.3 %collective-permute-start = (bf16[144,1152]{1,0:T(8,128)(2,1)S(1)}, bf16[144,1152]{1,0:T(8,128)(2,1)S(1)}, u32[]{:S(2)}, u32[]{:S(2)}) collective-permute-start(bf16[144,1152]{1,0:T(8,128)(2,1)S(1)} %reshape.12.refs_0_), channel_id=1, source_target_pairs={{0,1},{1,0},{2,3},{3,2},{4,5},{5,4},{6,7},{7,6},{8,9},{9,8},{10,11... | collective-permute-start | bytes 995336 | tf_op jit(solution)/shard_map/ppermute | solution.py:341
  37.1 26.8 %copy-start.3 = (bf16[144,1152]{1,0:T(8,128)(2,1)}, bf16[144,1152]{1,0:T(8,128)(2,1)S(1)}, u32[]{:S(2)}) copy-start(bf16[144,1152]{1,0:T(8,128)(2,1)S(1)} %reshape.13.refs_1_) | copy-start | bytes 995332
  37.1 11.3 %collective-permute-start.3 = (bf16[144,1152]{1,0:T(8,128)(2,1)S(1)}, bf16[144,1152]{1,0:T(8,128)(2,1)S(1)}, u32[]{:S(2)}, u32[]{:S(2)}) collective-permute-start(bf16[144,1152]{1,0:T(8,128)(2,1)S(1)} %reshape.13.refs_1_), channel_id=1, source_target_pairs={{0,66},{2,64},{64,2},{66,0},{1,67},{3,65},{65,3},{67,1},{4,70},{6,... | collective-permute-start | bytes 995336 | tf_op jit(solution)/shard_map/ppermute | solution.py:359
  37.2 11.2 %collective-permute-start.1 = (bf16[144,1152]{1,0:T(8,128)(2,1)S(1)}, bf16[144,1152]{1,0:T(8,128)(2,1)S(1)}, u32[]{:S(2)}, u32[]{:S(2)}) collective-permute-start(bf16[144,1152]{1,0:T(8,128)(2,1)S(1)} %reshape.13.refs_1_), channel_id=1, source_target_pairs={{0,1},{1,0},{2,3},{3,2},{4,5},{5,4},{6,7},{7,6},{8,9},{9,8},{10,11... | collective-permute-start | bytes 995336 | tf_op jit(solution)/shard_map/ppermute | solution.py:341
  41.2 37.8 %copy-start.6 = (bf16[144,1152]{1,0:T(8,128)(2,1)}, bf16[144,1152]{1,0:T(8,128)(2,1)S(1)}, u32[]{:S(2)}) copy-start(bf16[144,1152]{1,0:T(8,128)(2,1)S(1)} %collective-permute-done.2.refs_2_) | copy-start | bytes 995332
  41.2 9.9 %copy-start.7 = (bf16[144,1152]{1,0:T(8,128)(2,1)}, bf16[144,1152]{1,0:T(8,128)(2,1)S(1)}, u32[]{:S(2)}) copy-start(bf16[144,1152]{1,0:T(8,128)(2,1)S(1)} %collective-permute-done.refs_8_) | copy-start | bytes 995332
  48.4 2.8 %copy-start.8 = (bf16[144,1152]{1,0:T(8,128)(2,1)}, bf16[144,1152]{1,0:T(8,128)(2,1)S(1)}, u32[]{:S(2)}) copy-start(bf16[144,1152]{1,0:T(8,128)(2,1)S(1)} %collective-permute-done.3.refs_3_) | copy-start | bytes 995332
  48.4 2.8 %copy-start.10 = (bf16[144,1152]{1,0:T(8,128)(2,1)}, bf16[144,1152]{1,0:T(8,128)(2,1)S(1)}, u32[]{:S(2)}) copy-start(bf16[144,1152]{1,0:T(8,128)(2,1)S(1)} %collective-permute-done.1.refs_9_) | copy-start | bytes 995332
  48.4 15.6 %collective-permute-start.4 = (bf16[144,1152]{1,0:T(8,128)(2,1)S(1)}, bf16[144,1152]{1,0:T(8,128)(2,1)S(1)}, u32[]{:S(2)}, u32[]{:S(2)}) collective-permute-start(bf16[144,1152]{1,0:T(8,128)(2,1)S(1)} %reshape.12.refs_0_), channel_id=1, source_target_pairs={{0,16},{16,32},{32,48},{48,0},{1,17},{17,33},{33,49},{49,1},{2,18}... | collective-permute-start | bytes 995336 | tf_op jit(solution)/shard_map/ppermute | solution.py:341
  49.6 14.3 %collective-permute-start.5 = (bf16[144,1152]{1,0:T(8,128)(2,1)S(1)}, bf16[144,1152]{1,0:T(8,128)(2,1)}, u32[]{:S(2)}, u32[]{:S(2)}) collective-permute-start(bf16[144,1152]{1,0:T(8,128)(2,1)S(1)} %reshape.13.refs_1_), channel_id=1, source_target_pairs={{0,48},{16,0},{32,16},{48,32},{1,49},{17,1},{33,17},{49,33},{2,50}... | collective-permute-start | bytes 995336 | tf_op jit(solution)/shard_map/ppermute | solution.py:341
  51.2 13.5 %collective-permute-start.6 = (bf16[144,1152]{1,0:T(8,128)(2,1)S(1)}, bf16[144,1152]{1,0:T(8,128)(2,1)}, u32[]{:S(2)}, u32[]{:S(2)}) collective-permute-start(bf16[144,1152]{1,0:T(8,128)(2,1)S(1)} %collective-permute-done.2.refs_2_), channel_id=1, source_target_pairs={{0,16},{16,32},{32,48},{48,0},{1,17},{17,33},{33,49},{49,1},{2,18}... | collective-permute-start | bytes 995336 | tf_op jit(solution)/shard_map/ppermute | solution.py:341
  63.9 24.9 %copy-start.4 = (bf16[120,1152]{1,0:T(8,128)(2,1)S(1)}, bf16[120,1152]{1,0:T(8,128)(2,1)}, u32[]{:S(2)}) copy-start(bf16[120,1152]{1,0:T(8,128)(2,1)} %param.19) | copy-start | bytes 829444
  63.9 24.9 %copy-start.5 = (bf16[120,1152]{1,0:T(8,128)(2,1)S(1)}, bf16[120,1152]{1,0:T(8,128)(2,1)}, u32[]{:S(2)}) copy-start(bf16[120,1152]{1,0:T(8,128)(2,1)} %param.20) | copy-start | bytes 829444
  63.9 0.7 copy-start.11
  63.9 7.6 %copy-start.9 = (bf16[144,1152]{1,0:T(8,128)(2,1)S(1)}, bf16[144,1152]{1,0:T(8,128)(2,1)}, u32[]{:S(2)}) copy-start(bf16[144,1152]{1,0:T(8,128)(2,1)} %copy-done.8) | copy-start | bytes 995332
  64.7 14.9 %copy-start.12 = (bf16[144,1152]{1,0:T(8,128)(2,1)S(1)}, bf16[144,1152]{1,0:T(8,128)(2,1)}, u32[]{:S(2)}) copy-start(bf16[144,1152]{1,0:T(8,128)(2,1)} %copy-done.11) | copy-start | bytes 995332
  64.7 25.1 %all-to-all-start.2 = ((bf16[32,16,1152]{2,1,0:T(8,128)(2,1)}), bf16[32,16,1152]{2,1,0:T(8,128)(2,1)S(1)}, u32[]{:S(2)}, u32[]{:S(2)}) async-start(bf16[32,16,1152]{2,1,0:T(8,128)(2,1)} %temporal.1), calls=%async_computation.2 | async-start | bytes 2359296 | tf_op jit(solution)/shard_map/all_to_all | solution.py:387
  71.6 8.4 %collective-permute-start.9 = (bf16[144,1152]{1,0:T(8,128)(2,1)S(1)}, bf16[144,1152]{1,0:T(8,128)(2,1)S(1)}, u32[]{:S(2)}, u32[]{:S(2)}) collective-permute-start(bf16[144,1152]{1,0:T(8,128)(2,1)S(1)} %copy-done.9), channel_id=1, source_target_pairs={{0,1},{1,0},{2,3},{3,2},{4,5},{5,4},{6,7},{7,6},{8,9},{9,8},{10,11... | collective-permute-start | bytes 995336 | tf_op jit(solution)/shard_map/ppermute | solution.py:341
  75.2 12.3 %collective-permute-start.7 = (bf16[144,1152]{1,0:T(8,128)(2,1)}, bf16[144,1152]{1,0:T(8,128)(2,1)}, u32[]{:S(2)}, u32[]{:S(2)}) collective-permute-start(bf16[144,1152]{1,0:T(8,128)(2,1)} %collective-permute-done.5.refs_5_), channel_id=1, source_target_pairs={{0,66},{2,64},{64,2},{66,0},{1,67},{3,65},{65,3},{67,1},{4,70},{6,... | collective-permute-start | bytes 995336 | tf_op jit(solution)/shard_map/ppermute | solution.py:359
  79.1 9.9 %collective-permute-start.8 = (bf16[144,1152]{1,0:T(8,128)(2,1)S(1)}, bf16[144,1152]{1,0:T(8,128)(2,1)}, u32[]{:S(2)}, u32[]{:S(2)}) collective-permute-start(bf16[144,1152]{1,0:T(8,128)(2,1)S(1)} %collective-permute-done.2.refs_2_), channel_id=1, source_target_pairs={{0,1},{1,0},{2,3},{3,2},{4,5},{5,4},{6,7},{7,6},{8,9},{9,8},{10,11... | collective-permute-start | bytes 995336 | tf_op jit(solution)/shard_map/ppermute | solution.py:341
  79.4 9.5 %collective-permute-start.11 = (bf16[144,1152]{1,0:T(8,128)(2,1)}, bf16[144,1152]{1,0:T(8,128)(2,1)}, u32[]{:S(2)}, u32[]{:S(2)}) collective-permute-start(bf16[144,1152]{1,0:T(8,128)(2,1)} %collective-permute-done.5.refs_5_), channel_id=1, source_target_pairs={{0,1},{1,0},{2,3},{3,2},{4,5},{5,4},{6,7},{7,6},{8,9},{9,8},{10,11... | collective-permute-start | bytes 995336 | tf_op jit(solution)/shard_map/ppermute | solution.py:341
  79.6 9.4 %collective-permute-start.10 = (bf16[144,1152]{1,0:T(8,128)(2,1)S(1)}, bf16[144,1152]{1,0:T(8,128)(2,1)}, u32[]{:S(2)}, u32[]{:S(2)}) collective-permute-start(bf16[144,1152]{1,0:T(8,128)(2,1)S(1)} %copy-done.12), channel_id=1, source_target_pairs={{0,1},{1,0},{2,3},{3,2},{4,5},{5,4},{6,7},{7,6},{8,9},{9,8},{10,11... | collective-permute-start | bytes 995336 | tf_op jit(solution)/shard_map/ppermute | solution.py:341
  80.0 0.7 copy-start.13
  80.7 8.3 %collective-permute-start.12 = (bf16[144,1152]{1,0:T(8,128)(2,1)}, bf16[144,1152]{1,0:T(8,128)(2,1)S(1)}, u32[]{:S(2)}, u32[]{:S(2)}) collective-permute-start(bf16[144,1152]{1,0:T(8,128)(2,1)} %collective-permute-done.6.refs_6_), channel_id=1, source_target_pairs={{0,1},{1,0},{2,3},{3,2},{4,5},{5,4},{6,7},{7,6},{8,9},{9,8},{10,11... | collective-permute-start | bytes 995336 | tf_op jit(solution)/shard_map/ppermute | solution.py:341
  87.5 2.3 %collective-permute-start.13 = (bf16[144,1152]{1,0:T(8,128)(2,1)}, bf16[144,1152]{1,0:T(8,128)(2,1)}, u32[]{:S(2)}, u32[]{:S(2)}) collective-permute-start(bf16[144,1152]{1,0:T(8,128)(2,1)} %collective-permute-done.7.refs_7_), channel_id=1, source_target_pairs={{0,1},{1,0},{2,3},{3,2},{4,5},{5,4},{6,7},{7,6},{8,9},{9,8},{10,11... | collective-permute-start | bytes 995336 | tf_op jit(solution)/shard_map/ppermute | solution.py:341
  89.0 0.8 copy-start.14
